TPU v7x, 32 devices: a whole 2x2x4 slice. The times are simulated.
32 devices in a mesh: grp: 2 (over y), span: 4 (over z), stream: 2 (over x), vert: 2 (over core).
Axes of the slice: x: 2, y: 2, z: 4, core: 2. Of those that a mesh axis runs over, the one named last changes fastest.
Arguments:
- kappa: float32 [64, 64, 512], P(('grp', 'stream'), 'span', 'vert'), parts along dimension 0, may hold values from 0.01 to 0.16
- sigma: float32 [64, 64, 512], P(('grp', 'stream'), 'span', 'vert'), parts along dimension 0, may hold values from 0.5 to 2
- gate_residual: float32 [4, 2, 4096], P(('grp', 'stream'), 'vert', 'span'), parts along dimension 0, may hold values from -6 to 6
- gate_azimuth: float32 [4, 2, 4096], P(('grp', 'stream'), 'vert', 'span'), parts along dimension 0, may hold values from -3.140625 to 3.140625
- gate_elevation: float32 [4, 2, 4096], P(('grp', 'stream'), 'vert', 'span'), parts along dimension 0, may hold values from -0.3 to 0.3
- gate_brick: int32 [4, 2, 4096, 1], P(('grp', 'stream'), 'vert', 'span'), parts along dimension 0, may hold values from 0 to 3; in each aligned block of 1024 rows (0 to 1023, 1024 to 2047, ..., all dimensions but the last counted through in order) at most 768 rows name the same one
- gate_cell: int32 [4, 2, 4096], P(('grp', 'stream'), 'vert', 'span'), parts along dimension 0, may hold values from 0 to 65535
- blade_force: float32 [3, 4, 1024], P(None, ('grp', 'stream'), 'span'), parts along dimension 1, may hold values from -6 to 6
- point_x: float32 [4, 1024], P(('grp', 'stream'), 'span'), parts along dimension 0, may hold values from 6 to 9
- point_y: float32 [4, 1024], P(('grp', 'stream'), 'span'), parts along dimension 0, may hold values from 0 to 16
- point_z: float32 [4, 1024], P(('grp', 'stream'), 'span'), parts along dimension 0, may hold values from 0 to 512
Outputs:
- increment: float32 [3, 64, 64, 512], P(None, ('grp', 'stream'), 'span', 'vert'), parts along dimension 1
There are 2 independent parts, one for each index of `grp`. A program takes and returns all parts, laid end to end along the dimension named above; each array names one. Nothing has to cross between parts.
Inputs may be any that keep to these rules, and one draw needn't show every extreme that they name: `gate_brick`: among the 1024 gate rows of one brick (aligned blocks of rows), at most 768 name one spanwise brick, and in every draw some brick is named by exactly 768 of them.
All inputs are finite; a program needn't handle non-finite values.
Results may differ from a plain program's by a relative error of at most 0.0003.
Values sent between devices are 32-bit elements; how exact they have to be, the bound alone decides.
No kernel may reach another device: no remote copies, remote signals or barrier semaphores. Data moves between devices by JAX's collectives and lax.ppermute only.
A program may use at most 128 MiB of HBM per device.

v0:
```python
import jax
import jax.numpy as jnp
from jax import lax
from jax.sharding import PartitionSpec as P

SPREAD = 6
PASSES = 4


def with_halo(cells, sides, width):
    for axis, dim in sides:
        count = lax.axis_size(axis)
        head = lax.slice_in_dim(cells, 0, width, axis=dim)
        tail = lax.slice_in_dim(cells, cells.shape[dim] - width, cells.shape[dim], axis=dim)
        cells = jnp.concatenate(
            [
                lax.ppermute(tail, axis, [(i, (i + 1) % count) for i in range(count)]),
                cells,
                lax.ppermute(head, axis, [((i + 1) % count, i) for i in range(count)]),
            ],
            axis=dim,
        )
    return cells


def bump(distance, reach):
    scaled = distance / reach
    return jnp.square(jnp.maximum(0.0, 1.0 - scaled * scaled))


def wall_faces(kappa_ext, width):
    length_x, length_y, length_z = kappa_ext.shape
    inner_x = length_x - 2 * width
    inner_z = length_z - 2 * width
    start_x = lax.axis_index("stream") * inner_x - width
    start_z = lax.axis_index("vert") * inner_z - width
    limit_x = inner_x * lax.axis_size("stream")
    limit_z = inner_z * lax.axis_size("vert")
    left_x = start_x + jnp.arange(length_x - 1, dtype=jnp.int32)
    left_z = start_z + jnp.arange(length_z - 1, dtype=jnp.int32)
    keep_x = ((left_x >= 0) & (left_x + 1 < limit_x)).astype(jnp.float32)
    keep_z = ((left_z >= 0) & (left_z + 1 < limit_z)).astype(jnp.float32)
    along_x = jnp.sqrt(kappa_ext[:-1] * kappa_ext[1:]) * keep_x[:, None, None]
    along_y = jnp.sqrt(kappa_ext[:, :-1] * kappa_ext[:, 1:])
    along_z = jnp.sqrt(kappa_ext[:, :, :-1] * kappa_ext[:, :, 1:]) * keep_z[None, None, :]
    return (along_x, along_y, along_z)


def diffuse_once(field_ext, face_terms):
    along_x, along_y, along_z = face_terms
    center = field_ext[:, 1:-1, 1:-1, 1:-1]
    flux_x = along_x[:, 1:-1, 1:-1] * (field_ext[:, 1:, 1:-1, 1:-1] - field_ext[:, :-1, 1:-1, 1:-1])
    flux_y = along_y[1:-1, :, 1:-1] * (field_ext[:, 1:-1, 1:, 1:-1] - field_ext[:, 1:-1, :-1, 1:-1])
    flux_z = along_z[1:-1, 1:-1, :] * (field_ext[:, 1:-1, 1:-1, 1:] - field_ext[:, 1:-1, 1:-1, :-1])
    change = flux_x[:, 1:] - flux_x[:, :-1] + (flux_y[:, :, 1:] - flux_y[:, :, :-1])
    change = change + (flux_z[:, :, :, 1:] - flux_z[:, :, :, :-1])
    return center + change


def on_device(
    kappa,
    sigma,
    gate_residual,
    gate_azimuth,
    gate_elevation,
    gate_brick,
    gate_cell,
    blade_force,
    point_x,
    point_y,
    point_z,
):
    size_x, size_y, size_z = kappa.shape
    spans = lax.axis_size("span")
    count_points = blade_force.shape[2]
    reach = jnp.float32(SPREAD)
    stacked = jnp.concatenate([blade_force, point_x[None], point_y[None], point_z[None]], axis=0)
    nearby = with_halo(stacked, (("span", 2),), count_points)
    x_cells = jnp.arange(size_x, dtype=jnp.float32)
    y_cells = jnp.arange(size_y, dtype=jnp.float32)
    z_cells = (lax.axis_index("vert") * size_z + jnp.arange(size_z, dtype=jnp.int32)).astype(
        jnp.float32
    )
    kernel_x = bump(x_cells[:, None] - nearby[3, 0][None, :], reach)
    y_parts = []
    for which_side in range(3):
        shifted = y_cells - jnp.float32((which_side - 1) * size_y)
        y_here = nearby[4, 0, which_side * count_points : (which_side + 1) * count_points]
        y_parts.append(bump(shifted[:, None] - y_here[None, :], reach))
    kernel_y = jnp.concatenate(y_parts, axis=1)
    kernel_z = bump(z_cells[:, None] - nearby[5, 0][None, :], reach)
    rotor_blocks = []
    for component in range(3):
        weights = (
            nearby[component, 0][None, None, :] * kernel_x[:, None, :] * kernel_y[None, :, :]
        ).reshape(size_x * size_y, 3 * count_points)
        rotor_blocks.append(
            jnp.dot(weights, kernel_z.T, precision=lax.Precision.HIGHEST).reshape(
                size_x, size_y, size_z
            )
        )
    rotor = jnp.stack(rotor_blocks)
    azimuth = gate_azimuth[0, 0]
    elevation = gate_elevation[0, 0]
    cosine = jnp.cos(elevation)
    weighted = (
        jnp.stack([cosine * jnp.cos(azimuth), cosine * jnp.sin(azimuth), jnp.sin(elevation)])
        * gate_residual[0, 0][None]
    )
    target = gate_brick[0, 0, :, 0]
    cell_ids = gate_cell[0, 0]
    row_count = target.shape[0]
    capacity = 3 * row_count // spans
    one_hot = (target[:, None] == jnp.arange(spans, dtype=jnp.int32)[None, :]).astype(jnp.int32)
    ranks = jnp.sum((jnp.cumsum(one_hot, axis=0) - one_hot) * one_hot, axis=1)
    slot_index = target * capacity + ranks
    send_values = (
        jnp.zeros((3, spans * capacity), jnp.float32)
        .at[:, slot_index]
        .set(weighted)
        .reshape(3, spans, capacity)
    )
    send_cells = (
        jnp.zeros((1, spans * capacity), jnp.int32)
        .at[:, slot_index]
        .set(cell_ids[None])
        .reshape(1, spans, capacity)
    )
    got_values, got_cells = (
        lax.all_to_all(send_values, "span", split_axis=1, concat_axis=1, tiled=True),
        lax.all_to_all(send_cells, "span", split_axis=1, concat_axis=1, tiled=True),
    )
    flat_values = got_values.reshape(3, -1)
    flat_cells = got_cells.reshape(-1)
    lidar = jnp.zeros((3, size_x * size_y * size_z), jnp.float32).at[:, flat_cells].add(flat_values)
    field = (lidar.reshape(3, size_x, size_y, size_z) + rotor) * sigma[None]
    kappa_ext = with_halo(kappa, (("span", 1), ("stream", 0), ("vert", 2)), 1)
    face_terms = wall_faces(kappa_ext, 1)
    for pass_index in range(PASSES):
        field_ext = with_halo(field, (("span", 2), ("stream", 1), ("vert", 3)), 1)
        field = diffuse_once(field_ext, face_terms)
    return field


def solution(mesh):
    placed = (
        P(("grp", "stream"), "span", "vert"),
        P(("grp", "stream"), "span", "vert"),
        P(("grp", "stream"), "vert", "span"),
        P(("grp", "stream"), "vert", "span"),
        P(("grp", "stream"), "vert", "span"),
        P(("grp", "stream"), "vert", "span", None),
        P(("grp", "stream"), "vert", "span"),
        P(None, ("grp", "stream"), "span"),
        P(("grp", "stream"), "span"),
        P(("grp", "stream"), "span"),
        P(("grp", "stream"), "span"),
    )
    return jax.shard_map(
        on_device,
        mesh=mesh,
        in_specs=placed,
        out_specs=P(None, ("grp", "stream"), "span", "vert"),
        check_vma=False,
    )
```

profile of v0, /device:TPU:0, one launch (start us, length us, event | category | flops | bytes accessed | tf_op | source)
XLA Modules:
  0.0 197.5 jit_solution(2043657252768101559)
XLA Ops:
  0.7 5.1 %collective-permute-start.1 = (f32[6,1,256]{2,1,0:T(1,128)S(1)}, f32[6,1,256]{2,1,0:T(1,128)S(1)}, u32[]{:S(2)}, u32[]{:S(2)}) collective-permute-start(f32[6,1,256]{2,1,0:T(1,128)S(1)} %pad_maximum_fusion.92), channel_id=1, source_target_pairs={{4,0},{8,4},{12,8},{0,12},{5,1},{9,5},{13,9},{1,13},{6,2},{10,6},{... | collective-permute-start | bytes 18440 | tf_op jit(solution)/shard_map/ppermute | solution.py:19
  9.5 5.0 %scatter_custom_fusion = s32[3072]{0:T(1024)} fusion(s32[1024]{0:T(1024)S(1)} %bitcast.82, s32[1024]{0:T(1024)} %bitcast.87, s32[]{:T(128)} %constant.17.clone.1), kind=kCustom, calls=%fused_computation.211 | custom fusion | bytes 12800 | tf_op jit(solution)/shard_map/scatter | solution.py:126
  14.6 5.1 %all-to-all-start = ((s32[1,4,768]{2,0,1:T(1,128)}), s32[1,4,768]{2,0,1:T(1,128)S(1)}, u32[]{:S(2)}, u32[]{:S(2)}) async-start(s32[1,4,768]{2,0,1:T(1,128)} %bitcast.7), calls=%async_computation | async-start | bytes 24576 | tf_op jit(solution)/shard_map/all_to_all | solution.py:131
  20.7 3.9 %collective-permute-start.3 = (f32[16,1,256]{2,1,0:T(1,128)S(1)}, f32[16,1,256]{2,1,0:T(1,128)S(1)}, u32[]{:S(2)}, u32[]{:S(2)}) collective-permute-start(f32[16,1,256]{2,1,0:T(1,128)S(1)} %get-tuple-element.45), channel_id=1, source_target_pairs={{4,0},{8,4},{12,8},{0,12},{5,1},{9,5},{13,9},{1,13},{6,2},{10,6},{... | collective-permute-start | bytes 49160 | tf_op jit(solution)/shard_map/ppermute | solution.py:19
  27.9 3.5 %scatter_custom_fusion.1 = f32[3,3072]{0,1:T(8,128)S(1)} fusion(s32[1024]{0:T(1024)S(1)} %bitcast.83, f32[1024,3]{1,0:T(8,128)S(1)} %copy.34, f32[]{:T(128)} %constant.16.clone.1), kind=kCustom, calls=%fused_computation.133 | custom fusion | bytes 36868 | tf_op jit(solution)/shard_map/scatter | solution.py:120
  33.9 1.8 convolution_bitcast_fusion.1
  35.6 1.7 convolution_bitcast_fusion.2
  37.4 1.6 collective-permute-start.5
  43.5 5.1 %all-to-all-start.1 = ((f32[3,4,768]{2,0,1:T(4,128)}), f32[3,4,768]{2,0,1:T(4,128)}, u32[]{:S(2)}, u32[]{:S(2)}) async-start(f32[3,4,768]{2,0,1:T(4,128)} %copy.35), calls=%async_computation.1 | async-start | bytes 98304 | tf_op jit(solution)/shard_map/all_to_all | solution.py:130
  50.6 3.8 %all-to-all-done.1 = f32[3,4,768]{2,0,1:T(4,128)} async-done(((f32[3,4,768]{2,0,1:T(4,128)}), f32[3,4,768]{2,0,1:T(4,128)}, u32[]{:S(2)}, u32[]{:S(2)}) %all-to-all-start.1) | async-done | bytes 36896 | tf_op jit(solution)/shard_map/all_to_all | solution.py:130
  55.7 34.4 %scatter_custom_fusion.2 = f32[3,65536]{0,1:T(8,128)} fusion(s32[3072]{0:T(1024)S(1)} %bitcast.74, f32[3072,3]{1,0:T(8,128)S(1)} %copy.36, f32[]{:T(128)} %constant.16.clone.1), kind=kCustom, calls=%fused_computation.3 | custom fusion | flops 9216 | bytes 786436 | tf_op jit(solution)/shard_map/scatter-add | solution.py:135
  90.1 19.5 %copy.54 = f32[3,16,16,256]{3,2,1,0:T(8,128)S(1)} copy(f32[3,16,16,256]{0,3,2,1:T(8,128)} %bitcast.64) | data formatting | bytes 1572864 | tf_op jit(solution)/shard_map/reshape | solution.py:136
  111.2 1.8 collective-permute-start.8
  115.4 1.7 collective-permute-done.8
  117.7 1.5 collective-permute-start.11
  128.4 2.0 %copy.41 = f32[3,18,18,1]{3,2,1,0:T(8,128)} copy(f32[3,18,18,1]{2,3,1,0:T(1,128)} %collective-permute-done.13) | data formatting | bytes 7776 | tf_op jit(solution)/shard_map/ppermute | solution.py:17
  130.4 2.0 %copy.39 = f32[3,18,18,1]{3,2,1,0:T(8,128)} copy(f32[3,18,18,1]{2,3,1,0:T(1,128)} %collective-permute-done.12) | data formatting | bytes 7776 | tf_op jit(solution)/shard_map/ppermute | solution.py:19
  132.4 2.0 fusion.9
  135.1 2.0 %collective-permute-start.14 = (f32[3,16,1,256]{3,2,1,0:T(1,128)S(1)}, f32[3,16,1,256]{3,2,1,0:T(1,128)S(1)}, u32[]{:S(2)}, u32[]{:S(2)}) collective-permute-start(f32[3,16,1,256]{3,2,1,0:T(1,128)S(1)} %get-tuple-element.30), channel_id=1, source_target_pairs={{0,4},{4,8},{8,12},{12,0},{1,5},{5,9},{9,13},{13,1},{2,6},{6,10},{... | collective-permute-start | bytes 147464 | tf_op jit(solution)/shard_map/ppermute | solution.py:17
  137.1 2.1 %collective-permute-done.15 = f32[3,16,1,256]{3,2,1,0:T(1,128)S(1)} collective-permute-done((f32[3,16,1,256]{3,2,1,0:T(1,128)S(1)}, f32[3,16,1,256]{3,2,1,0:T(1,128)S(1)}, u32[]{:S(2)}, u32[]{:S(2)}) %collective-permute-start.15) | collective-permute-done | bytes 49184 | tf_op jit(solution)/shard_map/ppermute | solution.py:19
  139.2 1.9 collective-permute-done.14
  152.7 2.0 %copy.43 = f32[3,18,18,1]{3,2,1,0:T(8,128)} copy(f32[3,18,18,1]{2,3,1,0:T(1,128)} %collective-permute-done.18) | data formatting | bytes 7776 | tf_op jit(solution)/shard_map/ppermute | solution.py:19
  154.7 1.7 fusion.7
  157.2 1.8 collective-permute-start.20
  159.0 2.1 %collective-permute-done.21 = f32[3,16,1,256]{3,2,1,0:T(1,128)S(1)} collective-permute-done((f32[3,16,1,256]{3,2,1,0:T(1,128)S(1)}, f32[3,16,1,256]{3,2,1,0:T(1,128)S(1)}, u32[]{:S(2)}, u32[]{:S(2)}) %collective-permute-start.21) | collective-permute-done | bytes 49184 | tf_op jit(solution)/shard_map/ppermute | solution.py:19
  161.1 2.0 %collective-permute-done.20 = f32[3,16,1,256]{3,2,1,0:T(1,128)S(1)} collective-permute-done((f32[3,16,1,256]{3,2,1,0:T(1,128)S(1)}, f32[3,16,1,256]{3,2,1,0:T(1,128)S(1)}, u32[]{:S(2)}, u32[]{:S(2)}) %collective-permute-start.20) | collective-permute-done | bytes 49184 | tf_op jit(solution)/shard_map/ppermute | solution.py:17
  174.2 2.0 %copy.47 = f32[3,18,18,1]{3,2,1,0:T(8,128)} copy(f32[3,18,18,1]{2,3,1,0:T(1,128)} %collective-permute-done.24) | data formatting | bytes 7776 | tf_op jit(solution)/shard_map/ppermute | solution.py:19
  176.2 1.7 fusion.5
  179.0 1.6 collective-permute-start.26
  180.6 2.1 %collective-permute-done.27 = f32[3,16,1,256]{3,2,1,0:T(1,128)S(1)} collective-permute-done((f32[3,16,1,256]{3,2,1,0:T(1,128)S(1)}, f32[3,16,1,256]{3,2,1,0:T(1,128)S(1)}, u32[]{:S(2)}, u32[]{:S(2)}) %collective-permute-start.27) | collective-permute-done | bytes 49184 | tf_op jit(solution)/shard_map/ppermute | solution.py:19
  182.6 2.2 %collective-permute-done.26 = f32[3,16,1,256]{3,2,1,0:T(1,128)S(1)} collective-permute-done((f32[3,16,1,256]{3,2,1,0:T(1,128)S(1)}, f32[3,16,1,256]{3,2,1,0:T(1,128)S(1)}, u32[]{:S(2)}, u32[]{:S(2)}) %collective-permute-start.26) | collective-permute-done | bytes 49184 | tf_op jit(solution)/shard_map/ppermute | solution.py:17
  194.5 1.7 fusion.3
  (171 shorter events, 68.6 us)
Async XLA Ops:
  0.7 31.8 %collective-permute-start.1 = (f32[6,1,256]{2,1,0:T(1,128)S(1)}, f32[6,1,256]{2,1,0:T(1,128)S(1)}, u32[]{:S(2)}, u32[]{:S(2)}) collective-permute-start(f32[6,1,256]{2,1,0:T(1,128)S(1)} %pad_maximum_fusion.92), channel_id=1, source_target_pairs={{4,0},{8,4},{12,8},{0,12},{5,1},{9,5},{13,9},{1,13},{6,2},{10,6},{... | collective-permute-start | bytes 18440 | tf_op jit(solution)/shard_map/ppermute | solution.py:19
  5.8 26.8 %collective-permute-start = (f32[6,1,256]{2,1,0:T(1,128)S(1)}, f32[6,1,256]{2,1,0:T(1,128)S(1)}, u32[]{:S(2)}, u32[]{:S(2)}) collective-permute-start(f32[6,1,256]{2,1,0:T(1,128)S(1)} %pad_maximum_fusion.92), channel_id=1, source_target_pairs={{0,4},{4,8},{8,12},{12,0},{1,5},{5,9},{9,13},{13,1},{2,6},{6,10},{... | collective-permute-start | bytes 18440 | tf_op jit(solution)/shard_map/ppermute | solution.py:17
  14.6 28.9 %all-to-all-start = ((s32[1,4,768]{2,0,1:T(1,128)}), s32[1,4,768]{2,0,1:T(1,128)S(1)}, u32[]{:S(2)}, u32[]{:S(2)}) async-start(s32[1,4,768]{2,0,1:T(1,128)} %bitcast.7), calls=%async_computation | async-start | bytes 24576 | tf_op jit(solution)/shard_map/all_to_all | solution.py:131
  20.7 16.7 %collective-permute-start.3 = (f32[16,1,256]{2,1,0:T(1,128)S(1)}, f32[16,1,256]{2,1,0:T(1,128)S(1)}, u32[]{:S(2)}, u32[]{:S(2)}) collective-permute-start(f32[16,1,256]{2,1,0:T(1,128)S(1)} %get-tuple-element.45), channel_id=1, source_target_pairs={{4,0},{8,4},{12,8},{0,12},{5,1},{9,5},{13,9},{1,13},{6,2},{10,6},{... | collective-permute-start | bytes 49160 | tf_op jit(solution)/shard_map/ppermute | solution.py:19
  24.6 12.8 %collective-permute-start.2 = (f32[16,1,256]{2,1,0:T(1,128)S(1)}, f32[16,1,256]{2,1,0:T(1,128)S(1)}, u32[]{:S(2)}, u32[]{:S(2)}) collective-permute-start(f32[16,1,256]{2,1,0:T(1,128)S(1)} %get-tuple-element.44), channel_id=1, source_target_pairs={{0,4},{4,8},{8,12},{12,0},{1,5},{5,9},{9,13},{13,1},{2,6},{6,10},{... | collective-permute-start | bytes 49160 | tf_op jit(solution)/shard_map/ppermute | solution.py:17
  37.4 3.9 %collective-permute-start.5 = (f32[1,18,256]{2,1,0:T(8,128)S(1)}, f32[1,18,256]{2,1,0:T(8,128)S(1)}, u32[]{:S(2)}, u32[]{:S(2)}) collective-permute-start(f32[1,18,256]{2,1,0:T(8,128)S(1)} %get-tuple-element.43), channel_id=1, source_target_pairs={{2,0},{0,2},{3,1},{1,3},{6,4},{4,6},{7,5},{5,7},{10,8},{8,10},{11,... | collective-permute-start | bytes 55304 | tf_op jit(solution)/shard_map/ppermute | solution.py:19
  38.9 3.8 %collective-permute-start.4 = (f32[1,18,256]{2,1,0:T(8,128)S(1)}, f32[1,18,256]{2,1,0:T(8,128)S(1)}, u32[]{:S(2)}, u32[]{:S(2)}) collective-permute-start(f32[1,18,256]{2,1,0:T(8,128)S(1)} %get-tuple-element.42), channel_id=1, source_target_pairs={{0,2},{2,0},{1,3},{3,1},{4,6},{6,4},{5,7},{7,5},{8,10},{10,8},{9,1... | collective-permute-start | bytes 55304 | tf_op jit(solution)/shard_map/ppermute | solution.py:17
  43.0 5.7 %collective-permute-start.6 = (f32[18,18,1]{2,1,0:T(8,128)S(1)}, f32[18,18,1]{2,1,0:T(8,128)S(1)}, u32[]{:S(2)}, u32[]{:S(2)}) collective-permute-start(f32[18,18,1]{2,1,0:T(8,128)S(1)} %get-tuple-element.39), channel_id=1, source_target_pairs={{0,1},{1,0},{2,3},{3,2},{4,5},{5,4},{6,7},{7,6},{8,9},{9,8},{10,11... | collective-permute-start | bytes 3896 | tf_op jit(solution)/shard_map/ppermute | solution.py:17
  43.0 5.6 %collective-permute-start.7 = (f32[18,18,1]{2,1,0:T(8,128)S(1)}, f32[18,18,1]{2,1,0:T(8,128)S(1)}, u32[]{:S(2)}, u32[]{:S(2)}) collective-permute-start(f32[18,18,1]{2,1,0:T(8,128)S(1)} %get-tuple-element.38), channel_id=1, source_target_pairs={{1,0},{0,1},{3,2},{2,3},{5,4},{4,5},{7,6},{6,7},{9,8},{8,9},{11,10... | collective-permute-start | bytes 3896 | tf_op jit(solution)/shard_map/ppermute | solution.py:19
  43.5 10.9 %all-to-all-start.1 = ((f32[3,4,768]{2,0,1:T(4,128)}), f32[3,4,768]{2,0,1:T(4,128)}, u32[]{:S(2)}, u32[]{:S(2)}) async-start(f32[3,4,768]{2,0,1:T(4,128)} %copy.35), calls=%async_computation.1 | async-start | bytes 98304 | tf_op jit(solution)/shard_map/all_to_all | solution.py:130
  110.9 4.5 %collective-permute-start.9 = (f32[3,16,1,256]{3,2,1,0:T(1,128)S(1)}, f32[3,16,1,256]{3,2,1,0:T(1,128)S(1)}, u32[]{:S(2)}, u32[]{:S(2)}) collective-permute-start(f32[3,16,1,256]{3,2,1,0:T(1,128)S(1)} %get-tuple-element.33), channel_id=1, source_target_pairs={{4,0},{8,4},{12,8},{0,12},{5,1},{9,5},{13,9},{1,13},{6,2},{10,6},{... | collective-permute-start | bytes 147464 | tf_op jit(solution)/shard_map/ppermute | solution.py:19
  111.2 5.9 %collective-permute-start.8 = (f32[3,16,1,256]{3,2,1,0:T(1,128)S(1)}, f32[3,16,1,256]{3,2,1,0:T(1,128)S(1)}, u32[]{:S(2)}, u32[]{:S(2)}) collective-permute-start(f32[3,16,1,256]{3,2,1,0:T(1,128)S(1)} %get-tuple-element.32), channel_id=1, source_target_pairs={{0,4},{4,8},{8,12},{12,0},{1,5},{5,9},{9,13},{13,1},{2,6},{6,10},{... | collective-permute-start | bytes 147464 | tf_op jit(solution)/shard_map/ppermute | solution.py:17
  117.2 4.4 %collective-permute-start.10 = (f32[3,1,18,256]{3,2,1,0:T(8,128)S(1)}, f32[3,1,18,256]{3,2,1,0:T(8,128)S(1)}, u32[]{:S(2)}, u32[]{:S(2)}) collective-permute-start(f32[3,1,18,256]{3,2,1,0:T(8,128)S(1)} %get-tuple-element.25), channel_id=1, source_target_pairs={{2,0},{0,2},{3,1},{1,3},{6,4},{4,6},{7,5},{5,7},{10,8},{8,10},{11,... | collective-permute-start | bytes 165896 | tf_op jit(solution)/shard_map/ppermute | solution.py:19
  117.7 4.7 %collective-permute-start.11 = (f32[3,1,18,256]{3,2,1,0:T(8,128)S(1)}, f32[3,1,18,256]{3,2,1,0:T(8,128)S(1)}, u32[]{:S(2)}, u32[]{:S(2)}) collective-permute-start(f32[3,1,18,256]{3,2,1,0:T(8,128)S(1)} %get-tuple-element.24), channel_id=1, source_target_pairs={{0,2},{2,0},{1,3},{3,1},{4,6},{6,4},{5,7},{7,5},{8,10},{10,8},{9,1... | collective-permute-start | bytes 165896 | tf_op jit(solution)/shard_map/ppermute | solution.py:17
  125.6 2.7 %collective-permute-start.13 = (f32[3,18,18,1]{2,3,1,0:T(1,128)S(1)}, f32[3,18,18,1]{2,3,1,0:T(1,128)}, u32[]{:S(2)}, u32[]{:S(2)}) collective-permute-start(f32[3,18,18,1]{2,3,1,0:T(1,128)S(1)} %copy.40), channel_id=1, source_target_pairs={{0,1},{1,0},{2,3},{3,2},{4,5},{5,4},{6,7},{7,6},{8,9},{9,8},{10,11... | collective-permute-start | bytes 11672 | tf_op jit(solution)/shard_map/ppermute | solution.py:17
  126.7 3.7 %collective-permute-start.12 = (f32[3,18,18,1]{2,3,1,0:T(1,128)}, f32[3,18,18,1]{2,3,1,0:T(1,128)}, u32[]{:S(2)}, u32[]{:S(2)}) collective-permute-start(f32[3,18,18,1]{2,3,1,0:T(1,128)} %copy.38), channel_id=1, source_target_pairs={{1,0},{0,1},{3,2},{2,3},{5,4},{4,5},{7,6},{6,7},{9,8},{8,9},{11,10... | collective-permute-start | bytes 11672 | tf_op jit(solution)/shard_map/ppermute | solution.py:19
  135.1 4.1 %collective-permute-start.15 = (f32[3,16,1,256]{3,2,1,0:T(1,128)S(1)}, f32[3,16,1,256]{3,2,1,0:T(1,128)S(1)}, u32[]{:S(2)}, u32[]{:S(2)}) collective-permute-start(f32[3,16,1,256]{3,2,1,0:T(1,128)S(1)} %get-tuple-element.31), channel_id=1, source_target_pairs={{4,0},{8,4},{12,8},{0,12},{5,1},{9,5},{13,9},{1,13},{6,2},{10,6},{... | collective-permute-start | bytes 147464 | tf_op jit(solution)/shard_map/ppermute | solution.py:19
  135.1 5.9 %collective-permute-start.14 = (f32[3,16,1,256]{3,2,1,0:T(1,128)S(1)}, f32[3,16,1,256]{3,2,1,0:T(1,128)S(1)}, u32[]{:S(2)}, u32[]{:S(2)}) collective-permute-start(f32[3,16,1,256]{3,2,1,0:T(1,128)S(1)} %get-tuple-element.30), channel_id=1, source_target_pairs={{0,4},{4,8},{8,12},{12,0},{1,5},{5,9},{9,13},{13,1},{2,6},{6,10},{... | collective-permute-start | bytes 147464 | tf_op jit(solution)/shard_map/ppermute | solution.py:17
  141.1 4.4 %collective-permute-start.16 = (f32[3,1,18,256]{3,2,1,0:T(8,128)S(1)}, f32[3,1,18,256]{3,2,1,0:T(8,128)S(1)}, u32[]{:S(2)}, u32[]{:S(2)}) collective-permute-start(f32[3,1,18,256]{3,2,1,0:T(8,128)S(1)} %get-tuple-element.23), channel_id=1, source_target_pairs={{2,0},{0,2},{3,1},{1,3},{6,4},{4,6},{7,5},{5,7},{10,8},{8,10},{11,... | collective-permute-start | bytes 165896 | tf_op jit(solution)/shard_map/ppermute | solution.py:19
  142.4 4.4 %collective-permute-start.17 = (f32[3,1,18,256]{3,2,1,0:T(8,128)S(1)}, f32[3,1,18,256]{3,2,1,0:T(8,128)S(1)}, u32[]{:S(2)}, u32[]{:S(2)}) collective-permute-start(f32[3,1,18,256]{3,2,1,0:T(8,128)S(1)} %get-tuple-element.22), channel_id=1, source_target_pairs={{0,2},{2,0},{1,3},{3,1},{4,6},{6,4},{5,7},{7,5},{8,10},{10,8},{9,1... | collective-permute-start | bytes 165896 | tf_op jit(solution)/shard_map/ppermute | solution.py:17
  148.8 2.6 %collective-permute-start.19 = (f32[3,18,18,1]{2,3,1,0:T(1,128)}, f32[3,18,18,1]{2,3,1,0:T(1,128)}, u32[]{:S(2)}, u32[]{:S(2)}) collective-permute-start(f32[3,18,18,1]{2,3,1,0:T(1,128)} %copy.44), channel_id=1, source_target_pairs={{0,1},{1,0},{2,3},{3,2},{4,5},{5,4},{6,7},{7,6},{8,9},{9,8},{10,11... | collective-permute-start | bytes 11672 | tf_op jit(solution)/shard_map/ppermute | solution.py:17
  149.9 2.8 %collective-permute-start.18 = (f32[3,18,18,1]{2,3,1,0:T(1,128)}, f32[3,18,18,1]{2,3,1,0:T(1,128)}, u32[]{:S(2)}, u32[]{:S(2)}) collective-permute-start(f32[3,18,18,1]{2,3,1,0:T(1,128)} %copy.42), channel_id=1, source_target_pairs={{1,0},{0,1},{3,2},{2,3},{5,4},{4,5},{7,6},{6,7},{9,8},{8,9},{11,10... | collective-permute-start | bytes 11672 | tf_op jit(solution)/shard_map/ppermute | solution.py:19
  156.9 4.1 %collective-permute-start.21 = (f32[3,16,1,256]{3,2,1,0:T(1,128)S(1)}, f32[3,16,1,256]{3,2,1,0:T(1,128)S(1)}, u32[]{:S(2)}, u32[]{:S(2)}) collective-permute-start(f32[3,16,1,256]{3,2,1,0:T(1,128)S(1)} %get-tuple-element.29), channel_id=1, source_target_pairs={{4,0},{8,4},{12,8},{0,12},{5,1},{9,5},{13,9},{1,13},{6,2},{10,6},{... | collective-permute-start | bytes 147464 | tf_op jit(solution)/shard_map/ppermute | solution.py:19
  157.2 5.9 %collective-permute-start.20 = (f32[3,16,1,256]{3,2,1,0:T(1,128)S(1)}, f32[3,16,1,256]{3,2,1,0:T(1,128)S(1)}, u32[]{:S(2)}, u32[]{:S(2)}) collective-permute-start(f32[3,16,1,256]{3,2,1,0:T(1,128)S(1)} %get-tuple-element.28), channel_id=1, source_target_pairs={{0,4},{4,8},{8,12},{12,0},{1,5},{5,9},{9,13},{13,1},{2,6},{6,10},{... | collective-permute-start | bytes 147464 | tf_op jit(solution)/shard_map/ppermute | solution.py:17
  163.1 4.4 %collective-permute-start.22 = (f32[3,1,18,256]{3,2,1,0:T(8,128)S(1)}, f32[3,1,18,256]{3,2,1,0:T(8,128)S(1)}, u32[]{:S(2)}, u32[]{:S(2)}) collective-permute-start(f32[3,1,18,256]{3,2,1,0:T(8,128)S(1)} %get-tuple-element.21), channel_id=1, source_target_pairs={{2,0},{0,2},{3,1},{1,3},{6,4},{4,6},{7,5},{5,7},{10,8},{8,10},{11,... | collective-permute-start | bytes 165896 | tf_op jit(solution)/shard_map/ppermute | solution.py:19
  164.0 4.4 %collective-permute-start.23 = (f32[3,1,18,256]{3,2,1,0:T(8,128)S(1)}, f32[3,1,18,256]{3,2,1,0:T(8,128)S(1)}, u32[]{:S(2)}, u32[]{:S(2)}) collective-permute-start(f32[3,1,18,256]{3,2,1,0:T(8,128)S(1)} %get-tuple-element.20), channel_id=1, source_target_pairs={{0,2},{2,0},{1,3},{3,1},{4,6},{6,4},{5,7},{7,5},{8,10},{10,8},{9,1... | collective-permute-start | bytes 165896 | tf_op jit(solution)/shard_map/ppermute | solution.py:17
  170.4 2.6 %collective-permute-start.25 = (f32[3,18,18,1]{2,3,1,0:T(1,128)}, f32[3,18,18,1]{2,3,1,0:T(1,128)}, u32[]{:S(2)}, u32[]{:S(2)}) collective-permute-start(f32[3,18,18,1]{2,3,1,0:T(1,128)} %copy.48), channel_id=1, source_target_pairs={{0,1},{1,0},{2,3},{3,2},{4,5},{5,4},{6,7},{7,6},{8,9},{9,8},{10,11... | collective-permute-start | bytes 11672 | tf_op jit(solution)/shard_map/ppermute | solution.py:17
  171.5 2.8 %collective-permute-start.24 = (f32[3,18,18,1]{2,3,1,0:T(1,128)}, f32[3,18,18,1]{2,3,1,0:T(1,128)}, u32[]{:S(2)}, u32[]{:S(2)}) collective-permute-start(f32[3,18,18,1]{2,3,1,0:T(1,128)} %copy.46), channel_id=1, source_target_pairs={{1,0},{0,1},{3,2},{2,3},{5,4},{4,5},{7,6},{6,7},{9,8},{8,9},{11,10... | collective-permute-start | bytes 11672 | tf_op jit(solution)/shard_map/ppermute | solution.py:19
  178.5 4.1 %collective-permute-start.27 = (f32[3,16,1,256]{3,2,1,0:T(1,128)S(1)}, f32[3,16,1,256]{3,2,1,0:T(1,128)S(1)}, u32[]{:S(2)}, u32[]{:S(2)}) collective-permute-start(f32[3,16,1,256]{3,2,1,0:T(1,128)S(1)} %get-tuple-element.27), channel_id=1, source_target_pairs={{4,0},{8,4},{12,8},{0,12},{5,1},{9,5},{13,9},{1,13},{6,2},{10,6},{... | collective-permute-start | bytes 147464 | tf_op jit(solution)/shard_map/ppermute | solution.py:19
  179.0 5.9 %collective-permute-start.26 = (f32[3,16,1,256]{3,2,1,0:T(1,128)S(1)}, f32[3,16,1,256]{3,2,1,0:T(1,128)S(1)}, u32[]{:S(2)}, u32[]{:S(2)}) collective-permute-start(f32[3,16,1,256]{3,2,1,0:T(1,128)S(1)} %get-tuple-element.26), channel_id=1, source_target_pairs={{0,4},{4,8},{8,12},{12,0},{1,5},{5,9},{9,13},{13,1},{2,6},{6,10},{... | collective-permute-start | bytes 147464 | tf_op jit(solution)/shard_map/ppermute | solution.py:17
  184.9 4.4 %collective-permute-start.28 = (f32[3,1,18,256]{3,2,1,0:T(8,128)S(1)}, f32[3,1,18,256]{3,2,1,0:T(8,128)S(1)}, u32[]{:S(2)}, u32[]{:S(2)}) collective-permute-start(f32[3,1,18,256]{3,2,1,0:T(8,128)S(1)} %get-tuple-element.19), channel_id=1, source_target_pairs={{2,0},{0,2},{3,1},{1,3},{6,4},{4,6},{7,5},{5,7},{10,8},{8,10},{11,... | collective-permute-start | bytes 165896 | tf_op jit(solution)/shard_map/ppermute | solution.py:19
  186.1 4.4 %collective-permute-start.29 = (f32[3,1,18,256]{3,2,1,0:T(8,128)S(1)}, f32[3,1,18,256]{3,2,1,0:T(8,128)S(1)}, u32[]{:S(2)}, u32[]{:S(2)}) collective-permute-start(f32[3,1,18,256]{3,2,1,0:T(8,128)S(1)} %get-tuple-element.18), channel_id=1, source_target_pairs={{0,2},{2,0},{1,3},{3,1},{4,6},{6,4},{5,7},{7,5},{8,10},{10,8},{9,1... | collective-permute-start | bytes 165896 | tf_op jit(solution)/shard_map/ppermute | solution.py:17
  (22 other events, 128.2 us)
where the time goes:
time: 199 us; the launch traced here: 198 us
  other arithmetic  64.2 us (32%)
  local copies, waits for them, and re-layouts  57.2 us (29%)
  starting transfers between devices  40.6 us (20%)
  waiting for transfers between devices  30.4 us (15%)
  matrix products  4.53 us (2%)
    scatter-add x1, other arithmetic, on_device(): jnp.zeros((3, size_x * size_y * size_z), jnp.float32).at[:, flat_cells]  34.4 us
    reshape x1, local copies, waits for them, and re-layouts, on_device(): field = (lidar.reshape(3, size_x, size_y, size_z) + rotor) * sigma[None]  19.5 us
    ppermute x16, starting transfers between devices, with_halo(): lax.ppermute(head, axis, [((i + 1) % count, i) for i in range(count)])  18.1 us
    ppermute x16, waiting for transfers between devices, with_halo(): lax.ppermute(tail, axis, [(i, (i + 1) % count) for i in range(count)])  13.3 us
    ppermute x16, waiting for transfers between devices, with_halo(): lax.ppermute(head, axis, [((i + 1) % count, i) for i in range(count)])  13.2 us
    ppermute x16, starting transfers between devices, with_halo(): lax.ppermute(tail, axis, [(i, (i + 1) % count) for i in range(count)])  12.4 us
    ppermute x4, local copies, waits for them, and re-layouts, with_halo(): lax.ppermute(head, axis, [((i + 1) % count, i) for i in range(count)])  7.3 us
    mul x4, other arithmetic, diffuse_once(): along_z[1:-1, 1:-1, :]  7.1 us
  transfers between devices with their start and end apart: 34, of which 20 were waited for; matrix products, arithmetic and copies ran while one was open for 22% of the time, Pallas kernels for 0%

commit v1 on v0

v1 whole, which is shorter than its diff:
```python
import functools

import jax
import jax.numpy as jnp
from jax import lax
from jax.experimental import pallas as pl
from jax.experimental.pallas import tpu as pltpu
from jax.sharding import PartitionSpec as P

SPREAD = 6
PASSES = 4
HALO = 4
BF16 = jnp.bfloat16
F32 = jnp.float32
CONTRACT_LANES = (((1,), (1,)), ((), ()))


def bump(distance):
    scaled = distance * F32(1.0 / SPREAD)
    return jnp.square(jnp.maximum(0.0, 1.0 - scaled * scaled))


def two_parts(values):
    high = values.astype(BF16)
    return high, (values - high.astype(F32)).astype(BF16)


def dot_lanes(left, right):
    return lax.dot_general(left, right, CONTRACT_LANES, preferred_element_type=F32)


def pack_kernel(sides, res, azi, ele, brick, cell, force, px, py, pz, kappa, sigma, payload, *slabs):
    size_x = kappa.shape[0]
    cosine = jnp.cos(ele[0])
    value = res[0]
    payload[0:1, :] = cosine * jnp.cos(azi[0]) * value
    payload[1:2, :] = cosine * jnp.sin(azi[0]) * value
    payload[2:3, :] = jnp.sin(ele[0]) * value
    payload[3:4, :] = brick[...].astype(F32)
    payload[4:5, :] = cell[0].astype(F32)
    points = px.shape[1]
    payload[5:8, :] = jnp.zeros((3, payload.shape[1]), F32)
    for c in range(3):
        payload[5:6, c * points : (c + 1) * points] = force[c]
    payload[5:6, 3 * points : 4 * points] = px[...]
    payload[6:7, 0:points] = py[...]
    payload[6:7, points : 2 * points] = pz[...]
    if sides == 1:
        starts = [jnp.where(lax.axis_index("stream") == 0, size_x - HALO, 0)]
    else:
        starts = [size_x - HALO, 0]
    for slab, start in zip(slabs, starts):
        slab[0] = kappa[pl.ds(start, HALO)]
        slab[1] = sigma[pl.ds(start, HALO)]


def sort_kernel(spans, sides, count, *refs):
    payloads, (kappa, sigma), slabs, (rows, to_upper, to_lower) = (
        refs[:count],
        refs[count : count + 2],
        refs[count + 2 : count + 2 + sides],
        refs[count + 2 + sides :],
    )
    size_x, size_y, size_z = kappa.shape
    ext_y = size_y + 2 * HALO
    me = lax.axis_index("span")

    def payload_of(j):
        return payloads[j] if count > 1 else payloads[0].at[j]

    for j in range(spans):
        one = payload_of(j)
        brick = one[3:4, :].astype(jnp.int32)
        cell = one[4:5, :].astype(jnp.int32)
        away = brick - me
        away = jnp.where(away < 0, away + spans, away)
        x = cell // (size_y * size_z)
        y = cell // size_z % size_y
        z = cell % size_z
        row = jnp.where(
            away == 0,
            y,
            jnp.where(
                (away == 1) & (y < HALO),
                y + size_y,
                jnp.where((away == spans - 1) & (y >= size_y - HALO), y + 2 * HALO, -1),
            ),
        )
        place = jnp.where(row < 0, -1, (x * ext_y + row) * size_z + z)
        rows[j, 0:3, :] = one[0:3, :]
        rows[j, 3:4, :] = place.astype(F32)
    points = rows.shape[2] // 4
    rows[spans] = jnp.zeros(rows.shape[1:], F32)
    rows[spans + 1] = jnp.zeros(rows.shape[1:], F32)
    near = (0, 1, 2) if count > 1 else (0, spans - 1, 1)
    for k, (j, offset) in enumerate(zip(near, (0, -1, 1))):
        one = payload_of(j)
        lanes = slice(k * points, (k + 1) * points)
        for c in range(4):
            rows[spans, c : c + 1, lanes] = one[5:6, c * points : (c + 1) * points]
        rows[spans + 1, 0:1, lanes] = one[6:7, 0:points] + F32(offset * size_y)
        rows[spans + 1, 1:2, lanes] = one[6:7, points : 2 * points]
    for x in range(size_x + sides * HALO):
        if x < size_x:
            kap, sig = kappa.at[x], sigma.at[x]
        else:
            slab = slabs[(x - size_x) // HALO]
            kap, sig = slab.at[0, (x - size_x) % HALO], slab.at[1, (x - size_x) % HALO]
        to_upper[x, 0:HALO] = kap[size_y - HALO :]
        to_upper[x, HALO:] = sig[size_y - HALO :]
        to_lower[x, 0:HALO] = kap[0:HALO]
        to_lower[x, HALO:] = sig[0:HALO]


def spread(spans, rows, out, start_x, planes, ext_y, size_z):
    height = planes * ext_y
    shift = start_x * ext_y
    points = rows.shape[2] // 4 * 3
    px = rows[spans, 3:4, 0:points]
    py = rows[spans + 1, 0:1, 0:points]
    pz = rows[spans + 1, 1:2, 0:points]
    size_y = ext_y - 2 * HALO
    y_row = lax.broadcasted_iota(jnp.int32, (ext_y, points), 0)
    y_cell = jnp.where(y_row < size_y + HALO, y_row, y_row - ext_y).astype(F32)
    by = bump(y_cell - py)
    x_cell = (lax.broadcasted_iota(jnp.int32, (planes, points), 0) + start_x).astype(F32)
    bx = bump(x_cell - px)
    z_cell = lax.broadcasted_iota(jnp.int32, (size_z, points), 0) + lax.axis_index("vert") * size_z
    bz_high, bz_low = two_parts(bump(z_cell.astype(F32) - pz))
    cross = jnp.concatenate([by * bx[x : x + 1] for x in range(planes)], axis=0)
    for c in range(3):
        high, low = two_parts(cross * rows[spans, c : c + 1, 0:points])
        out[c] = dot_lanes(high, bz_high) + dot_lanes(low, bz_high) + dot_lanes(high, bz_low)

    gates = rows.shape[2]
    chunk = 512
    row_id = lax.broadcasted_iota(jnp.int32, (height, chunk), 0)
    z_id = lax.broadcasted_iota(jnp.int32, (size_z, chunk), 0)

    def one_chunk(step, carry):
        j = step // (gates // chunk)
        lanes = pl.ds(pl.multiple_of(step % (gates // chunk) * chunk, chunk), chunk)
        place = rows[j, 3:4, lanes].astype(jnp.int32)
        line = (place >> (size_z.bit_length() - 1)) - shift
        line = jnp.where(place < 0, -1, line)
        pick = jnp.where(row_id == line, 1.0, 0.0).astype(BF16)
        pick_z = jnp.where(z_id == (place & (size_z - 1)), 1.0, 0.0).astype(BF16)
        for c in range(3):
            high, low = two_parts(rows[j, c : c + 1, lanes])
            out[c] += dot_lanes(pick * high, pick_z) + dot_lanes(pick * low, pick_z)
        return carry

    lax.fori_loop(0, spans * (gates // chunk), one_chunk, 0)


def own_kernel(spans, size_x, ext_y, size_z, rows, out):
    spread(spans, rows, out, 0, size_x, ext_y, size_z)


def extend_kernel(spans, sides, *refs):
    others = refs[:sides]
    own, kappa, sigma = refs[sides : sides + 3]
    slabs = refs[sides + 3 : 2 * sides + 3]
    upper, lower = refs[2 * sides + 3 : 2 * sides + 5]
    source, kappa_ext, face = refs[2 * sides + 5 : 2 * sides + 8]
    strips = refs[2 * sides + 8 :]
    size_x, size_y, size_z = kappa.shape
    ext_y = size_y + 2 * HALO
    if sides == 1:
        starts = [jnp.where(lax.axis_index("stream") == 0, 0, size_x - HALO)]
    else:
        starts = [0, size_x - HALO]
    for rows, strip, start in zip(others, strips, starts):
        spread(spans, rows, strip, start, HALO, ext_y, size_z)
    lanes = face.shape[3]
    side = pl.ds(pl.multiple_of(jnp.where(lax.axis_index("vert") == 0, size_z - lanes, 0), lanes), lanes)
    for x in range(size_x + sides * HALO):
        if x < size_x:
            kap, sig = kappa[x], sigma[x]
        else:
            slab = slabs[(x - size_x) // HALO]
            kap, sig = slab[0, (x - size_x) % HALO], slab[1, (x - size_x) % HALO]
        kappa_ext[x] = jnp.concatenate([kap, upper[x, 0:HALO], lower[x, 0:HALO]], axis=0)
        sig = jnp.concatenate([sig, upper[x, HALO:], lower[x, HALO:]], axis=0)
        for c in range(3):
            if x < size_x:
                value = own[c, x * ext_y : (x + 1) * ext_y, :]
            else:
                place = (x - size_x) % HALO * ext_y
                value = strips[(x - size_x) // HALO][c, place : place + ext_y, :]
            source[c, x] = value * sig
            face[c, x] = source[c, x, :, side]
        face[3, x] = kappa_ext[x, :, side]


def diffuse_kernel(sides, source, kappa_ext, face, out, ping, pong, root, ax, ay, aym, az, azm, keep):
    planes, ext_y, size_z = kappa_ext.shape
    size_x, size_y = out.shape[1], out.shape[2]
    lanes = face.shape[3]
    ext_z = size_z + lanes
    stream, vert = lax.axis_index("stream"), lax.axis_index("vert")

    def fill(x, carry):
        for c in range(3):
            ping[c, x, :, 0:size_z] = source[c, x]
            ping[c, x, :, size_z:] = face[c, x]
        root[x, :, 0:size_z] = jnp.sqrt(kappa_ext[x])
        root[x, :, size_z:] = jnp.sqrt(face[3, x])
        return carry

    lax.fori_loop(0, planes, fill, 0)
    lane = lax.broadcasted_iota(jnp.int32, (ext_y, ext_z), 1)
    wall_z = jnp.where(lane == jnp.where(vert == 0, ext_z - 1, size_z - 1), 0.0, 1.0)
    last = lax.axis_size("stream") - 1

    def faces(x, carry):
        after = jnp.where(x == planes - 1, 0, x + 1)
        here = root[x]
        if sides == 1:
            wall = ((x == planes - 1) & (stream == 0)) | ((x == size_x - 1) & (stream == 1))
        else:
            wall = ((x == planes - 1) & (stream == 0)) | ((x == size_x - 1) & (stream == last))
        ax[x] = here * root[after] * jnp.where(wall, 0.0, 1.0)
        up = here * pltpu.roll(here, ext_y - 1, 0)
        ay[x] = up
        aym[x] = pltpu.roll(up, 1, 0)
        up = here * pltpu.roll(here, ext_z - 1, 1) * wall_z
        az[x] = up
        azm[x] = pltpu.roll(up, 1, 1)
        return carry

    lax.fori_loop(0, planes, faces, 0)

    def total(x, carry):
        before = jnp.where(x == 0, planes - 1, x - 1)
        keep[x] = 1.0 - (ax[x] + ax[before] + ay[x] + aym[x] + az[x] + azm[x])
        return carry

    lax.fori_loop(0, planes, total, 0)

    for p in range(PASSES):
        deep = PASSES - 1 - p
        old, new = (ping, pong) if p % 2 == 0 else (pong, ping)
        first = jnp.where(stream == 0, 0, planes - deep) if sides == 1 else planes - deep

        def one_plane(i, carry, old=old, new=new, first=first, p=p):
            x = i + first
            x = jnp.where(x >= planes, x - planes, x)
            after = jnp.where(x == planes - 1, 0, x + 1)
            before = jnp.where(x == 0, planes - 1, x - 1)
            for c in range(3):
                value = old[c, x]
                moved = keep[x] * value
                moved += ax[x] * old[c, after] + ax[before] * old[c, before]
                moved += ay[x] * pltpu.roll(value, ext_y - 1, 0) + aym[x] * pltpu.roll(value, 1, 0)
                moved += az[x] * pltpu.roll(value, ext_z - 1, 1) + azm[x] * pltpu.roll(value, 1, 1)
                if p == PASSES - 1:
                    out[c, x] = moved[0:size_y, 0:size_z]
                else:
                    new[c, x] = moved
            return carry

        lax.fori_loop(0, size_x + sides * deep, one_plane, 0)


def call(kernel, outs, scratch, flops, *args):
    moved = sum(4 * a.size for a in args) + sum(4 * o.size for o in outs)
    return pl.pallas_call(
        kernel,
        out_shape=outs,
        in_specs=[pl.BlockSpec(memory_space=pltpu.VMEM)] * len(args),
        out_specs=[pl.BlockSpec(memory_space=pltpu.VMEM)] * len(outs),
        scratch_shapes=scratch,
        compiler_params=pltpu.CompilerParams(vmem_limit_bytes=56 * 1024 * 1024),
        cost_estimate=pl.CostEstimate(flops=flops, bytes_accessed=moved, transcendentals=0),
    )(*args)


def ring(array, step):
    count = lax.axis_size("span")
    return lax.ppermute(array, "span", [(i, (i + step) % count) for i in range(count)])


def across_bands(arrays):
    count = lax.axis_size("stream")
    if count == 2:
        return [lax.ppermute(arrays[0], "stream", [(0, 1), (1, 0)])]
    return [
        lax.ppermute(arrays[1], "stream", [(i + 1, i) for i in range(count - 1)]),
        lax.ppermute(arrays[0], "stream", [(i, i + 1) for i in range(count - 1)]),
    ]


def on_device(
    kappa,
    sigma,
    gate_residual,
    gate_azimuth,
    gate_elevation,
    gate_brick,
    gate_cell,
    blade_force,
    point_x,
    point_y,
    point_z,
):
    size_x, size_y, size_z = kappa.shape
    spans = lax.axis_size("span")
    sides = 1 if lax.axis_size("stream") == 2 else 2
    gates = gate_residual.shape[2]
    lanes = 128
    ext_x, ext_y = size_x + sides * HALO, size_y + 2 * HALO
    shape = lambda *dims: jax.ShapeDtypeStruct(dims, F32)
    payload, *slabs = call(
        functools.partial(pack_kernel, sides),
        [shape(8, gates)] + [shape(2, HALO, size_y, size_z)] * sides,
        [],
        1000,
        gate_residual,
        gate_azimuth,
        gate_elevation,
        gate_brick.reshape(1, gates),
        gate_cell,
        blade_force,
        point_x,
        point_y,
        point_z,
        kappa,
        sigma,
    )
    if spans == 4:
        payloads = [payload, ring(payload, 1), ring(payload, -1), ring(payload, 2)]
    else:
        gathered = lax.all_gather(payload, "span")
        payloads = [jnp.roll(gathered, -lax.axis_index("span"), axis=0)]
    slabs = across_bands(slabs)
    rows, to_upper, to_lower = call(
        functools.partial(sort_kernel, spans, sides, len(payloads)),
        [shape(spans + 2, 4, gates), shape(ext_x, 2 * HALO, size_z), shape(ext_x, 2 * HALO, size_z)],
        [],
        1000,
        *payloads,
        kappa,
        sigma,
        *slabs,
    )
    others = across_bands([rows] * sides)
    from_lower, from_upper = ring(to_upper, 1), ring(to_lower, -1)
    (own,) = call(
        functools.partial(own_kernel, spans, size_x, ext_y, size_z),
        [shape(3, size_x * ext_y, size_z)],
        [],
        12 * size_x * ext_y * size_z * spans * gates,
        rows,
    )
    source, kappa_ext, face = call(
        functools.partial(extend_kernel, spans, sides),
        [shape(3, ext_x, ext_y, size_z), shape(ext_x, ext_y, size_z), shape(4, ext_x, ext_y, lanes)],
        [pltpu.VMEM((3, HALO * ext_y, size_z), F32)] * sides,
        12 * HALO * ext_y * size_z * spans * gates,
        *others,
        own,
        kappa,
        sigma,
        *slabs,
        from_upper,
        from_lower,
    )
    face = lax.ppermute(face, "vert", [(0, 1), (1, 0)])
    wide = (ext_x, ext_y, size_z + lanes)
    (field,) = call(
        functools.partial(diffuse_kernel, sides),
        [shape(3, size_x, size_y, size_z)],
        [pltpu.VMEM((3, *wide), F32)] * 2 + [pltpu.VMEM(wide, F32)] * 7,
        60 * 3 * ext_x * ext_y * size_z,
        source,
        kappa_ext,
        face,
    )
    return field


def solution(mesh):
    placed = (
        P(("grp", "stream"), "span", "vert"),
        P(("grp", "stream"), "span", "vert"),
        P(("grp", "stream"), "vert", "span"),
        P(("grp", "stream"), "vert", "span"),
        P(("grp", "stream"), "vert", "span"),
        P(("grp", "stream"), "vert", "span", None),
        P(("grp", "stream"), "vert", "span"),
        P(None, ("grp", "stream"), "span"),
        P(("grp", "stream"), "span"),
        P(("grp", "stream"), "span"),
        P(("grp", "stream"), "span"),
    )
    return jax.shard_map(
        on_device,
        mesh=mesh,
        in_specs=placed,
        out_specs=P(None, ("grp", "stream"), "span", "vert"),
        check_vma=False,
    )
```

time: 199 us -> 61.5 us (0.31)
  other arithmetic: 64.2 us -> 0 us
  local copies, waits for them, and re-layouts: 57.2 us -> 3.56 us
  Pallas kernels: 0 us -> 39.5 us
  starting transfers between devices: 40.6 us -> 10.1 us
  waiting for transfers between devices: 30.4 us -> 8.02 us
  matrix products: 4.53 us -> 0 us
    pallas_call x0 -> x5, Pallas kernels: none -> 39.5 us  [call(): pl.pallas_call(kernel, out_shape=outs, in_specs=[pl.BlockSpec(memory_spac...]
    scatter-add x1 -> x0, other arithmetic: 34.4 us -> none  [on_device(): jnp.zeros((3, size_x * size_y * size_z), jnp.float32).at[:, flat_cells]]
    reshape x3 -> x0, local copies, waits for them, and re-layouts: 21.9 us -> none  [the longest x1 19.5 us: on_device(): field = (lidar.reshape(3, size_x, size_y, size_z) + rotor) * sigma[None]]
    ppermute x32 -> x8, starting transfers between devices: 30.4 us -> 10.1 us  [the longest x5 6.64 us: ring(): lax.ppermute(array, 'span', [(i, (i + step) % count) for i in range(count)])]
    mul x18 -> x0, other arithmetic: 19.9 us -> none  [the longest x4 7.1 us: diffuse_once(): along_z[1:-1, 1:-1, :]]
    ppermute x32 -> x8, waiting for transfers between devices: 26.6 us -> 8.02 us  [the longest x5 5.25 us: ring(): lax.ppermute(array, 'span', [(i, (i + step) % count) for i in range(count)])]
    ppermute x8 -> x0, local copies, waits for them, and re-layouts: 12.1 us -> none  [the longest x4 7.3 us: with_halo(): lax.ppermute(head, axis, [((i + 1) % count, i) for i in range(count)])]
    slice x23 -> x0, local copies, waits for them, and re-layouts: 11.9 us -> none  [the longest x9 5.39 us: with_halo(): head = lax.slice_in_dim(cells, 0, width, axis=dim)]
  transfers between devices with their start and end apart: 34 -> 8, of which waited for: 20 -> 4; matrix products, arithmetic and copies ran while one was open for 22% -> 0% of each run, Pallas kernels for 0% -> 17%
where the time goes in v1:
time: 61.5 us; the launch traced here: 61.3 us
  Pallas kernels  39.5 us (64%)
  starting transfers between devices  10.1 us (16%)
  waiting for transfers between devices  8.02 us (13%)
  local copies, waits for them, and re-layouts  3.56 us (6%)
    pallas_call x5, Pallas kernels, call(): pl.pallas_call(kernel, out_shape=outs, in_specs=[pl.BlockSpec(memory_spac...  39.5 us
    ppermute x5, starting transfers between devices, ring(): lax.ppermute(array, 'span', [(i, (i + step) % count) for i in range(count)])  6.64 us
    ppermute x5, waiting for transfers between devices, ring(): lax.ppermute(array, 'span', [(i, (i + step) % count) for i in range(count)])  5.25 us
    unnamed x16, local copies, waits for them, and re-layouts  3.56 us
    ppermute x2, starting transfers between devices, across_bands(): return [lax.ppermute(arrays[0], 'stream', [(0, 1), (1, 0)])]  3.47 us
    ppermute x1, waiting for transfers between devices, on_device(): face = lax.ppermute(face, 'vert', [(0, 1), (1, 0)])  2.77 us
  transfers between devices with their start and end apart: 8, of which 4 were waited for; matrix products, arithmetic and copies ran while one was open for 0% of the time, Pallas kernels for 17%

profile of v1, /device:TPU:0, one launch (start us, length us, event | category | flops | bytes accessed | tf_op | source)
XLA Modules:
  0.0 61.3 jit_solution(12435539838109809014)
XLA Ops:
  0.0 1.8 %shard_map.109 = (f32[8,1024]{1,0:T(8,128)}, f32[2,4,16,256]{3,2,1,0:T(8,128)}) custom-call(f32[1,1,1024]{2,1,0:T(1,128)} %res.1, f32[1,1,1024]{2,1,0:T(1,128)} %azi.1, f32[1,1,1024]{2,1,0:T(1,128)} %ele.1, s32[1,1024]{1,0:T(1,128)} %bitcast.1, s32[1,1,1024]{2,1,0:T(1,128)} %cell.1, f32[3,1,256]{2,1,0:T(1,128)} %force.1, f32[1,256]{1,0:T(1,128)} %px.1, ...), custom_call_target="tpu_custom_call" | custom-call | flops 1000 | bytes 714752 | tf_op jit(solution)/shard_map/pallas_call | solution.py:268
  1.8 2.9 %collective-permute-start.3 = (f32[2,4,16,256]{3,2,1,0:T(8,128)}, f32[2,4,16,256]{3,2,1,0:T(8,128)S(1)}, u32[]{:S(2)}, u32[]{:S(2)}) collective-permute-start(f32[2,4,16,256]{3,2,1,0:T(8,128)} %get-tuple-element.14), channel_id=1, source_target_pairs={{0,2},{2,0},{1,3},{3,1},{4,6},{6,4},{5,7},{7,5},{8,10},{10,8},{9,1... | collective-permute-start | bytes 393224 | tf_op jit(solution)/shard_map/ppermute | solution.py:287
  4.8 2.6 %collective-permute-start.2 = (f32[8,1024]{1,0:T(8,128)}, f32[8,1024]{1,0:T(8,128)S(1)}, u32[]{:S(2)}, u32[]{:S(2)}) collective-permute-start(f32[8,1024]{1,0:T(8,128)} %get-tuple-element.13.refs_0_), channel_id=1, source_target_pairs={{0,8},{4,12},{8,0},{12,4},{1,9},{5,13},{9,1},{13,5},{2,10},{6,14},... | collective-permute-start | bytes 98312 | tf_op jit(solution)/shard_map/ppermute | solution.py:281
  7.4 1.3 %collective-permute-start.1 = (f32[8,1024]{1,0:T(8,128)}, f32[8,1024]{1,0:T(8,128)S(1)}, u32[]{:S(2)}, u32[]{:S(2)}) collective-permute-start(f32[8,1024]{1,0:T(8,128)} %get-tuple-element.13.refs_0_), channel_id=1, source_target_pairs={{0,12},{4,0},{8,4},{12,8},{1,13},{5,1},{9,5},{13,9},{2,14},{6,2},{... | collective-permute-start | bytes 98312 | tf_op jit(solution)/shard_map/ppermute | solution.py:281
  8.7 0.7 %collective-permute-start = (f32[8,1024]{1,0:T(8,128)}, f32[8,1024]{1,0:T(8,128)S(1)}, u32[]{:S(2)}, u32[]{:S(2)}) collective-permute-start(f32[8,1024]{1,0:T(8,128)} %get-tuple-element.13.refs_0_), channel_id=1, source_target_pairs={{0,4},{4,8},{8,12},{12,0},{1,5},{5,9},{9,13},{13,1},{2,6},{6,10},{... | collective-permute-start | bytes 98312 | tf_op jit(solution)/shard_map/ppermute | solution.py:281
  9.4 0.5 collective-permute-done.2.refs_3_
  9.9 0.0 copy-start.2
  9.9 1.6 %collective-permute-done.1.refs_2_ = f32[8,1024]{1,0:T(8,128)S(1)} collective-permute-done((f32[8,1024]{1,0:T(8,128)}, f32[8,1024]{1,0:T(8,128)S(1)}, u32[]{:S(2)}, u32[]{:S(2)}) %collective-permute-start.1) | collective-permute-done | bytes 32800 | tf_op jit(solution)/shard_map/ppermute | solution.py:281
  11.5 0.0 copy-start.3
  11.5 3.1 %collective-permute-done.refs_1_ = f32[8,1024]{1,0:T(8,128)S(1)} collective-permute-done((f32[8,1024]{1,0:T(8,128)}, f32[8,1024]{1,0:T(8,128)S(1)}, u32[]{:S(2)}, u32[]{:S(2)}) %collective-permute-start) | collective-permute-done | bytes 32800 | tf_op jit(solution)/shard_map/ppermute | solution.py:281
  14.6 0.0 collective-permute-done.3.refs_6_.refs_4_
  14.6 0.0 copy-done.2
  14.6 0.0 copy-done.3
  14.7 0.6 copy-done.4
  15.3 0.7 %copy-done.1 = f32[2,4,16,256]{3,2,1,0:T(8,128)} copy-done((f32[2,4,16,256]{3,2,1,0:T(8,128)}, f32[2,4,16,256]{3,2,1,0:T(8,128)S(1)}, u32[]{:S(2)}) %copy-start.1) | copy-done | bytes 131096
  15.9 1.9 %shard_map.110 = (f32[6,4,1024]{2,1,0:T(4,128)}, f32[20,8,256]{2,1,0:T(8,128)}, f32[20,8,256]{2,1,0:T(8,128)}) custom-call(f32[8,1024]{1,0:T(8,128)} %get-tuple-element.13.refs_0_, f32[8,1024]{1,0:T(8,128)} %copy-done.4, f32[8,1024]{1,0:T(8,128)} %copy-done.3, f32[8,1024]{1,0:T(8,128)} %copy-done.2, f32[16,16,256]{2,1,0:T(8,128)} %refs_2_.1, ...), custom_call_target="tpu_custom_call" | custom-call | flops 1000 | bytes 1212416 | tf_op jit(solution)/shard_map/pallas_call | solution.py:268
  17.9 0.5 collective-permute-start.4
  18.4 0.0 collective-permute-start.5
  18.4 2.0 %collective-permute-start.6 = (f32[20,8,256]{2,1,0:T(8,128)}, f32[20,8,256]{2,1,0:T(8,128)S(1)}, u32[]{:S(2)}, u32[]{:S(2)}) collective-permute-start(f32[20,8,256]{2,1,0:T(8,128)} %get-tuple-element.17), channel_id=1, source_target_pairs={{0,4},{4,8},{8,12},{12,0},{1,5},{5,9},{9,13},{13,1},{2,6},{6,10},{... | collective-permute-start | bytes 491528 | tf_op jit(solution)/shard_map/ppermute | solution.py:281
  20.4 10.3 %shard_map.111.refs_1_ = f32[3,384,256]{2,1,0:T(8,128)} custom-call(f32[6,4,1024]{2,1,0:T(4,128)} %get-tuple-element.15.rows), custom_call_target="tpu_custom_call" | custom-call | flops 4831838208 | bytes 1277952 | tf_op jit(solution)/shard_map/pallas_call | solution.py:268
  30.7 0.0 collective-permute-done.4.refs_0_
  30.7 0.0 collective-permute-done.5.refs_5_
  30.8 0.0 copy-start.5
  30.8 0.0 collective-permute-done.6.refs_6_
  30.8 0.6 %copy-done.7 = f32[6,4,1024]{2,1,0:T(4,128)} copy-done((f32[6,4,1024]{2,1,0:T(4,128)}, f32[6,4,1024]{2,1,0:T(4,128)S(1)}, u32[]{:S(2)}) %copy-start.7) | copy-done | bytes 98328
  31.4 0.1 copy-done.5
  31.5 0.7 %copy-done.6 = f32[20,8,256]{2,1,0:T(8,128)} copy-done((f32[20,8,256]{2,1,0:T(8,128)}, f32[20,8,256]{2,1,0:T(8,128)S(1)}, u32[]{:S(2)}) %copy-start.6) | copy-done | bytes 163864
  32.1 9.6 %shard_map.112 = (f32[3,20,24,256]{3,2,1,0:T(8,128)}, f32[20,24,256]{2,1,0:T(8,128)}, f32[4,20,24,128]{3,2,1,0:T(8,128)}) custom-call(f32[6,4,1024]{2,1,0:T(4,128)} %copy-done.7, f32[3,384,256]{2,1,0:T(8,128)} %shard_map.111.refs_1_, f32[16,16,256]{2,1,0:T(8,128)} %refs_2_.1, f32[16,16,256]{2,1,0:T(8,128)} %refs_3_.1, f32[2,4,16,256]{3,2,1,0:T(8,128)} %copy-done.1, ...), custom_call_target="tpu_custom_call" | custom-call | flops 1207959552 | bytes 5210112 | tf_op jit(solution)/shard_map/pallas_call | solution.py:268
  41.7 0.0 collective-permute-start.7
  41.7 2.8 %collective-permute-done.7.face = f32[4,20,24,128]{3,2,1,0:T(8,128)S(1)} collective-permute-done((f32[4,20,24,128]{3,2,1,0:T(8,128)}, f32[4,20,24,128]{3,2,1,0:T(8,128)S(1)}, u32[]{:S(2)}, u32[]{:S(2)}) %collective-permute-start.7) | collective-permute-done | bytes 983072 | tf_op jit(solution)/shard_map/ppermute | solution.py:369
  44.5 1.0 %copy-done = f32[4,20,24,128]{3,2,1,0:T(8,128)} copy-done((f32[4,20,24,128]{3,2,1,0:T(8,128)}, f32[4,20,24,128]{3,2,1,0:T(8,128)S(1)}, u32[]{:S(2)}) %copy-start) | copy-done | bytes 983064
  45.4 15.8 %shard_map.113 = f32[3,16,16,256]{3,2,1,0:T(8,128)} custom-call(f32[3,20,24,256]{3,2,1,0:T(8,128)} %get-tuple-element.18.source, f32[20,24,256]{2,1,0:T(8,128)} %get-tuple-element.19.kappa_ext, f32[4,20,24,128]{3,2,1,0:T(8,128)} %copy-done), custom_call_target="tpu_custom_call" | custom-call | flops 22118400 | bytes 3735552 | tf_op jit(solution)/shard_map/pallas_call | solution.py:268
  (5 shorter events, 0.0 us)
Async XLA Ops:
  1.8 12.8 %collective-permute-start.3 = (f32[2,4,16,256]{3,2,1,0:T(8,128)}, f32[2,4,16,256]{3,2,1,0:T(8,128)S(1)}, u32[]{:S(2)}, u32[]{:S(2)}) collective-permute-start(f32[2,4,16,256]{3,2,1,0:T(8,128)} %get-tuple-element.14), channel_id=1, source_target_pairs={{0,2},{2,0},{1,3},{3,1},{4,6},{6,4},{5,7},{7,5},{8,10},{10,8},{9,1... | collective-permute-start | bytes 393224 | tf_op jit(solution)/shard_map/ppermute | solution.py:287
  4.8 5.1 %collective-permute-start.2 = (f32[8,1024]{1,0:T(8,128)}, f32[8,1024]{1,0:T(8,128)S(1)}, u32[]{:S(2)}, u32[]{:S(2)}) collective-permute-start(f32[8,1024]{1,0:T(8,128)} %get-tuple-element.13.refs_0_), channel_id=1, source_target_pairs={{0,8},{4,12},{8,0},{12,4},{1,9},{5,13},{9,1},{13,5},{2,10},{6,14},... | collective-permute-start | bytes 98312 | tf_op jit(solution)/shard_map/ppermute | solution.py:281
  7.4 4.1 %collective-permute-start.1 = (f32[8,1024]{1,0:T(8,128)}, f32[8,1024]{1,0:T(8,128)S(1)}, u32[]{:S(2)}, u32[]{:S(2)}) collective-permute-start(f32[8,1024]{1,0:T(8,128)} %get-tuple-element.13.refs_0_), channel_id=1, source_target_pairs={{0,12},{4,0},{8,4},{12,8},{1,13},{5,1},{9,5},{13,9},{2,14},{6,2},{... | collective-permute-start | bytes 98312 | tf_op jit(solution)/shard_map/ppermute | solution.py:281
  8.7 5.9 %collective-permute-start = (f32[8,1024]{1,0:T(8,128)}, f32[8,1024]{1,0:T(8,128)S(1)}, u32[]{:S(2)}, u32[]{:S(2)}) collective-permute-start(f32[8,1024]{1,0:T(8,128)} %get-tuple-element.13.refs_0_), channel_id=1, source_target_pairs={{0,4},{4,8},{8,12},{12,0},{1,5},{5,9},{9,13},{13,1},{2,6},{6,10},{... | collective-permute-start | bytes 98312 | tf_op jit(solution)/shard_map/ppermute | solution.py:281
  9.9 4.7 %copy-start.2 = (f32[8,1024]{1,0:T(8,128)}, f32[8,1024]{1,0:T(8,128)S(1)}, u32[]{:S(2)}) copy-start(f32[8,1024]{1,0:T(8,128)S(1)} %collective-permute-done.2.refs_3_) | copy-start | bytes 98308
  11.5 3.2 %copy-start.3 = (f32[8,1024]{1,0:T(8,128)}, f32[8,1024]{1,0:T(8,128)S(1)}, u32[]{:S(2)}) copy-start(f32[8,1024]{1,0:T(8,128)S(1)} %collective-permute-done.1.refs_2_) | copy-start | bytes 98308
  14.6 0.6 %copy-start.4 = (f32[8,1024]{1,0:T(8,128)}, f32[8,1024]{1,0:T(8,128)S(1)}, u32[]{:S(2)}) copy-start(f32[8,1024]{1,0:T(8,128)S(1)} %collective-permute-done.refs_1_) | copy-start | bytes 98308
  15.3 0.7 %copy-start.1 = (f32[2,4,16,256]{3,2,1,0:T(8,128)}, f32[2,4,16,256]{3,2,1,0:T(8,128)S(1)}, u32[]{:S(2)}) copy-start(f32[2,4,16,256]{3,2,1,0:T(8,128)S(1)} %collective-permute-done.3.refs_6_.refs_4_) | copy-start | bytes 393220
  17.9 12.9 %collective-permute-start.4 = (f32[6,4,1024]{2,1,0:T(4,128)}, f32[6,4,1024]{2,1,0:T(4,128)S(1)}, u32[]{:S(2)}, u32[]{:S(2)}) collective-permute-start(f32[6,4,1024]{2,1,0:T(4,128)} %get-tuple-element.15.rows), channel_id=1, source_target_pairs={{0,2},{2,0},{1,3},{3,1},{4,6},{6,4},{5,7},{7,5},{8,10},{10,8},{9,1... | collective-permute-start | bytes 294920 | tf_op jit(solution)/shard_map/ppermute | solution.py:287
  18.4 12.4 %collective-permute-start.5 = (f32[20,8,256]{2,1,0:T(8,128)}, f32[20,8,256]{2,1,0:T(8,128)S(1)}, u32[]{:S(2)}, u32[]{:S(2)}) collective-permute-start(f32[20,8,256]{2,1,0:T(8,128)} %get-tuple-element.16), channel_id=1, source_target_pairs={{0,12},{4,0},{8,4},{12,8},{1,13},{5,1},{9,5},{13,9},{2,14},{6,2},{... | collective-permute-start | bytes 491528 | tf_op jit(solution)/shard_map/ppermute | solution.py:281
  18.4 12.4 %collective-permute-start.6 = (f32[20,8,256]{2,1,0:T(8,128)}, f32[20,8,256]{2,1,0:T(8,128)S(1)}, u32[]{:S(2)}, u32[]{:S(2)}) collective-permute-start(f32[20,8,256]{2,1,0:T(8,128)} %get-tuple-element.17), channel_id=1, source_target_pairs={{0,4},{4,8},{8,12},{12,0},{1,5},{5,9},{9,13},{13,1},{2,6},{6,10},{... | collective-permute-start | bytes 491528 | tf_op jit(solution)/shard_map/ppermute | solution.py:281
  30.7 0.7 %copy-start.7 = (f32[6,4,1024]{2,1,0:T(4,128)}, f32[6,4,1024]{2,1,0:T(4,128)S(1)}, u32[]{:S(2)}) copy-start(f32[6,4,1024]{2,1,0:T(4,128)S(1)} %collective-permute-done.4.refs_0_) | copy-start | bytes 294916
  30.8 0.7 %copy-start.5 = (f32[20,8,256]{2,1,0:T(8,128)}, f32[20,8,256]{2,1,0:T(8,128)S(1)}, u32[]{:S(2)}) copy-start(f32[20,8,256]{2,1,0:T(8,128)S(1)} %collective-permute-done.5.refs_5_) | copy-start | bytes 491524
  31.5 0.7 %copy-start.6 = (f32[20,8,256]{2,1,0:T(8,128)}, f32[20,8,256]{2,1,0:T(8,128)S(1)}, u32[]{:S(2)}) copy-start(f32[20,8,256]{2,1,0:T(8,128)S(1)} %collective-permute-done.6.refs_6_) | copy-start | bytes 491524
  41.7 2.8 %collective-permute-start.7 = (f32[4,20,24,128]{3,2,1,0:T(8,128)}, f32[4,20,24,128]{3,2,1,0:T(8,128)S(1)}, u32[]{:S(2)}, u32[]{:S(2)}) collective-permute-start(f32[4,20,24,128]{3,2,1,0:T(8,128)} %get-tuple-element.20), channel_id=1, source_target_pairs={{0,1},{1,0},{2,3},{3,2},{4,5},{5,4},{6,7},{7,6},{8,9},{9,8},{10,11... | collective-permute-start | bytes 2949128 | tf_op jit(solution)/shard_map/ppermute | solution.py:369
  44.5 1.0 %copy-start = (f32[4,20,24,128]{3,2,1,0:T(8,128)}, f32[4,20,24,128]{3,2,1,0:T(8,128)S(1)}, u32[]{:S(2)}) copy-start(f32[4,20,24,128]{3,2,1,0:T(8,128)S(1)} %collective-permute-done.7.face) | copy-start | bytes 2949124

commit v2 on v1

v2 whole, which is shorter than its diff:
```python
import functools

import jax
import jax.numpy as jnp
from jax import lax
from jax.experimental import pallas as pl
from jax.experimental.pallas import tpu as pltpu
from jax.sharding import PartitionSpec as P

SPREAD = 6
PASSES = 4
HALO = 4
BF16 = jnp.bfloat16
F32 = jnp.float32
CONTRACT_LANES = (((1,), (1,)), ((), ()))


def bump(distance):
    scaled = distance * F32(1.0 / SPREAD)
    return jnp.square(jnp.maximum(0.0, 1.0 - scaled * scaled))


def two_parts(values):
    high = values.astype(BF16)
    return high, (values - high.astype(F32)).astype(BF16)


def dot_lanes(left, right):
    return lax.dot_general(left, right, CONTRACT_LANES, preferred_element_type=F32)


def pack_kernel(residual, azimuth, elevation, brick, cell, force, px, py, pz, kappa, sigma, payload, to_upper, to_lower):
    cosine = jnp.cos(elevation[0])
    value = residual[0]
    payload[0:1, :] = cosine * jnp.cos(azimuth[0]) * value
    payload[1:2, :] = cosine * jnp.sin(azimuth[0]) * value
    payload[2:3, :] = jnp.sin(elevation[0]) * value
    payload[3:4, :] = brick[...].astype(F32)
    payload[4:5, :] = cell[0].astype(F32)
    points = px.shape[1]
    payload[5:8, :] = jnp.zeros((3, payload.shape[1]), F32)
    for c in range(3):
        payload[5:6, c * points : (c + 1) * points] = force[c]
    payload[5:6, 3 * points : 4 * points] = px[...]
    payload[6:7, 0:points] = py[...]
    payload[6:7, points : 2 * points] = pz[...]
    size_y = kappa.shape[1]
    to_upper[:, 0:HALO] = kappa[:, size_y - HALO :]
    to_upper[:, HALO:] = sigma[:, size_y - HALO :]
    to_lower[:, 0:HALO] = kappa[:, 0:HALO]
    to_lower[:, HALO:] = sigma[:, 0:HALO]


def lines_of(payload, spans, start_x, size_y, size_z):
    brick = payload[3:4, :].astype(jnp.int32)
    cell = payload[4:5, :].astype(jnp.int32)
    away = brick - lax.axis_index("span")
    away = jnp.where(away < 0, away + spans, away)
    x = cell // (size_y * size_z)
    y = cell // size_z % size_y
    upper = (away == 1) & (y < HALO)
    lower = (away == spans - 1) & (y >= size_y - HALO)
    row = jnp.where(away == 0, y, jnp.where(upper, y + size_y, jnp.where(lower, y + 2 * HALO, -1)))
    return jnp.where(row < 0, -1, (x - start_x) * (size_y + 2 * HALO) + row), cell % size_z


def spread(payload_of, spans, sources, near, out, start_x, planes, size_y, size_z, first, unroll=False):
    ext_y = size_y + 2 * HALO
    height = planes * ext_y
    points = payload_of(0).shape[1] // 4
    count = len(near) * points
    rows = [[payload_of(j)[r : r + 1, :] for r in (5, 6)] for j, _ in near]

    def joined(r, k):
        return jnp.concatenate([pair[r][:, k * points : (k + 1) * points] for pair in rows], axis=1)

    px, pz = joined(0, 3), joined(1, 1)
    py = jnp.concatenate(
        [pair[1][:, 0:points] + F32(side * size_y) for pair, (_, side) in zip(rows, near)], axis=1
    )
    y_row = lax.broadcasted_iota(jnp.int32, (ext_y, count), 0)
    by = bump(jnp.where(y_row < size_y + HALO, y_row, y_row - ext_y).astype(F32) - py)
    x_cell = (lax.broadcasted_iota(jnp.int32, (planes, count), 0) + start_x).astype(F32)
    bx = bump(x_cell - px)
    z_cell = lax.broadcasted_iota(jnp.int32, (size_z, count), 0) + lax.axis_index("vert") * size_z
    bz_high, bz_low = two_parts(bump(z_cell.astype(F32) - pz))
    cross = jnp.concatenate([by * bx[x : x + 1] for x in range(planes)], axis=0)
    parts = [two_parts(cross * joined(0, c)) for c in range(3)]
    by_high = dot_lanes(jnp.concatenate([part for pair in parts for part in pair], axis=0), bz_high)
    by_low = dot_lanes(jnp.concatenate([high for high, _ in parts], axis=0), bz_low)
    for c in range(3):
        high = 2 * c * height
        both = by_high[high : high + height] + by_high[high + height : high + 2 * height]
        both += by_low[c * height : (c + 1) * height]
        out[c] = both if first is None else first[c] + both

    gates = payload_of(0).shape[1]
    row_id = lax.broadcasted_iota(jnp.int32, (height, gates), 0)
    z_id = lax.broadcasted_iota(jnp.int32, (size_z, gates), 0)

    def one_source(j, carry):
        one = payload_of(j)
        line, z = lines_of(one, spans, start_x, size_y, size_z)
        pick = jnp.where(row_id == line, 1.0, 0.0).astype(BF16)
        pick_z = jnp.where(z_id == z, 1.0, 0.0).astype(BF16)
        parts = [part for c in range(3) for part in two_parts(one[c : c + 1, :])]
        sums = dot_lanes(jnp.concatenate([pick * part for part in parts], axis=0), pick_z)
        for c in range(3):
            high = 2 * c * height
            out[c] += sums[high : high + height] + sums[high + height : high + 2 * height]
        return carry

    if unroll:
        for j in range(*sources):
            one_source(j, 0)
    else:
        lax.fori_loop(*sources, one_source, 0)


def near_of(spans):
    return ((0, 0), (1, -1), (2, 1)) if spans == 4 else ((0, 0), (spans - 1, -1), (1, 1))


def first_kernel(spans, dims, payload, out):
    size_x, size_y, size_z = dims
    spread(lambda j: payload, spans, (0, 1), near_of(spans)[:1], out, 0, size_x, size_y, size_z, None, unroll=True)


def second_kernel(spans, dims, count, *refs):
    payloads, (first, out) = refs[:count], refs[count:]
    size_x, size_y, size_z = dims
    near = near_of(spans)[1:]
    pick = (lambda j: payloads[j]) if count > 1 else (lambda j: payloads[0].at[j])
    spread(pick, spans, (1, spans), near, out, 0, size_x, size_y, size_z, first, unroll=count > 1)


def bands_kernel(sides, count, *refs):
    payloads = refs[:count]
    kappa, sigma, upper, lower = refs[count : count + 4]
    outs = refs[count + 4 : count + 4 + sides]
    size_x, size_y, size_z = kappa.shape
    ext_y = size_y + 2 * HALO
    if sides == 1:
        starts = [jnp.where(lax.axis_index("stream") == 0, size_x - HALO, 0)]
    else:
        starts = [size_x - HALO, 0]
    for out, start in zip(outs, starts):
        places = [(payload, None) for payload in payloads] if count > 1 else [(payloads[0], j) for j in range(payloads[0].shape[0])]
        for j, (payload, k) in enumerate(places):
            one = payload[...] if k is None else payload[k]
            for part in range(one.shape[1] // size_z):
                out[j * one.shape[1] // size_z + part] = one[:, part * size_z : (part + 1) * size_z]
        base = out.shape[0] - HALO * 2 * ext_y // 8
        for i in range(HALO):
            rows = [kappa[start + i], upper[start + i, 0:HALO], lower[start + i, 0:HALO]]
            rows += [sigma[start + i], upper[start + i, HALO:], lower[start + i, HALO:]]
            rows = jnp.concatenate(rows, axis=0)
            for part in range(2 * ext_y // 8):
                out[base + i * (2 * ext_y // 8) + part] = rows[8 * part : 8 * part + 8]


def extend_kernel(spans, sides, *refs):
    others = refs[:sides]
    behind = refs[sides : sides + 5]
    source, kappa_ext, face = refs[sides + 5 : sides + 8]
    strips = refs[sides + 8 : 2 * sides + 8]
    held = refs[2 * sides + 8 : -1]
    copies = [pltpu.make_async_copy(a, b, refs[-1].at[i]) for i, (a, b) in enumerate(zip(behind, held))]
    for copy in copies:
        copy.start()
    own, kappa, sigma, upper, lower = held
    size_x, size_y, size_z = kappa.shape
    ext_y = size_y + 2 * HALO
    parts = others[0].shape[0] - HALO * 2 * ext_y // 8
    if sides == 1:
        starts = [jnp.where(lax.axis_index("stream") == 0, 0, size_x - HALO)]
    else:
        starts = [0, size_x - HALO]
    for packed, strip, start in zip(others, strips, starts):

        def payload_of(j, packed=packed):
            each = parts // spans
            return jnp.concatenate([packed[j * each + part] for part in range(each)], axis=1)

        spread(payload_of, spans, (0, spans), near_of(spans), strip, start, HALO, size_y, size_z, None)
    for copy in copies:
        copy.wait()
    vert = lax.axis_index("vert")
    side = pl.ds(pl.multiple_of(jnp.where(vert == 0, size_z - 128, 0), 128), 128)
    for x in range(size_x + sides * HALO):
        if x < size_x:
            kappa_ext[x] = jnp.concatenate([kappa[x], upper[x, 0:HALO], lower[x, 0:HALO]], axis=0)
            sig = jnp.concatenate([sigma[x], upper[x, HALO:], lower[x, HALO:]], axis=0)
        else:
            packed = others[(x - size_x) // HALO]
            tiles = ext_y // 8
            base = parts + (x - size_x) % HALO * 2 * tiles
            kappa_ext[x] = jnp.concatenate([packed[base + k] for k in range(tiles)], axis=0)
            sig = jnp.concatenate([packed[base + tiles + k] for k in range(tiles)], axis=0)
        for c in range(3):
            if x < size_x:
                value = own[c, x * ext_y : (x + 1) * ext_y, :]
            else:
                place = (x - size_x) % HALO * ext_y
                value = strips[(x - size_x) // HALO][c, place : place + ext_y, :]
            source[c, x] = value * sig
    lane = lax.broadcasted_iota(jnp.int32, (8, 128), 1)
    tiles = face_tiles(size_x + sides * HALO, ext_y)
    for g in range(0, len(tiles), 16):
        packed = jnp.zeros((8, 128), F32)
        for k, (c, x, y) in enumerate(tiles[g : g + 16]):
            tile = kappa_ext[x, y : y + 8, side] if c == 3 else source[c, x, y : y + 8, side]
            turned = pltpu.roll(tile, (8 * k + 8 * (1 - vert)) & 127, 1)
            packed = jnp.where(lane // 8 == k, turned, packed)
        face[g // 16] = packed


def face_tiles(planes, ext_y):
    return [(c, x, y) for c in range(4) for x in range(planes) for y in range(0, ext_y, 8)]


def lanes_on(values, step, lane):
    tiles = [values[:, k : k + 128] for k in range(0, values.shape[1], 128)]
    turned = [pltpu.roll(tile, step % 128, 1) for tile in tiles]
    edge = lane == (0 if step == 1 else 127)
    return jnp.concatenate(
        [jnp.where(edge, turned[(k - step) % len(tiles)], turned[k]) for k in range(len(tiles))], axis=1
    )


def each_plane(count, step, unroll=4):
    whole = count // unroll * unroll
    lax.fori_loop(0, whole, lambda i, carry: (step(i), carry)[1], 0, unroll=unroll)
    for i in range(whole, count):
        step(i)


def diffuse_kernel(sides, source, kappa_ext, face, out, ping, pong, root, ax, ay, aym, az, azm, keep):
    planes, ext_y, size_z = kappa_ext.shape
    size_x, size_y = out.shape[1], out.shape[2]
    ext_z = size_z + 128
    stream, vert = lax.axis_index("stream"), lax.axis_index("vert")

    def fill(x):
        for c in range(3):
            ping[c, x, :, 0:size_z] = source[c, x]
        root[x, :, 0:size_z] = jnp.sqrt(kappa_ext[x])

    each_plane(planes, fill)
    lane = lax.broadcasted_iota(jnp.int32, (ext_y, 128), 1)
    known = lax.broadcasted_iota(jnp.int32, (8, 128), 1) // 8 == vert * 15
    for t, (c, x, y) in enumerate(face_tiles(planes, ext_y)):
        turned = pltpu.roll(face[t // 16], (256 - 8 * (t % 16) - 8 * vert) & 127, 1)
        if c == 3:
            root[x, y : y + 8, size_z:] = jnp.sqrt(jnp.where(known, turned, 0.0))
        else:
            ping[c, x, y : y + 8, size_z:] = turned
    last = lax.axis_size("stream") - 1

    def faces(x):
        after = jnp.where(x == planes - 1, 0, x + 1)
        here = root[x]
        wall = ((x == planes - 1) & (stream == 0)) | ((x == size_x - 1) & (stream == last))
        ax[x] = here * root[after] * jnp.where(wall, 0.0, 1.0)
        up = here * pltpu.roll(here, ext_y - 1, 0)
        ay[x] = up
        aym[x] = pltpu.roll(up, 1, 0)
        up = here * lanes_on(here, -1, lane)
        az[x] = up
        azm[x] = lanes_on(up, 1, lane)

    each_plane(planes, faces)

    def total(x):
        before = jnp.where(x == 0, planes - 1, x - 1)
        keep[x] = 1.0 - (ax[x] + ax[before] + ay[x] + aym[x] + az[x] + azm[x])

    each_plane(planes, total)

    for p in range(PASSES):
        deep = PASSES - 1 - p
        old, new = (ping, pong) if p % 2 == 0 else (pong, ping)
        first = jnp.where(stream == 0, 0, planes - deep) if sides == 1 else planes - deep

        def one_plane(i, old=old, new=new, first=first, p=p):
            x = i + first
            x = jnp.where(x >= planes, x - planes, x)
            after = jnp.where(x == planes - 1, 0, x + 1)
            before = jnp.where(x == 0, planes - 1, x - 1)
            for c in range(3):
                value = old[c, x]
                moved = keep[x] * value
                moved += ax[x] * old[c, after] + ax[before] * old[c, before]
                moved += ay[x] * pltpu.roll(value, ext_y - 1, 0) + aym[x] * pltpu.roll(value, 1, 0)
                moved += az[x] * lanes_on(value, -1, lane) + azm[x] * lanes_on(value, 1, lane)
                if p == PASSES - 1:
                    out[c, x] = moved[0:size_y, 0:size_z]
                else:
                    new[c, x] = moved

        each_plane(size_x + sides * deep, one_plane)


def call(kernel, outs, scratch, flops, *args, left=(), aliases=()):
    moved = sum(4 * a.size for a in args) + sum(4 * o.size for o in outs)
    spaces = [pl.ANY if i in left else pltpu.VMEM for i in range(len(args))]
    return pl.pallas_call(
        kernel,
        out_shape=outs,
        in_specs=[pl.BlockSpec(memory_space=space) for space in spaces],
        out_specs=[pl.BlockSpec(memory_space=pltpu.VMEM)] * len(outs),
        scratch_shapes=scratch,
        input_output_aliases=dict(aliases),
        compiler_params=pltpu.CompilerParams(vmem_limit_bytes=56 * 1024 * 1024),
        cost_estimate=pl.CostEstimate(flops=flops, bytes_accessed=moved, transcendentals=0),
    )(*args)


def ring(array, step):
    count = lax.axis_size("span")
    return lax.ppermute(array, "span", [(i, (i + step) % count) for i in range(count)])


def across_bands(arrays):
    count = lax.axis_size("stream")
    if count == 2:
        return [lax.ppermute(arrays[0], "stream", [(0, 1), (1, 0)])]
    return [
        lax.ppermute(arrays[1], "stream", [(i + 1, i) for i in range(count - 1)]),
        lax.ppermute(arrays[0], "stream", [(i, i + 1) for i in range(count - 1)]),
    ]


def on_device(
    kappa,
    sigma,
    gate_residual,
    gate_azimuth,
    gate_elevation,
    gate_brick,
    gate_cell,
    blade_force,
    point_x,
    point_y,
    point_z,
):
    size_x, size_y, size_z = kappa.shape
    spans = lax.axis_size("span")
    sides = 1 if lax.axis_size("stream") == 2 else 2
    gates = gate_residual.shape[2]
    ext_x, ext_y = size_x + sides * HALO, size_y + 2 * HALO
    shape = lambda *dims: jax.ShapeDtypeStruct(dims, F32)
    payload, to_upper, to_lower = call(
        pack_kernel,
        [shape(8, gates)] + [shape(size_x, 2 * HALO, size_z)] * 2,
        [],
        1000,
        gate_residual,
        gate_azimuth,
        gate_elevation,
        gate_brick.reshape(1, gates),
        gate_cell,
        blade_force,
        point_x,
        point_y,
        point_z,
        kappa,
        sigma,
    )
    if spans == 4:
        payloads = [payload, ring(payload, 1), ring(payload, -1), ring(payload, 2)]
    else:
        payloads = [jnp.roll(lax.all_gather(payload, "span"), -lax.axis_index("span"), axis=0)]
    from_lower, from_upper = ring(to_upper, 1), ring(to_lower, -1)
    dims = (size_x, size_y, size_z)
    work = 12 * size_x * ext_y * size_z * gates
    planes = shape(3, size_x * ext_y, size_z)
    (own,) = call(functools.partial(first_kernel, spans, dims), [planes], [], work, payload)
    parts = spans * gates // size_z + HALO * 2 * ext_y // 8
    others = across_bands(
        call(
            functools.partial(bands_kernel, sides, len(payloads)),
            [shape(parts, 8, size_z)] * sides,
            [],
            1000,
            *payloads,
            kappa,
            sigma,
            from_upper,
            from_lower,
        )
    )
    (own,) = call(
        functools.partial(second_kernel, spans, dims, len(payloads)),
        [planes],
        [],
        work * (spans - 1),
        *payloads,
        own,
        aliases=((len(payloads), 0),),
    )
    behind = [own, kappa, sigma, from_upper, from_lower]
    tiles = len(face_tiles(ext_x, ext_y))
    source, kappa_ext, face = call(
        functools.partial(extend_kernel, spans, sides),
        [shape(3, ext_x, ext_y, size_z), shape(ext_x, ext_y, size_z), shape(-(-tiles // 16), 8, 128)],
        [pltpu.VMEM((3, HALO * ext_y, size_z), F32)] * sides
        + [pltpu.VMEM(a.shape, F32) for a in behind]
        + [pltpu.SemaphoreType.DMA((len(behind),))],
        work // 4 * spans,
        *others,
        *behind,
        left=range(sides, sides + len(behind)),
    )
    face = lax.ppermute(face, "vert", [(0, 1), (1, 0)])
    wide = (ext_x, ext_y, size_z + 128)
    (field,) = call(
        functools.partial(diffuse_kernel, sides),
        [shape(3, size_x, size_y, size_z)],
        [pltpu.VMEM((3, *wide), F32)] * 2 + [pltpu.VMEM(wide, F32)] * 7,
        60 * 3 * ext_x * ext_y * size_z,
        source,
        kappa_ext,
        face,
    )
    return field


def solution(mesh):
    placed = (
        P(("grp", "stream"), "span", "vert"),
        P(("grp", "stream"), "span", "vert"),
        P(("grp", "stream"), "vert", "span"),
        P(("grp", "stream"), "vert", "span"),
        P(("grp", "stream"), "vert", "span"),
        P(("grp", "stream"), "vert", "span", None),
        P(("grp", "stream"), "vert", "span"),
        P(None, ("grp", "stream"), "span"),
        P(("grp", "stream"), "span"),
        P(("grp", "stream"), "span"),
        P(("grp", "stream"), "span"),
    )
    return jax.shard_map(
        on_device,
        mesh=mesh,
        in_specs=placed,
        out_specs=P(None, ("grp", "stream"), "span", "vert"),
        check_vma=False,
    )
```

time: 61.5 us -> 48.6 us (0.79)
  Pallas kernels: 39.5 us -> 31.6 us
  waiting for transfers between devices: 8.02 us -> 3.03 us
  local copies, waits for them, and re-layouts: 3.56 us -> 2.63 us
  starting transfers between devices: 10.1 us -> 11 us
    pallas_call x5 -> x6, Pallas kernels: 39.5 us -> 31.6 us  [call(): pl.pallas_call(kernel, out_shape=outs, in_specs=[pl.BlockSpec(memory_spac...]
    ppermute x5, waiting for transfers between devices: 5.25 us -> 1.58 us  [ring(): lax.ppermute(array, 'span', [(i, (i + step) % count) for i in range(count)])]
    ppermute x5, starting transfers between devices: 6.64 us -> 9.44 us  [ring(): lax.ppermute(array, 'span', [(i, (i + step) % count) for i in range(count)])]
    ppermute x2 -> x1, starting transfers between devices: 3.47 us -> 1.49 us  [across_bands(): return [lax.ppermute(arrays[0], 'stream', [(0, 1), (1, 0)])]]
    ppermute x1, waiting for transfers between devices: 2.77 us -> 1.45 us  [on_device(): face = lax.ppermute(face, 'vert', [(0, 1), (1, 0)])]
    unnamed x16 -> x14, local copies, waits for them, and re-layouts: 3.56 us -> 2.63 us
  transfers between devices with their start and end apart: 8 -> 7, of which waited for: 4 -> 3; matrix products, arithmetic and copies ran while one was open for 0% -> 0% of each run, Pallas kernels for 17% -> 23%
where the time goes in v2:
time: 48.6 us; the launch traced here: 48.3 us
  Pallas kernels  31.6 us (65%)
  starting transfers between devices  11 us (23%)
  waiting for transfers between devices  3.03 us (6%)
  local copies, waits for them, and re-layouts  2.63 us (5%)
    pallas_call x6, Pallas kernels, call(): pl.pallas_call(kernel, out_shape=outs, in_specs=[pl.BlockSpec(memory_spac...  31.6 us
    ppermute x5, starting transfers between devices, ring(): lax.ppermute(array, 'span', [(i, (i + step) % count) for i in range(count)])  9.44 us
    unnamed x14, local copies, waits for them, and re-layouts  2.63 us
    ppermute x5, waiting for transfers between devices, ring(): lax.ppermute(array, 'span', [(i, (i + step) % count) for i in range(count)])  1.58 us
    ppermute x1, starting transfers between devices, across_bands(): return [lax.ppermute(arrays[0], 'stream', [(0, 1), (1, 0)])]  1.49 us
    ppermute x1, waiting for transfers between devices, on_device(): face = lax.ppermute(face, 'vert', [(0, 1), (1, 0)])  1.45 us
  transfers between devices with their start and end apart: 7, of which 3 were waited for; matrix products, arithmetic and copies ran while one was open for 0% of the time, Pallas kernels for 23%

profile of v2, /device:TPU:0, one launch (start us, length us, event | category | flops | bytes accessed | tf_op | source)
XLA Modules:
  0.0 48.3 jit_solution(11826694521364496741)
XLA Ops:
  0.0 1.9 %shard_map.109 = (f32[8,1024]{1,0:T(8,128)}, f32[16,8,256]{2,1,0:T(8,128)}, f32[16,8,256]{2,1,0:T(8,128)}) custom-call(f32[1,1,1024]{2,1,0:T(1,128)} %residual.1, f32[1,1,1024]{2,1,0:T(1,128)} %azimuth.1, f32[1,1,1024]{2,1,0:T(1,128)} %elevation.1, s32[1,1024]{1,0:T(1,128)} %bitcast.1, s32[1,1,1024]{2,1,0:T(1,128)} %cell.1, f32[3,1,256]{2,1,0:T(1,128)} %force.1, ...), custom_call_target="tpu_custom_call" | custom-call | flops 1000 | bytes 845824 | tf_op jit(solution)/shard_map/pallas_call | solution.py:307
  1.9 5.0 %collective-permute-start.3 = (f32[16,8,256]{2,1,0:T(8,128)}, f32[16,8,256]{2,1,0:T(8,128)S(1)}, u32[]{:S(2)}, u32[]{:S(2)}) collective-permute-start(f32[16,8,256]{2,1,0:T(8,128)} %get-tuple-element.12), channel_id=1, source_target_pairs={{0,12},{4,0},{8,4},{12,8},{1,13},{5,1},{9,5},{13,9},{2,14},{6,2},{... | collective-permute-start | bytes 393224 | tf_op jit(solution)/shard_map/ppermute | solution.py:321
  7.0 0.0 collective-permute-start.4
  7.0 1.0 %collective-permute-start.2 = (f32[8,1024]{1,0:T(8,128)}, f32[8,1024]{1,0:T(8,128)S(1)}, u32[]{:S(2)}, u32[]{:S(2)}) collective-permute-start(f32[8,1024]{1,0:T(8,128)} %get-tuple-element.11.refs_0_.payload), channel_id=1, source_target_pairs={{0,8},{4,12},{8,0},{12,4},{1,9},{5,13},{9,1},{13,5},{2,10},{6,14},... | collective-permute-start | bytes 98312 | tf_op jit(solution)/shard_map/ppermute | solution.py:321
  8.0 2.8 %collective-permute-start.1 = (f32[8,1024]{1,0:T(8,128)}, f32[8,1024]{1,0:T(8,128)S(1)}, u32[]{:S(2)}, u32[]{:S(2)}) collective-permute-start(f32[8,1024]{1,0:T(8,128)} %get-tuple-element.11.refs_0_.payload), channel_id=1, source_target_pairs={{0,12},{4,0},{8,4},{12,8},{1,13},{5,1},{9,5},{13,9},{2,14},{6,2},{... | collective-permute-start | bytes 98312 | tf_op jit(solution)/shard_map/ppermute | solution.py:321
  10.8 0.6 %collective-permute-start = (f32[8,1024]{1,0:T(8,128)}, f32[8,1024]{1,0:T(8,128)S(1)}, u32[]{:S(2)}, u32[]{:S(2)}) collective-permute-start(f32[8,1024]{1,0:T(8,128)} %get-tuple-element.11.refs_0_.payload), channel_id=1, source_target_pairs={{0,4},{4,8},{8,12},{12,0},{1,5},{5,9},{9,13},{13,1},{2,6},{6,10},{... | collective-permute-start | bytes 98312 | tf_op jit(solution)/shard_map/ppermute | solution.py:321
  11.4 3.8 %shard_map.111.refs_4_ = f32[3,384,256]{2,1,0:T(8,128)} custom-call(f32[8,1024]{1,0:T(8,128)} %get-tuple-element.11.refs_0_.payload), custom_call_target="tpu_custom_call" | custom-call | flops 1207959552 | bytes 1212416 | tf_op jit(solution)/shard_map/pallas_call | solution.py:307
  15.1 0.5 collective-permute-done.2.refs_3_
  15.6 0.0 copy-start.3
  15.6 0.0 collective-permute-done.1.refs_2_
  15.6 0.0 copy-start.4
  15.6 1.1 %collective-permute-done.refs_1_ = f32[8,1024]{1,0:T(8,128)S(1)} collective-permute-done((f32[8,1024]{1,0:T(8,128)}, f32[8,1024]{1,0:T(8,128)S(1)}, u32[]{:S(2)}, u32[]{:S(2)}) %collective-permute-start) | collective-permute-done | bytes 32800 | tf_op jit(solution)/shard_map/ppermute | solution.py:321
  16.7 0.0 copy-start.5
  16.7 0.0 collective-permute-done.3.refs_6_.refs_4_
  16.7 0.0 copy-start
  16.7 0.0 collective-permute-done.4.refs_7_.refs_5_
  16.7 0.0 copy-done.3
  16.7 0.0 copy-done.4
  16.7 0.6 %copy-done.5 = f32[8,1024]{1,0:T(8,128)} copy-done((f32[8,1024]{1,0:T(8,128)}, f32[8,1024]{1,0:T(8,128)S(1)}, u32[]{:S(2)}) %copy-start.5) | copy-done | bytes 32792
  17.3 0.1 copy-done
  17.4 0.0 copy-start.1
  17.4 0.6 %copy-done.1 = f32[16,8,256]{2,1,0:T(8,128)} copy-done((f32[16,8,256]{2,1,0:T(8,128)}, f32[16,8,256]{2,1,0:T(8,128)S(1)}, u32[]{:S(2)}) %copy-start.1) | copy-done | bytes 131096
  18.0 1.9 %shard_map.110 = f32[40,8,256]{2,1,0:T(8,128)} custom-call(f32[8,1024]{1,0:T(8,128)} %get-tuple-element.11.refs_0_.payload, f32[8,1024]{1,0:T(8,128)} %copy-done.5, f32[8,1024]{1,0:T(8,128)} %copy-done.4, f32[8,1024]{1,0:T(8,128)} %copy-done.3, f32[16,16,256]{2,1,0:T(8,128)} %refs_2_.1, f32[16,16,256]{2,1,0:T(8,128)} %refs_3_.1, f32[16,8,256]{2,1,0:T(8,128)} %copy-done, ...), custom_call_target="tpu_custom_call" | custom-call | flops 1000 | bytes 1245184 | tf_op jit(solution)/shard_map/pallas_call | solution.py:307
  19.9 1.5 %collective-permute-start.5 = (f32[40,8,256]{2,1,0:T(8,128)}, f32[40,8,256]{2,1,0:T(8,128)S(1)}, u32[]{:S(2)}, u32[]{:S(2)}) collective-permute-start(f32[40,8,256]{2,1,0:T(8,128)} %shard_map.110), channel_id=1, source_target_pairs={{0,2},{2,0},{1,3},{3,1},{4,6},{6,4},{5,7},{7,5},{8,10},{10,8},{9,1... | collective-permute-start | bytes 983048 | tf_op jit(solution)/shard_map/ppermute | solution.py:327
  21.4 7.4 %shard_map.112.refs_1_ = f32[3,384,256]{2,1,0:T(8,128)} custom-call(f32[8,1024]{1,0:T(8,128)} %get-tuple-element.11.refs_0_.payload, f32[8,1024]{1,0:T(8,128)} %copy-done.5, f32[8,1024]{1,0:T(8,128)} %copy-done.4, f32[8,1024]{1,0:T(8,128)} %copy-done.3, f32[3,384,256]{2,1,0:T(8,128)} %shard_map.111.refs_4_), custom_call_target="tpu_custom_call", output_to_operand_aliasing={{}: (4, {})} | custom-call | flops 3623878656 | bytes 2490368 | tf_op jit(solution)/shard_map/pallas_call | solution.py:307
  28.8 0.0 collective-permute-done.5.refs_0_
  28.8 0.7 %copy-done.6 = f32[40,8,256]{2,1,0:T(8,128)} copy-done((f32[40,8,256]{2,1,0:T(8,128)}, f32[40,8,256]{2,1,0:T(8,128)S(1)}, u32[]{:S(2)}) %copy-start.6) | copy-done | bytes 327704
  29.6 5.6 %shard_map.113 = (f32[3,20,24,256]{3,2,1,0:T(8,128)}, f32[20,24,256]{2,1,0:T(8,128)}, f32[15,8,128]{2,1,0:T(8,128)}) custom-call(f32[40,8,256]{2,1,0:T(8,128)} %copy-done.6, f32[3,384,256]{2,1,0:T(8,128)} %shard_map.112.refs_1_, f32[16,16,256]{2,1,0:T(8,128)} %refs_2_.1, f32[16,16,256]{2,1,0:T(8,128)} %refs_3_.1, f32[16,8,256]{2,1,0:T(8,128)} %copy-done, ...), custom_call_target="tpu_custom_call" | custom-call | flops 1207959552 | bytes 4321280 | tf_op jit(solution)/shard_map/pallas_call | solution.py:307
  35.2 0.1 collective-permute-start.6
  35.3 1.4 %collective-permute-done.6.face = f32[15,8,128]{2,1,0:T(8,128)S(1)} collective-permute-done((f32[15,8,128]{2,1,0:T(8,128)}, f32[15,8,128]{2,1,0:T(8,128)S(1)}, u32[]{:S(2)}, u32[]{:S(2)}) %collective-permute-start.6) | collective-permute-done | bytes 61472 | tf_op jit(solution)/shard_map/ppermute | solution.py:415
  36.7 0.6 %copy-done.2 = f32[15,8,128]{2,1,0:T(8,128)} copy-done((f32[15,8,128]{2,1,0:T(8,128)}, f32[15,8,128]{2,1,0:T(8,128)S(1)}, u32[]{:S(2)}) %copy-start.2) | copy-done | bytes 61464
  37.3 11.0 %shard_map.114 = f32[3,16,16,256]{3,2,1,0:T(8,128)} custom-call(f32[3,20,24,256]{3,2,1,0:T(8,128)} %get-tuple-element.14.source, f32[20,24,256]{2,1,0:T(8,128)} %get-tuple-element.15.kappa_ext, f32[15,8,128]{2,1,0:T(8,128)} %copy-done.2), custom_call_target="tpu_custom_call" | custom-call | flops 22118400 | bytes 2813952 | tf_op jit(solution)/shard_map/pallas_call | solution.py:307
  (2 shorter events, 0.0 us)
Async XLA Ops:
  1.9 14.8 %collective-permute-start.3 = (f32[16,8,256]{2,1,0:T(8,128)}, f32[16,8,256]{2,1,0:T(8,128)S(1)}, u32[]{:S(2)}, u32[]{:S(2)}) collective-permute-start(f32[16,8,256]{2,1,0:T(8,128)} %get-tuple-element.12), channel_id=1, source_target_pairs={{0,12},{4,0},{8,4},{12,8},{1,13},{5,1},{9,5},{13,9},{2,14},{6,2},{... | collective-permute-start | bytes 393224 | tf_op jit(solution)/shard_map/ppermute | solution.py:321
  7.0 9.8 %collective-permute-start.4 = (f32[16,8,256]{2,1,0:T(8,128)}, f32[16,8,256]{2,1,0:T(8,128)S(1)}, u32[]{:S(2)}, u32[]{:S(2)}) collective-permute-start(f32[16,8,256]{2,1,0:T(8,128)} %get-tuple-element.13), channel_id=1, source_target_pairs={{0,4},{4,8},{8,12},{12,0},{1,5},{5,9},{9,13},{13,1},{2,6},{6,10},{... | collective-permute-start | bytes 393224 | tf_op jit(solution)/shard_map/ppermute | solution.py:321
  7.0 8.6 %collective-permute-start.2 = (f32[8,1024]{1,0:T(8,128)}, f32[8,1024]{1,0:T(8,128)S(1)}, u32[]{:S(2)}, u32[]{:S(2)}) collective-permute-start(f32[8,1024]{1,0:T(8,128)} %get-tuple-element.11.refs_0_.payload), channel_id=1, source_target_pairs={{0,8},{4,12},{8,0},{12,4},{1,9},{5,13},{9,1},{13,5},{2,10},{6,14},... | collective-permute-start | bytes 98312 | tf_op jit(solution)/shard_map/ppermute | solution.py:321
  8.0 7.6 %collective-permute-start.1 = (f32[8,1024]{1,0:T(8,128)}, f32[8,1024]{1,0:T(8,128)S(1)}, u32[]{:S(2)}, u32[]{:S(2)}) collective-permute-start(f32[8,1024]{1,0:T(8,128)} %get-tuple-element.11.refs_0_.payload), channel_id=1, source_target_pairs={{0,12},{4,0},{8,4},{12,8},{1,13},{5,1},{9,5},{13,9},{2,14},{6,2},{... | collective-permute-start | bytes 98312 | tf_op jit(solution)/shard_map/ppermute | solution.py:321
  10.8 5.9 %collective-permute-start = (f32[8,1024]{1,0:T(8,128)}, f32[8,1024]{1,0:T(8,128)S(1)}, u32[]{:S(2)}, u32[]{:S(2)}) collective-permute-start(f32[8,1024]{1,0:T(8,128)} %get-tuple-element.11.refs_0_.payload), channel_id=1, source_target_pairs={{0,4},{4,8},{8,12},{12,0},{1,5},{5,9},{9,13},{13,1},{2,6},{6,10},{... | collective-permute-start | bytes 98312 | tf_op jit(solution)/shard_map/ppermute | solution.py:321
  15.6 1.1 %copy-start.3 = (f32[8,1024]{1,0:T(8,128)}, f32[8,1024]{1,0:T(8,128)S(1)}, u32[]{:S(2)}) copy-start(f32[8,1024]{1,0:T(8,128)S(1)} %collective-permute-done.2.refs_3_) | copy-start | bytes 98308
  15.6 1.1 %copy-start.4 = (f32[8,1024]{1,0:T(8,128)}, f32[8,1024]{1,0:T(8,128)S(1)}, u32[]{:S(2)}) copy-start(f32[8,1024]{1,0:T(8,128)S(1)} %collective-permute-done.1.refs_2_) | copy-start | bytes 98308
  16.7 0.6 %copy-start.5 = (f32[8,1024]{1,0:T(8,128)}, f32[8,1024]{1,0:T(8,128)S(1)}, u32[]{:S(2)}) copy-start(f32[8,1024]{1,0:T(8,128)S(1)} %collective-permute-done.refs_1_) | copy-start | bytes 98308
  16.7 0.7 %copy-start = (f32[16,8,256]{2,1,0:T(8,128)}, f32[16,8,256]{2,1,0:T(8,128)S(1)}, u32[]{:S(2)}) copy-start(f32[16,8,256]{2,1,0:T(8,128)S(1)} %collective-permute-done.3.refs_6_.refs_4_) | copy-start | bytes 393220
  17.4 0.6 %copy-start.1 = (f32[16,8,256]{2,1,0:T(8,128)}, f32[16,8,256]{2,1,0:T(8,128)S(1)}, u32[]{:S(2)}) copy-start(f32[16,8,256]{2,1,0:T(8,128)S(1)} %collective-permute-done.4.refs_7_.refs_5_) | copy-start | bytes 393220
  19.9 8.9 %collective-permute-start.5 = (f32[40,8,256]{2,1,0:T(8,128)}, f32[40,8,256]{2,1,0:T(8,128)S(1)}, u32[]{:S(2)}, u32[]{:S(2)}) collective-permute-start(f32[40,8,256]{2,1,0:T(8,128)} %shard_map.110), channel_id=1, source_target_pairs={{0,2},{2,0},{1,3},{3,1},{4,6},{6,4},{5,7},{7,5},{8,10},{10,8},{9,1... | collective-permute-start | bytes 983048 | tf_op jit(solution)/shard_map/ppermute | solution.py:327
  28.8 0.7 %copy-start.6 = (f32[40,8,256]{2,1,0:T(8,128)}, f32[40,8,256]{2,1,0:T(8,128)S(1)}, u32[]{:S(2)}) copy-start(f32[40,8,256]{2,1,0:T(8,128)S(1)} %collective-permute-done.5.refs_0_) | copy-start | bytes 983044
  35.2 1.5 %collective-permute-start.6 = (f32[15,8,128]{2,1,0:T(8,128)}, f32[15,8,128]{2,1,0:T(8,128)S(1)}, u32[]{:S(2)}, u32[]{:S(2)}) collective-permute-start(f32[15,8,128]{2,1,0:T(8,128)} %get-tuple-element.16), channel_id=1, source_target_pairs={{0,1},{1,0},{2,3},{3,2},{4,5},{5,4},{6,7},{7,6},{8,9},{9,8},{10,11... | collective-permute-start | bytes 184328 | tf_op jit(solution)/shard_map/ppermute | solution.py:415
  36.7 0.6 %copy-start.2 = (f32[15,8,128]{2,1,0:T(8,128)}, f32[15,8,128]{2,1,0:T(8,128)S(1)}, u32[]{:S(2)}) copy-start(f32[15,8,128]{2,1,0:T(8,128)S(1)} %collective-permute-done.6.face) | copy-start | bytes 184324

commit v3 on v2

--- a/solution.py
+++ b/solution.py
@@ -29,26 +29,40 @@
     return lax.dot_general(left, right, CONTRACT_LANES, preferred_element_type=F32)
 
 
-def pack_kernel(residual, azimuth, elevation, brick, cell, force, px, py, pz, kappa, sigma, payload, to_upper, to_lower):
+def pack_kernel(sides, *refs):
+    residual, azimuth, elevation, brick, cell, force, px, py, pz, kappa, sigma = refs[:11]
+    payload, to_upper, to_lower = refs[11:14]
+    slabs = refs[14:]
     cosine = jnp.cos(elevation[0])
     value = residual[0]
-    payload[0:1, :] = cosine * jnp.cos(azimuth[0]) * value
-    payload[1:2, :] = cosine * jnp.sin(azimuth[0]) * value
-    payload[2:3, :] = jnp.sin(elevation[0]) * value
-    payload[3:4, :] = brick[...].astype(F32)
-    payload[4:5, :] = cell[0].astype(F32)
-    points = px.shape[1]
-    payload[5:8, :] = jnp.zeros((3, payload.shape[1]), F32)
-    for c in range(3):
-        payload[5:6, c * points : (c + 1) * points] = force[c]
-    payload[5:6, 3 * points : 4 * points] = px[...]
-    payload[6:7, 0:points] = py[...]
-    payload[6:7, points : 2 * points] = pz[...]
-    size_y = kappa.shape[1]
+    gates, points = value.shape[1], px.shape[1]
+    rest = jnp.zeros((1, gates - 2 * points), F32)
+    rows = [
+        cosine * jnp.cos(azimuth[0]) * value,
+        cosine * jnp.sin(azimuth[0]) * value,
+        jnp.sin(elevation[0]) * value,
+        brick[...].astype(F32),
+        cell[0].astype(F32),
+        jnp.concatenate([force[0], force[1], force[2], px[...]], axis=1),
+        jnp.concatenate([py[...], pz[...], rest], axis=1),
+        jnp.zeros((1, gates), F32),
+    ]
+    for r, row in enumerate(rows):
+        payload[r : r + 1, :] = row
+    size_x, size_y, size_z = kappa.shape
     to_upper[:, 0:HALO] = kappa[:, size_y - HALO :]
     to_upper[:, HALO:] = sigma[:, size_y - HALO :]
     to_lower[:, 0:HALO] = kappa[:, 0:HALO]
     to_lower[:, HALO:] = sigma[:, 0:HALO]
+    for slab, start in zip(slabs, edges(sides, size_x)):
+        slab[:, 0:size_y] = kappa[pl.ds(start, HALO)]
+        slab[:, size_y:] = sigma[pl.ds(start, HALO)]
+
+
+def edges(sides, size_x):
+    if sides == 1:
+        return [jnp.where(lax.axis_index("stream") == 0, size_x - HALO, 0)]
+    return [size_x - HALO, 0]
 
 
 def lines_of(payload, spans, start_x, size_y, size_z):
@@ -126,65 +140,42 @@
     spread(lambda j: payload, spans, (0, 1), near_of(spans)[:1], out, 0, size_x, size_y, size_z, None, unroll=True)
 
 
+def payload_in(refs, j):
+    return refs[0].at[j] if len(refs) == 1 else refs[j]
+
+
 def second_kernel(spans, dims, count, *refs):
     payloads, (first, out) = refs[:count], refs[count:]
     size_x, size_y, size_z = dims
     near = near_of(spans)[1:]
-    pick = (lambda j: payloads[j]) if count > 1 else (lambda j: payloads[0].at[j])
-    spread(pick, spans, (1, spans), near, out, 0, size_x, size_y, size_z, first, unroll=count > 1)
-
-
-def bands_kernel(sides, count, *refs):
-    payloads = refs[:count]
-    kappa, sigma, upper, lower = refs[count : count + 4]
-    outs = refs[count + 4 : count + 4 + sides]
+    spread(lambda j: payload_in(payloads, j), spans, (1, spans), near, out, 0, size_x, size_y, size_z, first, unroll=count > 1)
+
+
+def gather_kernel(count, *refs):
+    for j in range(count):
+        refs[count][j] = refs[j][...]
+
+
+def corner_kernel(sides, upper, lower, *outs):
+    for out, start in zip(outs, edges(sides, upper.shape[0])):
+        out[:, 0 : 2 * HALO] = upper[pl.ds(start, HALO)]
+        out[:, 2 * HALO :] = lower[pl.ds(start, HALO)]
+
+
+def strip_kernel(spans, sides, dims, *refs):
+    size_x, size_y, size_z = dims
+    starts = edges(sides, size_x)
+    starts = [size_x - HALO - starts[0]] if sides == 1 else starts[::-1]
+    for payloads, strip, start in zip(refs[:sides], refs[sides:], starts):
+        spread(lambda j: payloads.at[j], spans, (0, spans), near_of(spans), strip, start, HALO, size_y, size_z, None)
+
+
+def extend_kernel(sides, *refs):
+    own, kappa, sigma, upper, lower = refs[:5]
+    strips, slabs, corners = (refs[5 + k * sides : 5 + (k + 1) * sides] for k in range(3))
+    source, kappa_ext, face = refs[5 + 3 * sides :]
     size_x, size_y, size_z = kappa.shape
     ext_y = size_y + 2 * HALO
-    if sides == 1:
-        starts = [jnp.where(lax.axis_index("stream") == 0, size_x - HALO, 0)]
-    else:
-        starts = [size_x - HALO, 0]
-    for out, start in zip(outs, starts):
-        places = [(payload, None) for payload in payloads] if count > 1 else [(payloads[0], j) for j in range(payloads[0].shape[0])]
-        for j, (payload, k) in enumerate(places):
-            one = payload[...] if k is None else payload[k]
-            for part in range(one.shape[1] // size_z):
-                out[j * one.shape[1] // size_z + part] = one[:, part * size_z : (part + 1) * size_z]
-        base = out.shape[0] - HALO * 2 * ext_y // 8
-        for i in range(HALO):
-            rows = [kappa[start + i], upper[start + i, 0:HALO], lower[start + i, 0:HALO]]
-            rows += [sigma[start + i], upper[start + i, HALO:], lower[start + i, HALO:]]
-            rows = jnp.concatenate(rows, axis=0)
-            for part in range(2 * ext_y // 8):
-                out[base + i * (2 * ext_y // 8) + part] = rows[8 * part : 8 * part + 8]
-
-
-def extend_kernel(spans, sides, *refs):
-    others = refs[:sides]
-    behind = refs[sides : sides + 5]
-    source, kappa_ext, face = refs[sides + 5 : sides + 8]
-    strips = refs[sides + 8 : 2 * sides + 8]
-    held = refs[2 * sides + 8 : -1]
-    copies = [pltpu.make_async_copy(a, b, refs[-1].at[i]) for i, (a, b) in enumerate(zip(behind, held))]
-    for copy in copies:
-        copy.start()
-    own, kappa, sigma, upper, lower = held
-    size_x, size_y, size_z = kappa.shape
-    ext_y = size_y + 2 * HALO
-    parts = others[0].shape[0] - HALO * 2 * ext_y // 8
-    if sides == 1:
-        starts = [jnp.where(lax.axis_index("stream") == 0, 0, size_x - HALO)]
-    else:
-        starts = [0, size_x - HALO]
-    for packed, strip, start in zip(others, strips, starts):
-
-        def payload_of(j, packed=packed):
-            each = parts // spans
-            return jnp.concatenate([packed[j * each + part] for part in range(each)], axis=1)
-
-        spread(payload_of, spans, (0, spans), near_of(spans), strip, start, HALO, size_y, size_z, None)
-    for copy in copies:
-        copy.wait()
     vert = lax.axis_index("vert")
     side = pl.ds(pl.multiple_of(jnp.where(vert == 0, size_z - 128, 0), 128), 128)
     for x in range(size_x + sides * HALO):
@@ -192,11 +183,11 @@
             kappa_ext[x] = jnp.concatenate([kappa[x], upper[x, 0:HALO], lower[x, 0:HALO]], axis=0)
             sig = jnp.concatenate([sigma[x], upper[x, HALO:], lower[x, HALO:]], axis=0)
         else:
-            packed = others[(x - size_x) // HALO]
-            tiles = ext_y // 8
-            base = parts + (x - size_x) % HALO * 2 * tiles
-            kappa_ext[x] = jnp.concatenate([packed[base + k] for k in range(tiles)], axis=0)
-            sig = jnp.concatenate([packed[base + tiles + k] for k in range(tiles)], axis=0)
+            slab, corner = slabs[(x - size_x) // HALO], corners[(x - size_x) // HALO]
+            i = (x - size_x) % HALO
+            up, low = corner[i, 0 : 2 * HALO], corner[i, 2 * HALO :]
+            kappa_ext[x] = jnp.concatenate([slab[i, 0:size_y], up[0:HALO], low[0:HALO]], axis=0)
+            sig = jnp.concatenate([slab[i, size_y:], up[HALO:], low[HALO:]], axis=0)
         for c in range(3):
             if x < size_x:
                 value = own[c, x * ext_y : (x + 1) * ext_y, :]
@@ -247,6 +238,9 @@
         root[x, :, 0:size_z] = jnp.sqrt(kappa_ext[x])
 
     each_plane(planes, fill)
+    for x in range(size_x, planes):
+        for c in range(3):
+            pong[c, x] = jnp.zeros((ext_y, ext_z), F32)
     lane = lax.broadcasted_iota(jnp.int32, (ext_y, 128), 1)
     known = lax.broadcasted_iota(jnp.int32, (8, 128), 1) // 8 == vert * 15
     for t, (c, x, y) in enumerate(face_tiles(planes, ext_y)):
@@ -301,9 +295,9 @@
         each_plane(size_x + sides * deep, one_plane)
 
 
-def call(kernel, outs, scratch, flops, *args, left=(), aliases=()):
+def call(kernel, outs, scratch, flops, *args, left=(), aliases=(), room=8):
     moved = sum(4 * a.size for a in args) + sum(4 * o.size for o in outs)
-    spaces = [pl.ANY if i in left else pltpu.VMEM for i in range(len(args))]
+    spaces = [pltpu.HBM if i in left else pltpu.VMEM for i in range(len(args))]
     return pl.pallas_call(
         kernel,
         out_shape=outs,
@@ -311,7 +305,7 @@
         out_specs=[pl.BlockSpec(memory_space=pltpu.VMEM)] * len(outs),
         scratch_shapes=scratch,
         input_output_aliases=dict(aliases),
-        compiler_params=pltpu.CompilerParams(vmem_limit_bytes=56 * 1024 * 1024),
+        compiler_params=pltpu.CompilerParams(vmem_limit_bytes=room * 1024 * 1024),
         cost_estimate=pl.CostEstimate(flops=flops, bytes_accessed=moved, transcendentals=0),
     )(*args)
 
@@ -350,11 +344,7 @@
     gates = gate_residual.shape[2]
     ext_x, ext_y = size_x + sides * HALO, size_y + 2 * HALO
     shape = lambda *dims: jax.ShapeDtypeStruct(dims, F32)
-    payload, to_upper, to_lower = call(
-        pack_kernel,
-        [shape(8, gates)] + [shape(size_x, 2 * HALO, size_z)] * 2,
-        [],
-        1000,
+    inputs = [
         gate_residual,
         gate_azimuth,
         gate_elevation,
@@ -366,30 +356,29 @@
         point_z,
         kappa,
         sigma,
+    ]
+    payload, to_upper, to_lower, *slabs = call(
+        functools.partial(pack_kernel, sides),
+        [shape(8, gates)] + [shape(size_x, 2 * HALO, size_z)] * 2 + [shape(HALO, 2 * size_y, size_z)] * sides,
+        [],
+        1000,
+        *inputs,
+        room=56,
     )
     if spans == 4:
         payloads = [payload, ring(payload, 1), ring(payload, -1), ring(payload, 2)]
     else:
         payloads = [jnp.roll(lax.all_gather(payload, "span"), -lax.axis_index("span"), axis=0)]
+    slabs = across_bands(slabs)
     from_lower, from_upper = ring(to_upper, 1), ring(to_lower, -1)
     dims = (size_x, size_y, size_z)
     work = 12 * size_x * ext_y * size_z * gates
     planes = shape(3, size_x * ext_y, size_z)
-    (own,) = call(functools.partial(first_kernel, spans, dims), [planes], [], work, payload)
-    parts = spans * gates // size_z + HALO * 2 * ext_y // 8
-    others = across_bands(
-        call(
-            functools.partial(bands_kernel, sides, len(payloads)),
-            [shape(parts, 8, size_z)] * sides,
-            [],
-            1000,
-            *payloads,
-            kappa,
-            sigma,
-            from_upper,
-            from_lower,
-        )
-    )
+    (own,) = call(functools.partial(first_kernel, spans, dims), [planes], [], work, payload, room=24)
+    gathered = payloads if len(payloads) == 1 else call(
+        functools.partial(gather_kernel, spans), [shape(spans, 8, gates)], [], 1000, *payloads
+    )
+    others = across_bands(gathered * sides)
     (own,) = call(
         functools.partial(second_kernel, spans, dims, len(payloads)),
         [planes],
@@ -398,19 +387,40 @@
         *payloads,
         own,
         aliases=((len(payloads), 0),),
-    )
-    behind = [own, kappa, sigma, from_upper, from_lower]
+        room=24,
+    )
+    corners = across_bands(
+        call(
+            functools.partial(corner_kernel, sides),
+            [shape(HALO, 4 * HALO, size_z)] * sides,
+            [],
+            1000,
+            from_upper,
+            from_lower,
+        )
+    )
+    strips = call(
+        functools.partial(strip_kernel, spans, sides, dims),
+        [shape(3, HALO * ext_y, size_z)] * sides,
+        [],
+        work // 4 * spans,
+        *others,
+        room=24,
+    )
     tiles = len(face_tiles(ext_x, ext_y))
     source, kappa_ext, face = call(
-        functools.partial(extend_kernel, spans, sides),
+        functools.partial(extend_kernel, sides),
         [shape(3, ext_x, ext_y, size_z), shape(ext_x, ext_y, size_z), shape(-(-tiles // 16), 8, 128)],
-        [pltpu.VMEM((3, HALO * ext_y, size_z), F32)] * sides
-        + [pltpu.VMEM(a.shape, F32) for a in behind]
-        + [pltpu.SemaphoreType.DMA((len(behind),))],
-        work // 4 * spans,
-        *others,
-        *behind,
-        left=range(sides, sides + len(behind)),
+        [],
+        1000,
+        own,
+        kappa,
+        sigma,
+        from_upper,
+        from_lower,
+        *strips,
+        *slabs,
+        *corners,
     )
     face = lax.ppermute(face, "vert", [(0, 1), (1, 0)])
     wide = (ext_x, ext_y, size_z + 128)
@@ -422,6 +432,7 @@
         source,
         kappa_ext,
         face,
+        room=20,
     )
     return field
 

time: 48.6 us -> 37.3 us (0.77)
  Pallas kernels: 31.6 us -> 21.9 us
  starting transfers between devices: 11 us -> 13 us
  local copies, waits for them, and re-layouts: 2.63 us -> 0.78 us
  waiting for transfers between devices: 3.03 us -> 1.26 us
    pallas_call x6 -> x8, Pallas kernels: 31.6 us -> 21.9 us  [call(): pl.pallas_call(kernel, out_shape=outs, in_specs=[pl.BlockSpec(memory_spac...]
    ppermute x1 -> x3, starting transfers between devices: 1.49 us -> 3.71 us  [across_bands(): return [lax.ppermute(arrays[0], 'stream', [(0, 1), (1, 0)])]]
    unnamed x14 -> x10, local copies, waits for them, and re-layouts: 2.63 us -> 0.78 us
    ppermute x5, waiting for transfers between devices: 1.58 us -> 0.01 us  [ring(): lax.ppermute(array, 'span', [(i, (i + step) % count) for i in range(count)])]
  transfers between devices with their start and end apart: 7 -> 9, of which waited for: 3 -> 1; matrix products, arithmetic and copies ran while one was open for 0% -> 0% of each run, Pallas kernels for 23% -> 27%
where the time goes in v3:
time: 37.3 us; the launch traced here: 37.1 us
  Pallas kernels  21.9 us (59%)
  starting transfers between devices  13 us (35%)
  waiting for transfers between devices  1.26 us (3%)
  local copies, waits for them, and re-layouts  0.78 us (2%)
    pallas_call x8, Pallas kernels, call(): pl.pallas_call(kernel, out_shape=outs, in_specs=[pl.BlockSpec(memory_spac...  21.9 us
    ppermute x5, starting transfers between devices, ring(): lax.ppermute(array, 'span', [(i, (i + step) % count) for i in range(count)])  9.21 us
    ppermute x3, starting transfers between devices, across_bands(): return [lax.ppermute(arrays[0], 'stream', [(0, 1), (1, 0)])]  3.71 us
    ppermute x1, waiting for transfers between devices, on_device(): face = lax.ppermute(face, 'vert', [(0, 1), (1, 0)])  1.23 us
    unnamed x10, local copies, waits for them, and re-layouts  0.78 us
  transfers between devices with their start and end apart: 9, of which 1 were waited for; matrix products, arithmetic and copies ran while one was open for 0% of the time, Pallas kernels for 27%

profile of v3, /device:TPU:0, one launch (start us, length us, event | category | flops | bytes accessed | tf_op | source)
XLA Modules:
  0.0 37.1 jit_solution(9901071644958234723)
XLA Ops:
  0.0 1.9 %shard_map.109 = (f32[8,1024]{1,0:T(8,128)}, f32[16,8,256]{2,1,0:T(8,128)}, f32[16,8,256]{2,1,0:T(8,128)}, f32[4,32,256]{2,1,0:T(8,128)}) custom-call(f32[1,1,1024]{2,1,0:T(1,128)} %refs_0_.1, f32[1,1,1024]{2,1,0:T(1,128)} %refs_1_.2, f32[1,1,1024]{2,1,0:T(1,128)} %refs_2_.2, s32[1,1024]{1,0:T(1,128)} %bitcast.1, s32[1,1,1024]{2,1,0:T(1,128)} %refs_4_.1, ...), custom_call_target="tpu_custom_call" | custom-call | flops 1000 | bytes 976896 | tf_op jit(solution)/shard_map/pallas_call | solution.py:301
  1.9 4.0 %collective-permute-start.2 = (f32[8,1024]{1,0:T(8,128)}, f32[8,1024]{1,0:T(8,128)S(1)}, u32[]{:S(2)}, u32[]{:S(2)}) collective-permute-start(f32[8,1024]{1,0:T(8,128)} %get-tuple-element.12.payload.refs_0_), channel_id=1, source_target_pairs={{0,8},{4,12},{8,0},{12,4},{1,9},{5,13},{9,1},{13,5},{2,10},{6,14},... | collective-permute-start | bytes 98312 | tf_op jit(solution)/shard_map/ppermute | solution.py:315
  6.0 1.3 %collective-permute-start.1 = (f32[8,1024]{1,0:T(8,128)}, f32[8,1024]{1,0:T(8,128)S(1)}, u32[]{:S(2)}, u32[]{:S(2)}) collective-permute-start(f32[8,1024]{1,0:T(8,128)} %get-tuple-element.12.payload.refs_0_), channel_id=1, source_target_pairs={{0,12},{4,0},{8,4},{12,8},{1,13},{5,1},{9,5},{13,9},{2,14},{6,2},{... | collective-permute-start | bytes 98312 | tf_op jit(solution)/shard_map/ppermute | solution.py:315
  7.3 0.7 %collective-permute-start = (f32[8,1024]{1,0:T(8,128)}, f32[8,1024]{1,0:T(8,128)S(1)}, u32[]{:S(2)}, u32[]{:S(2)}) collective-permute-start(f32[8,1024]{1,0:T(8,128)} %get-tuple-element.12.payload.refs_0_), channel_id=1, source_target_pairs={{0,4},{4,8},{8,12},{12,0},{1,5},{5,9},{9,13},{13,1},{2,6},{6,10},{... | collective-permute-start | bytes 98312 | tf_op jit(solution)/shard_map/ppermute | solution.py:315
  8.0 3.1 %collective-permute-start.3 = (f32[16,8,256]{2,1,0:T(8,128)}, f32[16,8,256]{2,1,0:T(8,128)S(1)}, u32[]{:S(2)}, u32[]{:S(2)}) collective-permute-start(f32[16,8,256]{2,1,0:T(8,128)} %get-tuple-element.13), channel_id=1, source_target_pairs={{0,12},{4,0},{8,4},{12,8},{1,13},{5,1},{9,5},{13,9},{2,14},{6,2},{... | collective-permute-start | bytes 393224 | tf_op jit(solution)/shard_map/ppermute | solution.py:315
  11.2 0.0 collective-permute-start.4
  11.2 0.8 %copy-done.2 = f32[8,1024]{1,0:T(8,128)S(1)} copy-done((f32[8,1024]{1,0:T(8,128)S(1)}, f32[8,1024]{1,0:T(8,128)}, u32[]{:S(2)}) %copy-start.2) | copy-done | bytes 32792
  11.9 0.0 copy-start.4
  11.9 1.9 %shard_map.110.refs_4_ = f32[3,384,256]{2,1,0:T(8,128)S(1)} custom-call(f32[8,1024]{1,0:T(8,128)S(1)} %copy-done.2), custom_call_target="tpu_custom_call" | custom-call | flops 1207959552 | bytes 1212416 | tf_op jit(solution)/shard_map/pallas_call | solution.py:301
  13.9 0.0 collective-permute-done.2.refs_3_
  13.9 0.0 copy-done.4
  13.9 1.6 %collective-permute-start.6 = (f32[4,32,256]{2,1,0:T(8,128)S(1)}, f32[4,32,256]{2,1,0:T(8,128)S(1)}, u32[]{:S(2)}, u32[]{:S(2)}) collective-permute-start(f32[4,32,256]{2,1,0:T(8,128)S(1)} %copy-done.4), channel_id=1, source_target_pairs={{0,2},{2,0},{1,3},{3,1},{4,6},{6,4},{5,7},{7,5},{8,10},{10,8},{9,1... | collective-permute-start | bytes 393224 | tf_op jit(solution)/shard_map/ppermute | solution.py:321
  15.4 0.0 collective-permute-done.1.refs_2_
  15.4 0.0 collective-permute-done.refs_1_
  15.5 0.6 %collective-permute-start.5 = (f32[4,8,1024]{2,1,0:T(8,128)S(1)}, f32[4,8,1024]{2,1,0:T(8,128)S(1)}, u32[]{:S(2)}, u32[]{:S(2)}) collective-permute-start(f32[4,8,1024]{2,1,0:T(8,128)S(1)} %shard_map.112), channel_id=1, source_target_pairs={{0,2},{2,0},{1,3},{3,1},{4,6},{6,4},{5,7},{7,5},{8,10},{10,8},{9,1... | collective-permute-start | bytes 393224 | tf_op jit(solution)/shard_map/ppermute | solution.py:321
  16.1 0.0 copy-done.3
  16.1 5.2 %shard_map.111.refs_0_ = f32[3,384,256]{2,1,0:T(8,128)S(1)} custom-call(f32[8,1024]{1,0:T(8,128)S(1)} %copy-done.3, f32[8,1024]{1,0:T(8,128)S(1)} %collective-permute-done.refs_1_, f32[8,1024]{1,0:T(8,128)S(1)} %collective-permute-done.1.refs_2_, f32[8,1024]{1,0:T(8,128)S(1)} %collective-permute-done.2.refs_3_, ...), custom_call_target="tpu_custom_call", output_to_operand_aliasing={{}: (4, {})} | custom-call | flops 3623878656 | bytes 2490368 | tf_op jit(solution)/shard_map/pallas_call | solution.py:301
  21.2 0.0 collective-permute-done.3.upper.refs_3_
  21.3 0.0 collective-permute-done.4.lower.refs_4_
  21.3 0.0 copy-start
  21.3 0.0 copy-start.1
  21.3 1.6 %collective-permute-start.7 = (f32[4,16,256]{2,1,0:T(8,128)S(1)}, f32[4,16,256]{2,1,0:T(8,128)S(1)}, u32[]{:S(2)}, u32[]{:S(2)}) collective-permute-start(f32[4,16,256]{2,1,0:T(8,128)S(1)} %shard_map.114), channel_id=1, source_target_pairs={{0,2},{2,0},{1,3},{3,1},{4,6},{6,4},{5,7},{7,5},{8,10},{10,8},{9,1... | collective-permute-start | bytes 196616 | tf_op jit(solution)/shard_map/ppermute | solution.py:321
  22.9 0.0 collective-permute-done.5.refs_0_
  22.9 2.8 %shard_map.113.refs_5_ = f32[3,96,256]{2,1,0:T(8,128)S(1)} custom-call(f32[4,8,1024]{2,1,0:T(8,128)S(1)} %collective-permute-done.5.refs_0_), custom_call_target="tpu_custom_call" | custom-call | flops 1207959552 | bytes 425984 | tf_op jit(solution)/shard_map/pallas_call | solution.py:301
  25.6 0.0 collective-permute-done.6.refs_6_
  25.6 0.0 collective-permute-done.7.refs_7_
  25.7 0.0 copy-done
  25.7 0.0 copy-done.1
  25.7 0.5 %shard_map.115 = (f32[3,20,24,256]{3,2,1,0:T(8,128)S(1)}, f32[20,24,256]{2,1,0:T(8,128)S(1)}, f32[15,8,128]{2,1,0:T(8,128)S(1)}) custom-call(f32[3,384,256]{2,1,0:T(8,128)S(1)} %shard_map.111.refs_0_, f32[16,16,256]{2,1,0:T(8,128)S(1)} %copy-done, f32[16,16,256]{2,1,0:T(8,128)S(1)} %copy-done.1, f32[16,8,256]{2,1,0:T(8,128)S(1)} %collective-permute-done.3.upper.refs_3_, ...), custom_call_target="tpu_custom_call" | custom-call | flops 1000 | bytes 4485120 | tf_op jit(solution)/shard_map/pallas_call | solution.py:301
  26.2 0.1 collective-permute-start.8
  26.3 1.2 %collective-permute-done.8.face = f32[15,8,128]{2,1,0:T(8,128)S(1)} collective-permute-done((f32[15,8,128]{2,1,0:T(8,128)S(1)}, f32[15,8,128]{2,1,0:T(8,128)S(1)}, u32[]{:S(2)}, u32[]{:S(2)}) %collective-permute-start.8) | collective-permute-done | bytes 61472 | tf_op jit(solution)/shard_map/ppermute | solution.py:425
  27.5 9.5 %shard_map.116 = f32[3,16,16,256]{3,2,1,0:T(8,128)} custom-call(f32[3,20,24,256]{3,2,1,0:T(8,128)S(1)} %get-tuple-element.16.source, f32[20,24,256]{2,1,0:T(8,128)S(1)} %get-tuple-element.17.kappa_ext, f32[15,8,128]{2,1,0:T(8,128)S(1)} %collective-permute-done.8.face), custom_call_target="tpu_custom_call" | custom-call | flops 22118400 | bytes 2813952 | tf_op jit(solution)/shard_map/pallas_call | solution.py:301
  (4 shorter events, 0.0 us)
Async XLA Ops:
  1.9 11.9 %collective-permute-start.2 = (f32[8,1024]{1,0:T(8,128)}, f32[8,1024]{1,0:T(8,128)S(1)}, u32[]{:S(2)}, u32[]{:S(2)}) collective-permute-start(f32[8,1024]{1,0:T(8,128)} %get-tuple-element.12.payload.refs_0_), channel_id=1, source_target_pairs={{0,8},{4,12},{8,0},{12,4},{1,9},{5,13},{9,1},{13,5},{2,10},{6,14},... | collective-permute-start | bytes 98312 | tf_op jit(solution)/shard_map/ppermute | solution.py:315
  6.0 9.5 %collective-permute-start.1 = (f32[8,1024]{1,0:T(8,128)}, f32[8,1024]{1,0:T(8,128)S(1)}, u32[]{:S(2)}, u32[]{:S(2)}) collective-permute-start(f32[8,1024]{1,0:T(8,128)} %get-tuple-element.12.payload.refs_0_), channel_id=1, source_target_pairs={{0,12},{4,0},{8,4},{12,8},{1,13},{5,1},{9,5},{13,9},{2,14},{6,2},{... | collective-permute-start | bytes 98312 | tf_op jit(solution)/shard_map/ppermute | solution.py:315
  7.3 8.1 %collective-permute-start = (f32[8,1024]{1,0:T(8,128)}, f32[8,1024]{1,0:T(8,128)S(1)}, u32[]{:S(2)}, u32[]{:S(2)}) collective-permute-start(f32[8,1024]{1,0:T(8,128)} %get-tuple-element.12.payload.refs_0_), channel_id=1, source_target_pairs={{0,4},{4,8},{8,12},{12,0},{1,5},{5,9},{9,13},{13,1},{2,6},{6,10},{... | collective-permute-start | bytes 98312 | tf_op jit(solution)/shard_map/ppermute | solution.py:315
  8.0 13.2 %collective-permute-start.3 = (f32[16,8,256]{2,1,0:T(8,128)}, f32[16,8,256]{2,1,0:T(8,128)S(1)}, u32[]{:S(2)}, u32[]{:S(2)}) collective-permute-start(f32[16,8,256]{2,1,0:T(8,128)} %get-tuple-element.13), channel_id=1, source_target_pairs={{0,12},{4,0},{8,4},{12,8},{1,13},{5,1},{9,5},{13,9},{2,14},{6,2},{... | collective-permute-start | bytes 393224 | tf_op jit(solution)/shard_map/ppermute | solution.py:315
  11.2 10.1 %collective-permute-start.4 = (f32[16,8,256]{2,1,0:T(8,128)}, f32[16,8,256]{2,1,0:T(8,128)S(1)}, u32[]{:S(2)}, u32[]{:S(2)}) collective-permute-start(f32[16,8,256]{2,1,0:T(8,128)} %get-tuple-element.14), channel_id=1, source_target_pairs={{0,4},{4,8},{8,12},{12,0},{1,5},{5,9},{9,13},{13,1},{2,6},{6,10},{... | collective-permute-start | bytes 393224 | tf_op jit(solution)/shard_map/ppermute | solution.py:315
  11.2 0.8 %copy-start.2 = (f32[8,1024]{1,0:T(8,128)S(1)}, f32[8,1024]{1,0:T(8,128)}, u32[]{:S(2)}) copy-start(f32[8,1024]{1,0:T(8,128)} %get-tuple-element.12.payload.refs_0_) | copy-start | bytes 98308
  11.9 2.0 %copy-start.4 = (f32[4,32,256]{2,1,0:T(8,128)S(1)}, f32[4,32,256]{2,1,0:T(8,128)}, u32[]{:S(2)}) copy-start(f32[4,32,256]{2,1,0:T(8,128)} %get-tuple-element.15) | copy-start | bytes 393220
  11.9 4.2 %copy-start.3 = (f32[8,1024]{1,0:T(8,128)S(1)}, f32[8,1024]{1,0:T(8,128)}, u32[]{:S(2)}) copy-start(f32[8,1024]{1,0:T(8,128)} %get-tuple-element.12.payload.refs_0_) | copy-start | bytes 98308
  13.9 11.7 %collective-permute-start.6 = (f32[4,32,256]{2,1,0:T(8,128)S(1)}, f32[4,32,256]{2,1,0:T(8,128)S(1)}, u32[]{:S(2)}, u32[]{:S(2)}) collective-permute-start(f32[4,32,256]{2,1,0:T(8,128)S(1)} %copy-done.4), channel_id=1, source_target_pairs={{0,2},{2,0},{1,3},{3,1},{4,6},{6,4},{5,7},{7,5},{8,10},{10,8},{9,1... | collective-permute-start | bytes 393224 | tf_op jit(solution)/shard_map/ppermute | solution.py:321
  15.5 7.4 %collective-permute-start.5 = (f32[4,8,1024]{2,1,0:T(8,128)S(1)}, f32[4,8,1024]{2,1,0:T(8,128)S(1)}, u32[]{:S(2)}, u32[]{:S(2)}) collective-permute-start(f32[4,8,1024]{2,1,0:T(8,128)S(1)} %shard_map.112), channel_id=1, source_target_pairs={{0,2},{2,0},{1,3},{3,1},{4,6},{6,4},{5,7},{7,5},{8,10},{10,8},{9,1... | collective-permute-start | bytes 393224 | tf_op jit(solution)/shard_map/ppermute | solution.py:321
  21.3 4.4 %copy-start = (f32[16,16,256]{2,1,0:T(8,128)S(1)}, f32[16,16,256]{2,1,0:T(8,128)}, u32[]{:S(2)}) copy-start(f32[16,16,256]{2,1,0:T(8,128)} %refs_1_.3) | copy-start | bytes 786436
  21.3 4.4 %copy-start.1 = (f32[16,16,256]{2,1,0:T(8,128)S(1)}, f32[16,16,256]{2,1,0:T(8,128)}, u32[]{:S(2)}) copy-start(f32[16,16,256]{2,1,0:T(8,128)} %refs_2_.3) | copy-start | bytes 786436
  21.3 4.3 %collective-permute-start.7 = (f32[4,16,256]{2,1,0:T(8,128)S(1)}, f32[4,16,256]{2,1,0:T(8,128)S(1)}, u32[]{:S(2)}, u32[]{:S(2)}) collective-permute-start(f32[4,16,256]{2,1,0:T(8,128)S(1)} %shard_map.114), channel_id=1, source_target_pairs={{0,2},{2,0},{1,3},{3,1},{4,6},{6,4},{5,7},{7,5},{8,10},{10,8},{9,1... | collective-permute-start | bytes 196616 | tf_op jit(solution)/shard_map/ppermute | solution.py:321
  26.2 1.3 %collective-permute-start.8 = (f32[15,8,128]{2,1,0:T(8,128)S(1)}, f32[15,8,128]{2,1,0:T(8,128)S(1)}, u32[]{:S(2)}, u32[]{:S(2)}) collective-permute-start(f32[15,8,128]{2,1,0:T(8,128)S(1)} %get-tuple-element.18), channel_id=1, source_target_pairs={{0,1},{1,0},{2,3},{3,2},{4,5},{5,4},{6,7},{7,6},{8,9},{9,8},{10,11... | collective-permute-start | bytes 184328 | tf_op jit(solution)/shard_map/ppermute | solution.py:425

commit v4 on v3

--- a/solution.py
+++ b/solution.py
@@ -29,10 +29,14 @@
     return lax.dot_general(left, right, CONTRACT_LANES, preferred_element_type=F32)
 
 
-def pack_kernel(sides, *refs):
-    residual, azimuth, elevation, brick, cell, force, px, py, pz, kappa, sigma = refs[:11]
-    payload, to_upper, to_lower = refs[11:14]
-    slabs = refs[14:]
+def pack_kernel(*refs):
+    sources, payload, held, sems = refs[:9], refs[9], refs[10:19], refs[19]
+    copies = [pltpu.make_async_copy(a, b, sems.at[i]) for i, (a, b) in enumerate(zip(sources, held))]
+    for copy in copies:
+        copy.start()
+    for copy in copies:
+        copy.wait()
+    residual, azimuth, elevation, brick, cell, force, px, py, pz = held
     cosine = jnp.cos(elevation[0])
     value = residual[0]
     gates, points = value.shape[1], px.shape[1]
@@ -49,14 +53,6 @@
     ]
     for r, row in enumerate(rows):
         payload[r : r + 1, :] = row
-    size_x, size_y, size_z = kappa.shape
-    to_upper[:, 0:HALO] = kappa[:, size_y - HALO :]
-    to_upper[:, HALO:] = sigma[:, size_y - HALO :]
-    to_lower[:, 0:HALO] = kappa[:, 0:HALO]
-    to_lower[:, HALO:] = sigma[:, 0:HALO]
-    for slab, start in zip(slabs, edges(sides, size_x)):
-        slab[:, 0:size_y] = kappa[pl.ds(start, HALO)]
-        slab[:, size_y:] = sigma[pl.ds(start, HALO)]
 
 
 def edges(sides, size_x):
@@ -132,7 +128,7 @@
 
 
 def near_of(spans):
-    return ((0, 0), (1, -1), (2, 1)) if spans == 4 else ((0, 0), (spans - 1, -1), (1, 1))
+    return ((0, 0), (spans - 1, -1), (2 if spans == 4 else 1, 1))
 
 
 def first_kernel(spans, dims, payload, out):
@@ -151,9 +147,24 @@
     spread(lambda j: payload_in(payloads, j), spans, (1, spans), near, out, 0, size_x, size_y, size_z, first, unroll=count > 1)
 
 
-def gather_kernel(count, *refs):
-    for j in range(count):
-        refs[count][j] = refs[j][...]
+def gather_kernel(spans, sides, count, *refs):
+    payloads, (kappa, sigma, to_upper, to_lower), outs = refs[:count], refs[count : count + 4], refs[count + 4 :]
+    size_x, size_y, size_z = kappa.shape
+    for out, start in zip(outs, edges(sides, size_x)):
+        each = payloads[0].shape[-1] // size_z
+        for j in range(spans):
+            one = payload_in(payloads, j)
+            for part in range(each):
+                out[j * each + part] = one[:, part * size_z : (part + 1) * size_z]
+        for i in range(HALO):
+            for k, field in enumerate((kappa, sigma)):
+                plane = field[start + i]
+                for part in range(size_y // 8):
+                    out[spans * each + (2 * i + k) * (size_y // 8) + part] = plane[8 * part : 8 * part + 8]
+    to_upper[:, 0:HALO] = kappa[:, size_y - HALO :]
+    to_upper[:, HALO:] = sigma[:, size_y - HALO :]
+    to_lower[:, 0:HALO] = kappa[:, 0:HALO]
+    to_lower[:, HALO:] = sigma[:, 0:HALO]
 
 
 def corner_kernel(sides, upper, lower, *outs):
@@ -166,13 +177,18 @@
     size_x, size_y, size_z = dims
     starts = edges(sides, size_x)
     starts = [size_x - HALO - starts[0]] if sides == 1 else starts[::-1]
-    for payloads, strip, start in zip(refs[:sides], refs[sides:], starts):
-        spread(lambda j: payloads.at[j], spans, (0, spans), near_of(spans), strip, start, HALO, size_y, size_z, None)
+    for packed, strip, start in zip(refs[:sides], refs[sides:], starts):
+        each = (packed.shape[0] - HALO * 2 * size_y // 8) // spans
+
+        def payload_of(j, packed=packed, each=each):
+            return jnp.concatenate([packed[j * each + part] for part in range(each)], axis=1)
+
+        spread(payload_of, spans, (0, spans), near_of(spans), strip, start, HALO, size_y, size_z, None)
 
 
 def extend_kernel(sides, *refs):
     own, kappa, sigma, upper, lower = refs[:5]
-    strips, slabs, corners = (refs[5 + k * sides : 5 + (k + 1) * sides] for k in range(3))
+    strips, others, corners = (refs[5 + k * sides : 5 + (k + 1) * sides] for k in range(3))
     source, kappa_ext, face = refs[5 + 3 * sides :]
     size_x, size_y, size_z = kappa.shape
     ext_y = size_y + 2 * HALO
@@ -183,11 +199,14 @@
             kappa_ext[x] = jnp.concatenate([kappa[x], upper[x, 0:HALO], lower[x, 0:HALO]], axis=0)
             sig = jnp.concatenate([sigma[x], upper[x, HALO:], lower[x, HALO:]], axis=0)
         else:
-            slab, corner = slabs[(x - size_x) // HALO], corners[(x - size_x) // HALO]
+            packed, corner = others[(x - size_x) // HALO], corners[(x - size_x) // HALO]
             i = (x - size_x) % HALO
+            tiles = size_y // 8
+            base = packed.shape[0] - (HALO - i) * 2 * tiles
+            slab = [packed[base + k] for k in range(2 * tiles)]
             up, low = corner[i, 0 : 2 * HALO], corner[i, 2 * HALO :]
-            kappa_ext[x] = jnp.concatenate([slab[i, 0:size_y], up[0:HALO], low[0:HALO]], axis=0)
-            sig = jnp.concatenate([slab[i, size_y:], up[HALO:], low[HALO:]], axis=0)
+            kappa_ext[x] = jnp.concatenate([*slab[:tiles], up[0:HALO], low[0:HALO]], axis=0)
+            sig = jnp.concatenate([*slab[tiles:], up[HALO:], low[HALO:]], axis=0)
         for c in range(3):
             if x < size_x:
                 value = own[c, x * ext_y : (x + 1) * ext_y, :]
@@ -226,30 +245,16 @@
         step(i)
 
 
-def diffuse_kernel(sides, source, kappa_ext, face, out, ping, pong, root, ax, ay, aym, az, azm, keep):
+def coefficient_kernel(sides, size_x, kappa_ext, root, ax, ay, aym, az, azm, keep):
     planes, ext_y, size_z = kappa_ext.shape
-    size_x, size_y = out.shape[1], out.shape[2]
-    ext_z = size_z + 128
-    stream, vert = lax.axis_index("stream"), lax.axis_index("vert")
-
-    def fill(x):
-        for c in range(3):
-            ping[c, x, :, 0:size_z] = source[c, x]
-        root[x, :, 0:size_z] = jnp.sqrt(kappa_ext[x])
-
-    each_plane(planes, fill)
-    for x in range(size_x, planes):
-        for c in range(3):
-            pong[c, x] = jnp.zeros((ext_y, ext_z), F32)
+    stream, last = lax.axis_index("stream"), lax.axis_size("stream") - 1
+    place = lax.broadcasted_iota(jnp.int32, (ext_y, size_z), 1)
     lane = lax.broadcasted_iota(jnp.int32, (ext_y, 128), 1)
-    known = lax.broadcasted_iota(jnp.int32, (8, 128), 1) // 8 == vert * 15
-    for t, (c, x, y) in enumerate(face_tiles(planes, ext_y)):
-        turned = pltpu.roll(face[t // 16], (256 - 8 * (t % 16) - 8 * vert) & 127, 1)
-        if c == 3:
-            root[x, y : y + 8, size_z:] = jnp.sqrt(jnp.where(known, turned, 0.0))
-        else:
-            ping[c, x, y : y + 8, size_z:] = turned
-    last = lax.axis_size("stream") - 1
+
+    def roots(x):
+        root[x] = jnp.sqrt(kappa_ext[x])
+
+    each_plane(planes, roots)
 
     def faces(x):
         after = jnp.where(x == planes - 1, 0, x + 1)
@@ -259,34 +264,92 @@
         up = here * pltpu.roll(here, ext_y - 1, 0)
         ay[x] = up
         aym[x] = pltpu.roll(up, 1, 0)
-        up = here * lanes_on(here, -1, lane)
+        up = jnp.where(place == size_z - 1, 0.0, here * lanes_on(here, -1, lane))
         az[x] = up
         azm[x] = lanes_on(up, 1, lane)
 
     each_plane(planes, faces)
 
-    def total(x):
+    def rest(x):
         before = jnp.where(x == 0, planes - 1, x - 1)
         keep[x] = 1.0 - (ax[x] + ax[before] + ay[x] + aym[x] + az[x] + azm[x])
 
-    each_plane(planes, total)
+    each_plane(planes, rest)
+
+
+def diffuse_kernel(sides, source, root, ax, ay, aym, az, azm, keep, face, out, *scratch):
+    ping, pong, halo, root_h, ax_h, ay_h, aym_h, az_all, azm_all, keep_all = scratch
+    planes, ext_y, size_z = root.shape
+    size_x, size_y = out.shape[1], out.shape[2]
+    ext_z = size_z + 128
+    stream, vert = lax.axis_index("stream"), lax.axis_index("vert")
+    last = lax.axis_size("stream") - 1
+    for x in range(size_x, planes):
+        for c in range(3):
+            ping[c, x] = jnp.zeros((ext_y, ext_z), F32)
+            pong[c, x] = jnp.zeros((ext_y, ext_z), F32)
+    lane = lax.broadcasted_iota(jnp.int32, (ext_y, 128), 1)
+    known = lax.broadcasted_iota(jnp.int32, (8, 128), 1) // 8 == vert * 15
+    for t, (c, x, y) in enumerate(face_tiles(planes, ext_y)):
+        turned = pltpu.roll(face[t // 16], (256 - 8 * (t % 16) - 8 * vert) & 127, 1)
+        if c == 3:
+            root_h[x, y : y + 8, :] = jnp.sqrt(jnp.where(known, turned, 0.0))
+        else:
+            halo[c, x, y : y + 8, :] = turned
+
+    def faces(x):
+        after = jnp.where(x == planes - 1, 0, x + 1)
+        here, low, high = root_h[x], root[x, :, 0:128], root[x, :, size_z - 128 :]
+        wall = ((x == planes - 1) & (stream == 0)) | ((x == size_x - 1) & (stream == last))
+        ax_h[x] = here * root_h[after] * jnp.where(wall, 0.0, 1.0)
+        up = here * pltpu.roll(here, ext_y - 1, 0)
+        ay_h[x] = up
+        aym_h[x] = pltpu.roll(up, 1, 0)
+        over, under = pltpu.roll(here, 127, 1), pltpu.roll(here, 1, 1)
+        az_h = here * jnp.where(lane == 127, pltpu.roll(low, 127, 1), over)
+        azm_h = here * jnp.where(lane == 0, pltpu.roll(high, 1, 1), under)
+        top = jnp.where(lane == 127, high * over, 0.0)
+        bottom = jnp.where(lane == 0, low * under, 0.0)
+        none = [jnp.zeros((ext_y, 128), F32)] * (size_z // 128 - 1)
+        top, bottom = jnp.concatenate([*none, top], axis=1), jnp.concatenate([bottom, *none], axis=1)
+        az_all[x, :, 0:size_z] = az[x] + top
+        az_all[x, :, size_z:] = az_h
+        azm_all[x, :, 0:size_z] = azm[x] + bottom
+        azm_all[x, :, size_z:] = azm_h
+        keep_all[x, :, 0:size_z] = keep[x] - (top + bottom)
+
+    each_plane(planes, faces)
+
+    def rest(x):
+        before = jnp.where(x == 0, planes - 1, x - 1)
+        sides_sum = ax_h[x] + ax_h[before] + ay_h[x] + aym_h[x]
+        keep_all[x, :, size_z:] = 1.0 - (sides_sum + az_all[x, :, size_z:] + azm_all[x, :, size_z:])
+
+    each_plane(planes, rest)
+
+    def wide(main, beside):
+        return jnp.concatenate([main, beside], axis=1)
 
     for p in range(PASSES):
         deep = PASSES - 1 - p
         old, new = (ping, pong) if p % 2 == 0 else (pong, ping)
         first = jnp.where(stream == 0, 0, planes - deep) if sides == 1 else planes - deep
 
-        def one_plane(i, old=old, new=new, first=first, p=p):
+        def value_of(c, x, old=old, p=p):
+            return wide(source[c, x], halo[c, x]) if p == 0 else old[c, x]
+
+        def one_plane(i, value_of=value_of, new=new, first=first, p=p):
             x = i + first
             x = jnp.where(x >= planes, x - planes, x)
             after = jnp.where(x == planes - 1, 0, x + 1)
             before = jnp.where(x == 0, planes - 1, x - 1)
             for c in range(3):
-                value = old[c, x]
-                moved = keep[x] * value
-                moved += ax[x] * old[c, after] + ax[before] * old[c, before]
-                moved += ay[x] * pltpu.roll(value, ext_y - 1, 0) + aym[x] * pltpu.roll(value, 1, 0)
-                moved += az[x] * lanes_on(value, -1, lane) + azm[x] * lanes_on(value, 1, lane)
+                value = value_of(c, x)
+                moved = keep_all[x] * value
+                moved += wide(ax[x], ax_h[x]) * value_of(c, after) + wide(ax[before], ax_h[before]) * value_of(c, before)
+                moved += wide(ay[x], ay_h[x]) * pltpu.roll(value, ext_y - 1, 0)
+                moved += wide(aym[x], aym_h[x]) * pltpu.roll(value, 1, 0)
+                moved += az_all[x] * lanes_on(value, -1, lane) + azm_all[x] * lanes_on(value, 1, lane)
                 if p == PASSES - 1:
                     out[c, x] = moved[0:size_y, 0:size_z]
                 else:
@@ -354,31 +417,35 @@
         point_x,
         point_y,
         point_z,
-        kappa,
-        sigma,
     ]
-    payload, to_upper, to_lower, *slabs = call(
-        functools.partial(pack_kernel, sides),
-        [shape(8, gates)] + [shape(size_x, 2 * HALO, size_z)] * 2 + [shape(HALO, 2 * size_y, size_z)] * sides,
-        [],
+    (payload,) = call(
+        pack_kernel,
+        [shape(8, gates)],
+        [pltpu.VMEM(a.shape, a.dtype) for a in inputs] + [pltpu.SemaphoreType.DMA((len(inputs),))],
         1000,
-        *inputs,
-        room=56,
+        *[pltpu.with_memory_space_constraint(a, pltpu.HBM) for a in inputs],
+        left=range(len(inputs)),
     )
     if spans == 4:
-        payloads = [payload, ring(payload, 1), ring(payload, -1), ring(payload, 2)]
+        payloads = [payload, ring(payload, 2), ring(payload, -1), ring(payload, 1)]
     else:
         payloads = [jnp.roll(lax.all_gather(payload, "span"), -lax.axis_index("span"), axis=0)]
-    slabs = across_bands(slabs)
-    from_lower, from_upper = ring(to_upper, 1), ring(to_lower, -1)
     dims = (size_x, size_y, size_z)
     work = 12 * size_x * ext_y * size_z * gates
     planes = shape(3, size_x * ext_y, size_z)
     (own,) = call(functools.partial(first_kernel, spans, dims), [planes], [], work, payload, room=24)
-    gathered = payloads if len(payloads) == 1 else call(
-        functools.partial(gather_kernel, spans), [shape(spans, 8, gates)], [], 1000, *payloads
-    )
-    others = across_bands(gathered * sides)
+    parts = spans * gates // size_z + HALO * 2 * size_y // 8
+    to_upper, to_lower, *others = call(
+        functools.partial(gather_kernel, spans, sides, len(payloads)),
+        [shape(size_x, 2 * HALO, size_z)] * 2 + [shape(parts, 8, size_z)] * sides,
+        [],
+        1000,
+        *payloads,
+        kappa,
+        sigma,
+    )
+    others = across_bands(others)
+    from_lower, from_upper = ring(to_upper, 1), ring(to_lower, -1)
     (own,) = call(
         functools.partial(second_kernel, spans, dims, len(payloads)),
         [planes],
@@ -419,18 +486,22 @@
         from_upper,
         from_lower,
         *strips,
-        *slabs,
+        *others,
         *corners,
     )
     face = lax.ppermute(face, "vert", [(0, 1), (1, 0)])
-    wide = (ext_x, ext_y, size_z + 128)
+    main, beside, wide = ((ext_x, ext_y, width) for width in (size_z, 128, size_z + 128))
+    coefficients = call(
+        functools.partial(coefficient_kernel, sides, size_x), [shape(*main)] * 7, [], 30 * ext_x * ext_y * size_z, kappa_ext
+    )
+    scratch = [(3, *wide)] * 2 + [(3, *beside)] + [beside] * 4 + [wide] * 3
     (field,) = call(
         functools.partial(diffuse_kernel, sides),
         [shape(3, size_x, size_y, size_z)],
-        [pltpu.VMEM((3, *wide), F32)] * 2 + [pltpu.VMEM(wide, F32)] * 7,
+        [pltpu.VMEM(dims, F32) for dims in scratch],
         60 * 3 * ext_x * ext_y * size_z,
         source,
-        kappa_ext,
+        *coefficients,
         face,
         room=20,
     )

time: 37.3 us -> 35.1 us (0.941)
  starting transfers between devices: 13 us -> 11.4 us
  local copies, waits for them, and re-layouts: 0.78 us -> 0.01 us
  waiting for transfers between devices: 1.26 us -> 2 us
  Pallas kernels: 21.9 us -> 21.3 us
    ppermute x5, waiting for transfers between devices: 0.01 us -> 1.99 us  [ring(): lax.ppermute(array, 'span', [(i, (i + step) % count) for i in range(count)])]
    ppermute x1, waiting for transfers between devices: 1.23 us -> 0.01 us  [on_device(): face = lax.ppermute(face, 'vert', [(0, 1), (1, 0)])]
    ppermute x5, starting transfers between devices: 9.21 us -> 8.37 us  [ring(): lax.ppermute(array, 'span', [(i, (i + step) % count) for i in range(count)])]
    unnamed x10 -> x4, local copies, waits for them, and re-layouts: 0.78 us -> 0.01 us
    ppermute x3 -> x2, starting transfers between devices: 3.71 us -> 2.98 us  [across_bands(): return [lax.ppermute(arrays[0], 'stream', [(0, 1), (1, 0)])]]
    pallas_call x8 -> x9, Pallas kernels: 21.9 us -> 21.3 us  [call(): pl.pallas_call(kernel, out_shape=outs, in_specs=[pl.BlockSpec(memory_spac...]
  transfers between devices with their start and end apart: 9 -> 8, of which waited for: 1 -> 2; matrix products, arithmetic and copies ran while one was open for 0% -> 0% of each run, Pallas kernels for 27% -> 32%
where the time goes in v4:
time: 35.1 us; the launch traced here: 34.8 us
  Pallas kernels  21.3 us (61%)
  starting transfers between devices  11.4 us (32%)
  waiting for transfers between devices  2 us (6%)
    pallas_call x9, Pallas kernels, call(): pl.pallas_call(kernel, out_shape=outs, in_specs=[pl.BlockSpec(memory_spac...  21.3 us
    ppermute x5, starting transfers between devices, ring(): lax.ppermute(array, 'span', [(i, (i + step) % count) for i in range(count)])  8.37 us
    ppermute x2, starting transfers between devices, across_bands(): return [lax.ppermute(arrays[0], 'stream', [(0, 1), (1, 0)])]  2.98 us
    ppermute x5, waiting for transfers between devices, ring(): lax.ppermute(array, 'span', [(i, (i + step) % count) for i in range(count)])  1.99 us
  transfers between devices with their start and end apart: 8, of which 2 were waited for; matrix products, arithmetic and copies ran while one was open for 0% of the time, Pallas kernels for 32%

profile of v4, /device:TPU:0, one launch (start us, length us, event | category | flops | bytes accessed | tf_op | source)
XLA Modules:
  0.0 34.8 jit_solution(16753097992753911955)
XLA Ops:
  0.0 0.9 %shard_map.109.payload.refs_0_ = f32[8,1024]{1,0:T(8,128)S(1)} custom-call(f32[1,1,1024]{2,1,0:T(1,128)} %refs_0_.1, f32[1,1,1024]{2,1,0:T(1,128)} %refs_1_.2, f32[1,1,1024]{2,1,0:T(1,128)} %refs_2_.2, s32[1,1024]{1,0:T(1,128)} %bitcast.1, s32[1,1,1024]{2,1,0:T(1,128)} %refs_4_.2, f32[3,1,256]{2,1,0:T(1,128)} %refs_5_.2, f32[1,256]{1,0:T(1,128)} %refs_6_.1, ...), custom_call_target="tpu_custom_call" | custom-call | flops 1000 | bytes 59392 | tf_op jit(solution)/shard_map/pallas_call | solution.py:364
  0.9 0.0 copy-start
  1.0 0.0 copy-start.1
  1.0 3.1 %collective-permute-start.2 = (f32[8,1024]{1,0:T(8,128)S(1)}, f32[8,1024]{1,0:T(8,128)S(1)}, u32[]{:S(2)}, u32[]{:S(2)}) collective-permute-start(f32[8,1024]{1,0:T(8,128)S(1)} %shard_map.109.payload.refs_0_), channel_id=1, source_target_pairs={{0,4},{4,8},{8,12},{12,0},{1,5},{5,9},{9,13},{13,1},{2,6},{6,10},{... | collective-permute-start | bytes 98312 | tf_op jit(solution)/shard_map/ppermute | solution.py:378
  4.0 2.1 %collective-permute-start.1 = (f32[8,1024]{1,0:T(8,128)S(1)}, f32[8,1024]{1,0:T(8,128)S(1)}, u32[]{:S(2)}, u32[]{:S(2)}) collective-permute-start(f32[8,1024]{1,0:T(8,128)S(1)} %shard_map.109.payload.refs_0_), channel_id=1, source_target_pairs={{0,12},{4,0},{8,4},{12,8},{1,13},{5,1},{9,5},{13,9},{2,14},{6,2},{... | collective-permute-start | bytes 98312 | tf_op jit(solution)/shard_map/ppermute | solution.py:378
  6.1 0.9 %collective-permute-start = (f32[8,1024]{1,0:T(8,128)S(1)}, f32[8,1024]{1,0:T(8,128)S(1)}, u32[]{:S(2)}, u32[]{:S(2)}) collective-permute-start(f32[8,1024]{1,0:T(8,128)S(1)} %shard_map.109.payload.refs_0_), channel_id=1, source_target_pairs={{0,8},{4,12},{8,0},{12,4},{1,9},{5,13},{9,1},{13,5},{2,10},{6,14},... | collective-permute-start | bytes 98312 | tf_op jit(solution)/shard_map/ppermute | solution.py:378
  7.1 1.9 %shard_map.110.refs_4_ = f32[3,384,256]{2,1,0:T(8,128)S(1)} custom-call(f32[8,1024]{1,0:T(8,128)S(1)} %shard_map.109.payload.refs_0_), custom_call_target="tpu_custom_call" | custom-call | flops 1207959552 | bytes 1212416 | tf_op jit(solution)/shard_map/pallas_call | solution.py:364
  9.0 0.0 collective-permute-done.2.refs_3_
  9.0 0.0 collective-permute-done.1.refs_2_
  9.1 1.9 %collective-permute-done.refs_1_ = f32[8,1024]{1,0:T(8,128)S(1)} collective-permute-done((f32[8,1024]{1,0:T(8,128)S(1)}, f32[8,1024]{1,0:T(8,128)S(1)}, u32[]{:S(2)}, u32[]{:S(2)}) %collective-permute-start) | collective-permute-done | bytes 32800 | tf_op jit(solution)/shard_map/ppermute | solution.py:378
  11.0 0.0 copy-done
  11.0 0.0 copy-done.1
  11.0 0.1 shard_map.112
  11.0 2.2 %collective-permute-start.3 = (f32[16,8,256]{2,1,0:T(8,128)S(1)}, f32[16,8,256]{2,1,0:T(8,128)S(1)}, u32[]{:S(2)}, u32[]{:S(2)}) collective-permute-start(f32[16,8,256]{2,1,0:T(8,128)S(1)} %get-tuple-element.18), channel_id=1, source_target_pairs={{0,12},{4,0},{8,4},{12,8},{1,13},{5,1},{9,5},{13,9},{2,14},{6,2},{... | collective-permute-start | bytes 393224 | tf_op jit(solution)/shard_map/ppermute | solution.py:378
  13.3 0.0 collective-permute-start.4
  13.3 1.5 %collective-permute-start.5 = (f32[32,8,256]{2,1,0:T(8,128)S(1)}, f32[32,8,256]{2,1,0:T(8,128)S(1)}, u32[]{:S(2)}, u32[]{:S(2)}) collective-permute-start(f32[32,8,256]{2,1,0:T(8,128)S(1)} %get-tuple-element.20), channel_id=1, source_target_pairs={{0,2},{2,0},{1,3},{3,1},{4,6},{6,4},{5,7},{7,5},{8,10},{10,8},{9,1... | collective-permute-start | bytes 786440 | tf_op jit(solution)/shard_map/ppermute | solution.py:384
  14.8 5.2 %shard_map.111.refs_0_ = f32[3,384,256]{2,1,0:T(8,128)S(1)} custom-call(f32[8,1024]{1,0:T(8,128)S(1)} %shard_map.109.payload.refs_0_, f32[8,1024]{1,0:T(8,128)S(1)} %collective-permute-done.refs_1_, f32[8,1024]{1,0:T(8,128)S(1)} %collective-permute-done.1.refs_2_, f32[8,1024]{1,0:T(8,128)S(1)} %collective-permute-done.2.refs_3_, ...), custom_call_target="tpu_custom_call", output_to_operand_aliasing={{}: (4, {})} | custom-call | flops 3623878656 | bytes 2490368 | tf_op jit(solution)/shard_map/pallas_call | solution.py:364
  19.9 0.0 collective-permute-done.3.upper.refs_3_
  20.0 0.1 collective-permute-done.4.lower.refs_4_
  20.1 1.5 %collective-permute-start.6 = (f32[4,16,256]{2,1,0:T(8,128)S(1)}, f32[4,16,256]{2,1,0:T(8,128)S(1)}, u32[]{:S(2)}, u32[]{:S(2)}) collective-permute-start(f32[4,16,256]{2,1,0:T(8,128)S(1)} %shard_map.114), channel_id=1, source_target_pairs={{0,2},{2,0},{1,3},{3,1},{4,6},{6,4},{5,7},{7,5},{8,10},{10,8},{9,1... | collective-permute-start | bytes 196616 | tf_op jit(solution)/shard_map/ppermute | solution.py:384
  21.5 0.0 collective-permute-done.5.refs_0_.refs_6_
  21.5 2.9 %shard_map.113.refs_5_ = f32[3,96,256]{2,1,0:T(8,128)S(1)} custom-call(f32[32,8,256]{2,1,0:T(8,128)S(1)} %collective-permute-done.5.refs_0_.refs_6_), custom_call_target="tpu_custom_call" | custom-call | flops 1207959552 | bytes 557056 | tf_op jit(solution)/shard_map/pallas_call | solution.py:364
  24.5 0.0 collective-permute-done.6.refs_7_
  24.5 0.5 %shard_map.115 = (f32[3,20,24,256]{3,2,1,0:T(8,128)S(1)}, f32[20,24,256]{2,1,0:T(8,128)S(1)}, f32[15,8,128]{2,1,0:T(8,128)S(1)}) custom-call(f32[3,384,256]{2,1,0:T(8,128)S(1)} %shard_map.111.refs_0_, f32[16,16,256]{2,1,0:T(8,128)S(1)} %copy-done, f32[16,16,256]{2,1,0:T(8,128)S(1)} %copy-done.1, f32[16,8,256]{2,1,0:T(8,128)S(1)} %collective-permute-done.3.upper.refs_3_, ...), custom_call_target="tpu_custom_call" | custom-call | flops 1000 | bytes 4616192 | tf_op jit(solution)/shard_map/pallas_call | solution.py:364
  25.0 0.1 collective-permute-start.7
  25.1 1.2 %shard_map.116 = (f32[20,24,256]{2,1,0:T(8,128)S(1)}, f32[20,24,256]{2,1,0:T(8,128)S(1)}, f32[20,24,256]{2,1,0:T(8,128)S(1)}, f32[20,24,256]{2,1,0:T(8,128)S(1)}...) custom-call(f32[20,24,256]{2,1,0:T(8,128)S(1)} %get-tuple-element.22.kappa_ext), custom_call_target="tpu_custom_call" | custom-call | flops 3686400 | bytes 3932160 | tf_op jit(solution)/shard_map/pallas_call | solution.py:364
  26.3 0.0 collective-permute-done.7.face
  26.3 8.5 %shard_map.117 = f32[3,16,16,256]{3,2,1,0:T(8,128)} custom-call(f32[3,20,24,256]{3,2,1,0:T(8,128)S(1)} %get-tuple-element.21.source, f32[20,24,256]{2,1,0:T(8,128)S(1)} %get-tuple-element.23.root, f32[20,24,256]{2,1,0:T(8,128)S(1)} %get-tuple-element.24.ax, f32[20,24,256]{2,1,0:T(8,128)S(1)} %get-tuple-element.25.ay, ...), custom_call_target="tpu_custom_call" | custom-call | flops 22118400 | bytes 5763072 | tf_op jit(solution)/shard_map/pallas_call | solution.py:364
  (1 shorter events, 0.0 us)
Async XLA Ops:
  0.9 10.0 %copy-start = (f32[16,16,256]{2,1,0:T(8,128)S(1)}, f32[16,16,256]{2,1,0:T(8,128)}, u32[]{:S(2)}) copy-start(f32[16,16,256]{2,1,0:T(8,128)} %refs_1_.3) | copy-start | bytes 786436
  1.0 10.0 %copy-start.1 = (f32[16,16,256]{2,1,0:T(8,128)S(1)}, f32[16,16,256]{2,1,0:T(8,128)}, u32[]{:S(2)}) copy-start(f32[16,16,256]{2,1,0:T(8,128)} %refs_2_.3) | copy-start | bytes 786436
  1.0 8.1 %collective-permute-start.2 = (f32[8,1024]{1,0:T(8,128)S(1)}, f32[8,1024]{1,0:T(8,128)S(1)}, u32[]{:S(2)}, u32[]{:S(2)}) collective-permute-start(f32[8,1024]{1,0:T(8,128)S(1)} %shard_map.109.payload.refs_0_), channel_id=1, source_target_pairs={{0,4},{4,8},{8,12},{12,0},{1,5},{5,9},{9,13},{13,1},{2,6},{6,10},{... | collective-permute-start | bytes 98312 | tf_op jit(solution)/shard_map/ppermute | solution.py:378
  4.0 5.0 %collective-permute-start.1 = (f32[8,1024]{1,0:T(8,128)S(1)}, f32[8,1024]{1,0:T(8,128)S(1)}, u32[]{:S(2)}, u32[]{:S(2)}) collective-permute-start(f32[8,1024]{1,0:T(8,128)S(1)} %shard_map.109.payload.refs_0_), channel_id=1, source_target_pairs={{0,12},{4,0},{8,4},{12,8},{1,13},{5,1},{9,5},{13,9},{2,14},{6,2},{... | collective-permute-start | bytes 98312 | tf_op jit(solution)/shard_map/ppermute | solution.py:378
  6.1 4.8 %collective-permute-start = (f32[8,1024]{1,0:T(8,128)S(1)}, f32[8,1024]{1,0:T(8,128)S(1)}, u32[]{:S(2)}, u32[]{:S(2)}) collective-permute-start(f32[8,1024]{1,0:T(8,128)S(1)} %shard_map.109.payload.refs_0_), channel_id=1, source_target_pairs={{0,8},{4,12},{8,0},{12,4},{1,9},{5,13},{9,1},{13,5},{2,10},{6,14},... | collective-permute-start | bytes 98312 | tf_op jit(solution)/shard_map/ppermute | solution.py:378
  11.0 8.9 %collective-permute-start.3 = (f32[16,8,256]{2,1,0:T(8,128)S(1)}, f32[16,8,256]{2,1,0:T(8,128)S(1)}, u32[]{:S(2)}, u32[]{:S(2)}) collective-permute-start(f32[16,8,256]{2,1,0:T(8,128)S(1)} %get-tuple-element.18), channel_id=1, source_target_pairs={{0,12},{4,0},{8,4},{12,8},{1,13},{5,1},{9,5},{13,9},{2,14},{6,2},{... | collective-permute-start | bytes 393224 | tf_op jit(solution)/shard_map/ppermute | solution.py:378
  13.3 6.8 %collective-permute-start.4 = (f32[16,8,256]{2,1,0:T(8,128)S(1)}, f32[16,8,256]{2,1,0:T(8,128)S(1)}, u32[]{:S(2)}, u32[]{:S(2)}) collective-permute-start(f32[16,8,256]{2,1,0:T(8,128)S(1)} %get-tuple-element.19), channel_id=1, source_target_pairs={{0,4},{4,8},{8,12},{12,0},{1,5},{5,9},{9,13},{13,1},{2,6},{6,10},{... | collective-permute-start | bytes 393224 | tf_op jit(solution)/shard_map/ppermute | solution.py:378
  13.3 8.3 %collective-permute-start.5 = (f32[32,8,256]{2,1,0:T(8,128)S(1)}, f32[32,8,256]{2,1,0:T(8,128)S(1)}, u32[]{:S(2)}, u32[]{:S(2)}) collective-permute-start(f32[32,8,256]{2,1,0:T(8,128)S(1)} %get-tuple-element.20), channel_id=1, source_target_pairs={{0,2},{2,0},{1,3},{3,1},{4,6},{6,4},{5,7},{7,5},{8,10},{10,8},{9,1... | collective-permute-start | bytes 786440 | tf_op jit(solution)/shard_map/ppermute | solution.py:384
  20.1 4.4 %collective-permute-start.6 = (f32[4,16,256]{2,1,0:T(8,128)S(1)}, f32[4,16,256]{2,1,0:T(8,128)S(1)}, u32[]{:S(2)}, u32[]{:S(2)}) collective-permute-start(f32[4,16,256]{2,1,0:T(8,128)S(1)} %shard_map.114), channel_id=1, source_target_pairs={{0,2},{2,0},{1,3},{3,1},{4,6},{6,4},{5,7},{7,5},{8,10},{10,8},{9,1... | collective-permute-start | bytes 196616 | tf_op jit(solution)/shard_map/ppermute | solution.py:384
  25.0 1.3 %collective-permute-start.7 = (f32[15,8,128]{2,1,0:T(8,128)S(1)}, f32[15,8,128]{2,1,0:T(8,128)S(1)}, u32[]{:S(2)}, u32[]{:S(2)}) collective-permute-start(f32[15,8,128]{2,1,0:T(8,128)S(1)} %get-tuple-element.30), channel_id=1, source_target_pairs={{0,1},{1,0},{2,3},{3,2},{4,5},{5,4},{6,7},{7,6},{8,9},{9,8},{10,11... | collective-permute-start | bytes 184328 | tf_op jit(solution)/shard_map/ppermute | solution.py:492

commit v5 on v4

--- a/solution.py
+++ b/solution.py
@@ -12,6 +12,7 @@
 HALO = 4
 BF16 = jnp.bfloat16
 F32 = jnp.float32
+F8 = jnp.float8_e4m3fn
 CONTRACT_LANES = (((1,), (1,)), ((), ()))
 
 
@@ -30,9 +31,18 @@
 
 
 def pack_kernel(*refs):
-    sources, payload, held, sems = refs[:9], refs[9], refs[10:19], refs[19]
-    copies = [pltpu.make_async_copy(a, b, sems.at[i]) for i, (a, b) in enumerate(zip(sources, held))]
-    for copy in copies:
+    sources, (payload, *fields), held, sems = refs[:11], refs[11:14], refs[14:23], refs[23]
+    copies = [pltpu.make_async_copy(a, b, sems.at[i]) for i, (a, b) in enumerate(zip(sources[:9], held))]
+    pieces = (sems.shape[0] - 9) // 2
+    step = fields[0].shape[0] // pieces
+    slow = [
+        pltpu.make_async_copy(
+            a.at[pl.ds(k * step, step)], b.at[pl.ds(k * step, step)], sems.at[9 + n * pieces + k]
+        )
+        for n, (a, b) in enumerate(zip(sources[9:], fields))
+        for k in range(pieces)
+    ]
+    for copy in copies + slow:
         copy.start()
     for copy in copies:
         copy.wait()
@@ -53,6 +63,8 @@
     ]
     for r, row in enumerate(rows):
         payload[r : r + 1, :] = row
+    for copy in slow:
+        copy.wait()
 
 
 def edges(sides, size_x):
@@ -74,7 +86,7 @@
     return jnp.where(row < 0, -1, (x - start_x) * (size_y + 2 * HALO) + row), cell % size_z
 
 
-def spread(payload_of, spans, sources, near, out, start_x, planes, size_y, size_z, first, unroll=False):
+def spread_points(payload_of, near, out, start_x, planes, size_y, size_z, first):
     ext_y = size_y + 2 * HALO
     height = planes * ext_y
     points = payload_of(0).shape[1] // 4
@@ -104,6 +116,9 @@
         both += by_low[c * height : (c + 1) * height]
         out[c] = both if first is None else first[c] + both
 
+
+def spread_gates(payload_of, spans, sources, out, start_x, planes, size_y, size_z, unroll=False):
+    height = planes * (size_y + 2 * HALO)
     gates = payload_of(0).shape[1]
     row_id = lax.broadcasted_iota(jnp.int32, (height, gates), 0)
     z_id = lax.broadcasted_iota(jnp.int32, (size_z, gates), 0)
@@ -112,12 +127,21 @@
         one = payload_of(j)
         line, z = lines_of(one, spans, start_x, size_y, size_z)
         pick = jnp.where(row_id == line, 1.0, 0.0).astype(BF16)
-        pick_z = jnp.where(z_id == z, 1.0, 0.0).astype(BF16)
-        parts = [part for c in range(3) for part in two_parts(one[c : c + 1, :])]
-        sums = dot_lanes(jnp.concatenate([pick * part for part in parts], axis=0), pick_z)
+        there = jnp.where(z_id == z, 1.0, 0.0).astype(BF16)
+        high, low = zip(*[two_parts(one[c : c + 1, :]) for c in range(3)])
+        if height <= 128:
+            sums = dot_lanes(jnp.concatenate([pick * part for part in high + low], axis=0), there)
+            for c in range(3):
+                more = sums[(c + 3) * height : (c + 4) * height]
+                out[c] += sums[c * height : (c + 1) * height] + more
+            return carry
+        scale = [256.0 / jnp.maximum(jnp.max(jnp.abs(part.astype(F32)), axis=1, keepdims=True), 1e-30) for part in low]
+        low = [(pick * (part.astype(F32) * by).astype(BF16)).astype(F8) for part, by in zip(low, scale)]
+        sums = dot_lanes(jnp.concatenate([pick * part for part in high], axis=0), there)
+        rest = dot_lanes(jnp.concatenate(low, axis=0), there.astype(F8))
         for c in range(3):
-            high = 2 * c * height
-            out[c] += sums[high : high + height] + sums[high + height : high + 2 * height]
+            lines = slice(c * height, (c + 1) * height)
+            out[c] += sums[lines] + rest[lines] * (1.0 / scale[c])
         return carry
 
     if unroll:
@@ -133,7 +157,8 @@
 
 def first_kernel(spans, dims, payload, out):
     size_x, size_y, size_z = dims
-    spread(lambda j: payload, spans, (0, 1), near_of(spans)[:1], out, 0, size_x, size_y, size_z, None, unroll=True)
+    spread_points(lambda j: payload, near_of(spans)[:1], out, 0, size_x, size_y, size_z, None)
+    spread_gates(lambda j: payload, spans, (0, 1), out, 0, size_x, size_y, size_z, unroll=True)
 
 
 def payload_in(refs, j):
@@ -142,13 +167,18 @@
 
 def second_kernel(spans, dims, count, *refs):
     payloads, (first, out) = refs[:count], refs[count:]
-    size_x, size_y, size_z = dims
-    near = near_of(spans)[1:]
-    spread(lambda j: payload_in(payloads, j), spans, (1, spans), near, out, 0, size_x, size_y, size_z, first, unroll=count > 1)
+    for c in range(3):
+        out[c] = first[c]
+    spread_gates(lambda j: payload_in(payloads, j), spans, (1, spans), out, 0, *dims, unroll=count > 1)
+
+
+def third_kernel(spans, dims, count, *refs):
+    payloads, second, out = refs[:count], refs[count], refs[-1]
+    spread_points(lambda j: payload_in(payloads, j), near_of(spans)[1:], out, 0, *dims, second)
 
 
 def gather_kernel(spans, sides, count, *refs):
-    payloads, (kappa, sigma, to_upper, to_lower), outs = refs[:count], refs[count : count + 4], refs[count + 4 :]
+    payloads, (kappa, sigma), outs = refs[:count], refs[count : count + 2], refs[count + 2 :]
     size_x, size_y, size_z = kappa.shape
     for out, start in zip(outs, edges(sides, size_x)):
         each = payloads[0].shape[-1] // size_z
@@ -161,6 +191,9 @@
                 plane = field[start + i]
                 for part in range(size_y // 8):
                     out[spans * each + (2 * i + k) * (size_y // 8) + part] = plane[8 * part : 8 * part + 8]
+
+def slab_kernel(kappa, sigma, to_upper, to_lower):
+    size_y = kappa.shape[1]
     to_upper[:, 0:HALO] = kappa[:, size_y - HALO :]
     to_upper[:, HALO:] = sigma[:, size_y - HALO :]
     to_lower[:, 0:HALO] = kappa[:, 0:HALO]
@@ -183,7 +216,8 @@
         def payload_of(j, packed=packed, each=each):
             return jnp.concatenate([packed[j * each + part] for part in range(each)], axis=1)
 
-        spread(payload_of, spans, (0, spans), near_of(spans), strip, start, HALO, size_y, size_z, None)
+        spread_points(payload_of, near_of(spans), strip, start, HALO, size_y, size_z, None)
+        spread_gates(payload_of, spans, (0, spans), strip, start, HALO, size_y, size_z, unroll=spans == 4)
 
 
 def extend_kernel(sides, *refs):
@@ -238,7 +272,7 @@
     )
 
 
-def each_plane(count, step, unroll=4):
+def each_plane(count, step, unroll=8):
     whole = count // unroll * unroll
     lax.fori_loop(0, whole, lambda i, carry: (step(i), carry)[1], 0, unroll=unroll)
     for i in range(whole, count):
@@ -278,7 +312,7 @@
 
 
 def diffuse_kernel(sides, source, root, ax, ay, aym, az, azm, keep, face, out, *scratch):
-    ping, pong, halo, root_h, ax_h, ay_h, aym_h, az_all, azm_all, keep_all = scratch
+    ping, pong, halo, root_h, ax_h, ay_h, aym_h, az_all, azm_all, keep_all, done, sems = scratch
     planes, ext_y, size_z = root.shape
     size_x, size_y = out.shape[1], out.shape[2]
     ext_z = size_z + 128
@@ -333,7 +367,7 @@
     for p in range(PASSES):
         deep = PASSES - 1 - p
         old, new = (ping, pong) if p % 2 == 0 else (pong, ping)
-        first = jnp.where(stream == 0, 0, planes - deep) if sides == 1 else planes - deep
+        first = (jnp.where(stream == 0, 0, planes - deep) if sides == 1 else planes - deep) if deep else 0
 
         def value_of(c, x, old=old, p=p):
             return wide(source[c, x], halo[c, x]) if p == 0 else old[c, x]
@@ -351,21 +385,31 @@
                 moved += wide(aym[x], aym_h[x]) * pltpu.roll(value, 1, 0)
                 moved += az_all[x] * lanes_on(value, -1, lane) + azm_all[x] * lanes_on(value, 1, lane)
                 if p == PASSES - 1:
-                    out[c, x] = moved[0:size_y, 0:size_z]
+                    done[c, x] = moved[0:size_y, 0:size_z]
                 else:
                     new[c, x] = moved
 
-        each_plane(size_x + sides * deep, one_plane)
-
-
-def call(kernel, outs, scratch, flops, *args, left=(), aliases=(), room=8):
+        if p < PASSES - 1:
+            each_plane(size_x + sides * deep, one_plane)
+    step = size_x // sems.shape[0]
+    copies = []
+    for k in range(sems.shape[0]):
+        each_plane(step, lambda i, k=k: one_plane(i + k * step))
+        part = pl.ds(k * step, step)
+        copies.append(pltpu.make_async_copy(done.at[:, part], out.at[:, part], sems.at[k]))
+        copies[-1].start()
+    for copy in copies:
+        copy.wait()
+
+
+def call(kernel, outs, scratch, flops, *args, left=(), aliases=(), room=8, far=False):
     moved = sum(4 * a.size for a in args) + sum(4 * o.size for o in outs)
     spaces = [pltpu.HBM if i in left else pltpu.VMEM for i in range(len(args))]
     return pl.pallas_call(
         kernel,
         out_shape=outs,
         in_specs=[pl.BlockSpec(memory_space=space) for space in spaces],
-        out_specs=[pl.BlockSpec(memory_space=pltpu.VMEM)] * len(outs),
+        out_specs=[pl.BlockSpec(memory_space=pltpu.HBM if far else pltpu.VMEM)] * len(outs),
         scratch_shapes=scratch,
         input_output_aliases=dict(aliases),
         compiler_params=pltpu.CompilerParams(vmem_limit_bytes=room * 1024 * 1024),
@@ -417,11 +461,13 @@
         point_x,
         point_y,
         point_z,
+        kappa,
+        sigma,
     ]
-    (payload,) = call(
+    payload, kappa, sigma = call(
         pack_kernel,
-        [shape(8, gates)],
-        [pltpu.VMEM(a.shape, a.dtype) for a in inputs] + [pltpu.SemaphoreType.DMA((len(inputs),))],
+        [shape(8, gates)] + [shape(size_x, size_y, size_z)] * 2,
+        [pltpu.VMEM(a.shape, a.dtype) for a in inputs[:9]] + [pltpu.SemaphoreType.DMA((9 + 2 * 4,))],
         1000,
         *[pltpu.with_memory_space_constraint(a, pltpu.HBM) for a in inputs],
         left=range(len(inputs)),
@@ -435,9 +481,10 @@
     planes = shape(3, size_x * ext_y, size_z)
     (own,) = call(functools.partial(first_kernel, spans, dims), [planes], [], work, payload, room=24)
     parts = spans * gates // size_z + HALO * 2 * size_y // 8
-    to_upper, to_lower, *others = call(
+    to_upper, to_lower = call(slab_kernel, [shape(size_x, 2 * HALO, size_z)] * 2, [], 1000, kappa, sigma)
+    others = call(
         functools.partial(gather_kernel, spans, sides, len(payloads)),
-        [shape(size_x, 2 * HALO, size_z)] * 2 + [shape(parts, 8, size_z)] * sides,
+        [shape(parts, 8, size_z)] * sides,
         [],
         1000,
         *payloads,
@@ -456,16 +503,26 @@
         aliases=((len(payloads), 0),),
         room=24,
     )
-    corners = across_bands(
-        call(
-            functools.partial(corner_kernel, sides),
-            [shape(HALO, 4 * HALO, size_z)] * sides,
-            [],
-            1000,
-            from_upper,
-            from_lower,
-        )
-    )
+    corners = call(
+        functools.partial(corner_kernel, sides),
+        [shape(HALO, 4 * HALO, size_z)] * sides,
+        [],
+        1000,
+        from_upper,
+        from_lower,
+    )
+    (own,) = call(
+        functools.partial(third_kernel, spans, dims, len(payloads)),
+        [planes],
+        [],
+        work // 4,
+        *payloads,
+        own,
+        *corners,
+        aliases=((len(payloads), 0),),
+        room=24,
+    )
+    corners = across_bands(corners)
     strips = call(
         functools.partial(strip_kernel, spans, sides, dims),
         [shape(3, HALO * ext_y, size_z)] * sides,
@@ -494,16 +551,17 @@
     coefficients = call(
         functools.partial(coefficient_kernel, sides, size_x), [shape(*main)] * 7, [], 30 * ext_x * ext_y * size_z, kappa_ext
     )
-    scratch = [(3, *wide)] * 2 + [(3, *beside)] + [beside] * 4 + [wide] * 3
+    scratch = [(3, *wide)] * 2 + [(3, *beside)] + [beside] * 4 + [wide] * 3 + [(3, size_x, size_y, size_z)]
     (field,) = call(
         functools.partial(diffuse_kernel, sides),
         [shape(3, size_x, size_y, size_z)],
-        [pltpu.VMEM(dims, F32) for dims in scratch],
+        [pltpu.VMEM(dims, F32) for dims in scratch] + [pltpu.SemaphoreType.DMA((4,))],
         60 * 3 * ext_x * ext_y * size_z,
         source,
         *coefficients,
         face,
         room=20,
+        far=True,
     )
     return field
 

time: 35.1 us -> 31.3 us (0.89)
  Pallas kernels: 21.3 us -> 19.1 us
  waiting for transfers between devices: 2 us -> 0.55 us
    pallas_call x9 -> x11, Pallas kernels: 21.3 us -> 19.1 us  [call(): pl.pallas_call(kernel, out_shape=outs, in_specs=[pl.BlockSpec(memory_spac...]
    ppermute x5, waiting for transfers between devices: 1.99 us -> 0.36 us  [ring(): lax.ppermute(array, 'span', [(i, (i + step) % count) for i in range(count)])]
  transfers between devices with their start and end apart: 8 -> 8, of which waited for: 2 -> 2; matrix products, arithmetic and copies ran while one was open for 0% -> 0% of each run, Pallas kernels for 32% -> 30%
where the time goes in v5:
time: 31.3 us; the launch traced here: 31.1 us
  Pallas kernels  19.1 us (61%)
  starting transfers between devices  11.1 us (35%)
  waiting for transfers between devices  0.55 us (2%)
    pallas_call x11, Pallas kernels, call(): pl.pallas_call(kernel, out_shape=outs, in_specs=[pl.BlockSpec(memory_spac...  19.1 us
    ppermute x5, starting transfers between devices, ring(): lax.ppermute(array, 'span', [(i, (i + step) % count) for i in range(count)])  8.19 us
    ppermute x2, starting transfers between devices, across_bands(): return [lax.ppermute(arrays[0], 'stream', [(0, 1), (1, 0)])]  2.88 us
  transfers between devices with their start and end apart: 8, of which 2 were waited for; matrix products, arithmetic and copies ran while one was open for 0% of the time, Pallas kernels for 30%

profile of v5, /device:TPU:0, one launch (start us, length us, event | category | flops | bytes accessed | tf_op | source)
XLA Modules:
  0.0 31.1 jit_solution(12986337213377766677)
XLA Ops:
  0.0 1.3 %shard_map.109 = (f32[8,1024]{1,0:T(8,128)S(1)}, f32[16,16,256]{2,1,0:T(8,128)S(1)}, f32[16,16,256]{2,1,0:T(8,128)S(1)}) custom-call(f32[1,1,1024]{2,1,0:T(1,128)} %refs_0_.1, f32[1,1,1024]{2,1,0:T(1,128)} %refs_1_.1, f32[1,1,1024]{2,1,0:T(1,128)} %refs_2_.1, s32[1,1024]{1,0:T(1,128)} %bitcast.1, s32[1,1,1024]{2,1,0:T(1,128)} %refs_4_.1, ...), custom_call_target="tpu_custom_call" | custom-call | flops 1000 | bytes 1107968 | tf_op jit(solution)/shard_map/pallas_call | solution.py:408
  1.3 3.1 %collective-permute-start.2 = (f32[8,1024]{1,0:T(8,128)S(1)}, f32[8,1024]{1,0:T(8,128)S(1)}, u32[]{:S(2)}, u32[]{:S(2)}) collective-permute-start(f32[8,1024]{1,0:T(8,128)S(1)} %get-tuple-element.20.payload.refs_0_), channel_id=1, source_target_pairs={{0,4},{4,8},{8,12},{12,0},{1,5},{5,9},{9,13},{13,1},{2,6},{6,10},{... | collective-permute-start | bytes 98312 | tf_op jit(solution)/shard_map/ppermute | solution.py:422
  4.4 2.1 %collective-permute-start.1 = (f32[8,1024]{1,0:T(8,128)S(1)}, f32[8,1024]{1,0:T(8,128)S(1)}, u32[]{:S(2)}, u32[]{:S(2)}) collective-permute-start(f32[8,1024]{1,0:T(8,128)S(1)} %get-tuple-element.20.payload.refs_0_), channel_id=1, source_target_pairs={{0,12},{4,0},{8,4},{12,8},{1,13},{5,1},{9,5},{13,9},{2,14},{6,2},{... | collective-permute-start | bytes 98312 | tf_op jit(solution)/shard_map/ppermute | solution.py:422
  6.5 0.9 %collective-permute-start = (f32[8,1024]{1,0:T(8,128)S(1)}, f32[8,1024]{1,0:T(8,128)S(1)}, u32[]{:S(2)}, u32[]{:S(2)}) collective-permute-start(f32[8,1024]{1,0:T(8,128)S(1)} %get-tuple-element.20.payload.refs_0_), channel_id=1, source_target_pairs={{0,8},{4,12},{8,0},{12,4},{1,9},{5,13},{9,1},{13,5},{2,10},{6,14},... | collective-permute-start | bytes 98312 | tf_op jit(solution)/shard_map/ppermute | solution.py:422
  7.5 0.1 shard_map.112
  7.5 1.4 %collective-permute-start.3 = (f32[16,8,256]{2,1,0:T(8,128)S(1)}, f32[16,8,256]{2,1,0:T(8,128)S(1)}, u32[]{:S(2)}, u32[]{:S(2)}) collective-permute-start(f32[16,8,256]{2,1,0:T(8,128)S(1)} %get-tuple-element.23), channel_id=1, source_target_pairs={{0,12},{4,0},{8,4},{12,8},{1,13},{5,1},{9,5},{13,9},{2,14},{6,2},{... | collective-permute-start | bytes 393224 | tf_op jit(solution)/shard_map/ppermute | solution.py:422
  8.9 0.7 %collective-permute-start.4 = (f32[16,8,256]{2,1,0:T(8,128)S(1)}, f32[16,8,256]{2,1,0:T(8,128)S(1)}, u32[]{:S(2)}, u32[]{:S(2)}) collective-permute-start(f32[16,8,256]{2,1,0:T(8,128)S(1)} %get-tuple-element.24), channel_id=1, source_target_pairs={{0,4},{4,8},{8,12},{12,0},{1,5},{5,9},{9,13},{13,1},{2,6},{6,10},{... | collective-permute-start | bytes 393224 | tf_op jit(solution)/shard_map/ppermute | solution.py:422
  9.6 1.7 %shard_map.110.refs_4_ = f32[3,384,256]{2,1,0:T(8,128)S(1)} custom-call(f32[8,1024]{1,0:T(8,128)S(1)} %get-tuple-element.20.payload.refs_0_), custom_call_target="tpu_custom_call" | custom-call | flops 1207959552 | bytes 1212416 | tf_op jit(solution)/shard_map/pallas_call | solution.py:408
  11.3 0.0 collective-permute-done.2.refs_3_
  11.3 0.0 collective-permute-done.1.refs_2_
  11.3 0.3 %collective-permute-done.refs_1_ = f32[8,1024]{1,0:T(8,128)S(1)} collective-permute-done((f32[8,1024]{1,0:T(8,128)S(1)}, f32[8,1024]{1,0:T(8,128)S(1)}, u32[]{:S(2)}, u32[]{:S(2)}) %collective-permute-start) | collective-permute-done | bytes 32800 | tf_op jit(solution)/shard_map/ppermute | solution.py:422
  11.7 1.7 %collective-permute-start.5 = (f32[32,8,256]{2,1,0:T(8,128)S(1)}, f32[32,8,256]{2,1,0:T(8,128)S(1)}, u32[]{:S(2)}, u32[]{:S(2)}) collective-permute-start(f32[32,8,256]{2,1,0:T(8,128)S(1)} %shard_map.115), channel_id=1, source_target_pairs={{0,2},{2,0},{1,3},{3,1},{4,6},{6,4},{5,7},{7,5},{8,10},{10,8},{9,1... | collective-permute-start | bytes 786440 | tf_op jit(solution)/shard_map/ppermute | solution.py:428
  13.4 3.4 %shard_map.111.refs_4_ = f32[3,384,256]{2,1,0:T(8,128)S(1)} custom-call(f32[8,1024]{1,0:T(8,128)S(1)} %get-tuple-element.20.payload.refs_0_, f32[8,1024]{1,0:T(8,128)S(1)} %collective-permute-done.refs_1_, f32[8,1024]{1,0:T(8,128)S(1)} %collective-permute-done.1.refs_2_, ...), custom_call_target="tpu_custom_call", output_to_operand_aliasing={{}: (4, {})} | custom-call | flops 3623878656 | bytes 2490368 | tf_op jit(solution)/shard_map/pallas_call | solution.py:408
  16.8 0.0 collective-permute-done.3.upper.refs_3_
  16.8 0.0 collective-permute-done.4.lower.refs_4_
  16.8 1.1 %collective-permute-start.6 = (f32[4,16,256]{2,1,0:T(8,128)S(1)}, f32[4,16,256]{2,1,0:T(8,128)S(1)}, u32[]{:S(2)}, u32[]{:S(2)}) collective-permute-start(f32[4,16,256]{2,1,0:T(8,128)S(1)} %shard_map.113.refs_5_), channel_id=1, source_target_pairs={{0,2},{2,0},{1,3},{3,1},{4,6},{6,4},{5,7},{7,5},{8,10},{10,8},{9,1... | collective-permute-start | bytes 196616 | tf_op jit(solution)/shard_map/ppermute | solution.py:428
  18.0 1.3 %shard_map.114.refs_0_ = f32[3,384,256]{2,1,0:T(8,128)S(1)} custom-call(f32[8,1024]{1,0:T(8,128)S(1)} %get-tuple-element.20.payload.refs_0_, f32[8,1024]{1,0:T(8,128)S(1)} %collective-permute-done.refs_1_, f32[8,1024]{1,0:T(8,128)S(1)} %collective-permute-done.1.refs_2_, ...), custom_call_target="tpu_custom_call", output_to_operand_aliasing={{}: (4, {})} | custom-call | flops 301989888 | bytes 2555904 | tf_op jit(solution)/shard_map/pallas_call | solution.py:408
  19.3 0.0 collective-permute-done.5.refs_0_.refs_6_
  19.3 1.9 %shard_map.116.refs_5_ = f32[3,96,256]{2,1,0:T(8,128)S(1)} custom-call(f32[32,8,256]{2,1,0:T(8,128)S(1)} %collective-permute-done.5.refs_0_.refs_6_), custom_call_target="tpu_custom_call" | custom-call | flops 1207959552 | bytes 557056 | tf_op jit(solution)/shard_map/pallas_call | solution.py:408
  21.2 0.0 collective-permute-done.6.refs_7_
  21.2 0.5 %shard_map.117 = (f32[3,20,24,256]{3,2,1,0:T(8,128)S(1)}, f32[20,24,256]{2,1,0:T(8,128)S(1)}, f32[15,8,128]{2,1,0:T(8,128)S(1)}) custom-call(f32[3,384,256]{2,1,0:T(8,128)S(1)} %shard_map.114.refs_0_, f32[16,16,256]{2,1,0:T(8,128)S(1)} %get-tuple-element.21.kappa.refs_4_.refs_1_, f32[16,16,256]{2,1,0:T(8,128)S(1)} %get-tuple-element.22.sigma.refs_5_.refs_2_, ...), custom_call_target="tpu_custom_call" | custom-call | flops 1000 | bytes 4616192 | tf_op jit(solution)/shard_map/pallas_call | solution.py:408
  21.8 0.1 collective-permute-start.7
  21.8 1.0 %shard_map.118 = (f32[20,24,256]{2,1,0:T(8,128)S(1)}, f32[20,24,256]{2,1,0:T(8,128)S(1)}, f32[20,24,256]{2,1,0:T(8,128)S(1)}, f32[20,24,256]{2,1,0:T(8,128)S(1)}...) custom-call(f32[20,24,256]{2,1,0:T(8,128)S(1)} %get-tuple-element.26.kappa_ext), custom_call_target="tpu_custom_call" | custom-call | flops 3686400 | bytes 3932160 | tf_op jit(solution)/shard_map/pallas_call | solution.py:408
  22.9 0.2 collective-permute-done.7.face
  23.1 7.9 %shard_map.119 = f32[3,16,16,256]{3,2,1,0:T(8,128)} custom-call(f32[3,20,24,256]{3,2,1,0:T(8,128)S(1)} %get-tuple-element.25.source, f32[20,24,256]{2,1,0:T(8,128)S(1)} %get-tuple-element.27.root, f32[20,24,256]{2,1,0:T(8,128)S(1)} %get-tuple-element.28.ax, f32[20,24,256]{2,1,0:T(8,128)S(1)} %get-tuple-element.29.ay, ...), custom_call_target="tpu_custom_call" | custom-call | flops 22118400 | bytes 5763072 | tf_op jit(solution)/shard_map/pallas_call | solution.py:408
  (2 shorter events, 0.0 us)
Async XLA Ops:
  1.3 9.9 %collective-permute-start.2 = (f32[8,1024]{1,0:T(8,128)S(1)}, f32[8,1024]{1,0:T(8,128)S(1)}, u32[]{:S(2)}, u32[]{:S(2)}) collective-permute-start(f32[8,1024]{1,0:T(8,128)S(1)} %get-tuple-element.20.payload.refs_0_), channel_id=1, source_target_pairs={{0,4},{4,8},{8,12},{12,0},{1,5},{5,9},{9,13},{13,1},{2,6},{6,10},{... | collective-permute-start | bytes 98312 | tf_op jit(solution)/shard_map/ppermute | solution.py:422
  4.4 6.9 %collective-permute-start.1 = (f32[8,1024]{1,0:T(8,128)S(1)}, f32[8,1024]{1,0:T(8,128)S(1)}, u32[]{:S(2)}, u32[]{:S(2)}) collective-permute-start(f32[8,1024]{1,0:T(8,128)S(1)} %get-tuple-element.20.payload.refs_0_), channel_id=1, source_target_pairs={{0,12},{4,0},{8,4},{12,8},{1,13},{5,1},{9,5},{13,9},{2,14},{6,2},{... | collective-permute-start | bytes 98312 | tf_op jit(solution)/shard_map/ppermute | solution.py:422
  6.5 5.1 %collective-permute-start = (f32[8,1024]{1,0:T(8,128)S(1)}, f32[8,1024]{1,0:T(8,128)S(1)}, u32[]{:S(2)}, u32[]{:S(2)}) collective-permute-start(f32[8,1024]{1,0:T(8,128)S(1)} %get-tuple-element.20.payload.refs_0_), channel_id=1, source_target_pairs={{0,8},{4,12},{8,0},{12,4},{1,9},{5,13},{9,1},{13,5},{2,10},{6,14},... | collective-permute-start | bytes 98312 | tf_op jit(solution)/shard_map/ppermute | solution.py:422
  7.5 9.3 %collective-permute-start.3 = (f32[16,8,256]{2,1,0:T(8,128)S(1)}, f32[16,8,256]{2,1,0:T(8,128)S(1)}, u32[]{:S(2)}, u32[]{:S(2)}) collective-permute-start(f32[16,8,256]{2,1,0:T(8,128)S(1)} %get-tuple-element.23), channel_id=1, source_target_pairs={{0,12},{4,0},{8,4},{12,8},{1,13},{5,1},{9,5},{13,9},{2,14},{6,2},{... | collective-permute-start | bytes 393224 | tf_op jit(solution)/shard_map/ppermute | solution.py:422
  8.9 7.9 %collective-permute-start.4 = (f32[16,8,256]{2,1,0:T(8,128)S(1)}, f32[16,8,256]{2,1,0:T(8,128)S(1)}, u32[]{:S(2)}, u32[]{:S(2)}) collective-permute-start(f32[16,8,256]{2,1,0:T(8,128)S(1)} %get-tuple-element.24), channel_id=1, source_target_pairs={{0,4},{4,8},{8,12},{12,0},{1,5},{5,9},{9,13},{13,1},{2,6},{6,10},{... | collective-permute-start | bytes 393224 | tf_op jit(solution)/shard_map/ppermute | solution.py:422
  11.7 7.6 %collective-permute-start.5 = (f32[32,8,256]{2,1,0:T(8,128)S(1)}, f32[32,8,256]{2,1,0:T(8,128)S(1)}, u32[]{:S(2)}, u32[]{:S(2)}) collective-permute-start(f32[32,8,256]{2,1,0:T(8,128)S(1)} %shard_map.115), channel_id=1, source_target_pairs={{0,2},{2,0},{1,3},{3,1},{4,6},{6,4},{5,7},{7,5},{8,10},{10,8},{9,1... | collective-permute-start | bytes 786440 | tf_op jit(solution)/shard_map/ppermute | solution.py:428
  16.8 4.4 %collective-permute-start.6 = (f32[4,16,256]{2,1,0:T(8,128)S(1)}, f32[4,16,256]{2,1,0:T(8,128)S(1)}, u32[]{:S(2)}, u32[]{:S(2)}) collective-permute-start(f32[4,16,256]{2,1,0:T(8,128)S(1)} %shard_map.113.refs_5_), channel_id=1, source_target_pairs={{0,2},{2,0},{1,3},{3,1},{4,6},{6,4},{5,7},{7,5},{8,10},{10,8},{9,1... | collective-permute-start | bytes 196616 | tf_op jit(solution)/shard_map/ppermute | solution.py:428
  21.8 1.3 %collective-permute-start.7 = (f32[15,8,128]{2,1,0:T(8,128)S(1)}, f32[15,8,128]{2,1,0:T(8,128)S(1)}, u32[]{:S(2)}, u32[]{:S(2)}) collective-permute-start(f32[15,8,128]{2,1,0:T(8,128)S(1)} %get-tuple-element.34), channel_id=1, source_target_pairs={{0,1},{1,0},{2,3},{3,2},{4,5},{5,4},{6,7},{7,6},{8,9},{9,8},{10,11... | collective-permute-start | bytes 184328 | tf_op jit(solution)/shard_map/ppermute | solution.py:549

commit v6 on v5

--- a/solution.py
+++ b/solution.py
@@ -226,8 +226,6 @@
     source, kappa_ext, face = refs[5 + 3 * sides :]
     size_x, size_y, size_z = kappa.shape
     ext_y = size_y + 2 * HALO
-    vert = lax.axis_index("vert")
-    side = pl.ds(pl.multiple_of(jnp.where(vert == 0, size_z - 128, 0), 128), 128)
     for x in range(size_x + sides * HALO):
         if x < size_x:
             kappa_ext[x] = jnp.concatenate([kappa[x], upper[x, 0:HALO], lower[x, 0:HALO]], axis=0)
@@ -248,28 +246,32 @@
                 place = (x - size_x) % HALO * ext_y
                 value = strips[(x - size_x) // HALO][c, place : place + ext_y, :]
             source[c, x] = value * sig
-    lane = lax.broadcasted_iota(jnp.int32, (8, 128), 1)
-    tiles = face_tiles(size_x + sides * HALO, ext_y)
-    for g in range(0, len(tiles), 16):
-        packed = jnp.zeros((8, 128), F32)
-        for k, (c, x, y) in enumerate(tiles[g : g + 16]):
-            tile = kappa_ext[x, y : y + 8, side] if c == 3 else source[c, x, y : y + 8, side]
-            turned = pltpu.roll(tile, (8 * k + 8 * (1 - vert)) & 127, 1)
-            packed = jnp.where(lane // 8 == k, turned, packed)
-        face[g // 16] = packed
-
-
-def face_tiles(planes, ext_y):
-    return [(c, x, y) for c in range(4) for x in range(planes) for y in range(0, ext_y, 8)]
-
-
-def lanes_on(values, step, lane):
+    planes, vert = kappa_ext.shape[0], lax.axis_index("vert")
+    side = pl.ds(pl.multiple_of(jnp.where(vert == 0, size_z - 128, 0), 128), 128)
+    fields = [[source[c, x, :, side] for x in range(planes)] for c in range(3)]
+    fields.append([kappa_ext[x, :, side] for x in range(planes)])
+    fields = jnp.concatenate([jnp.concatenate(field, axis=1) for field in fields], axis=0)
+    lane = lax.broadcasted_iota(jnp.int32, (1, 128), 1)
+    lane = (lane + vert + 127) & 127
+    layer = jnp.where(vert == 0, 127 - lane // 32, lane // 32)
+    place = lax.broadcasted_iota(jnp.int32, (planes * 128, 128), 0)
+    pick = jnp.where(place == lane % 32 * 128 + layer, 1.0, 0.0).astype(BF16)
+    high, rest = two_parts(fields)
+    low = (fields - high.astype(F32) - rest.astype(F32)).astype(BF16)
+    sums = jnp.dot(jnp.concatenate([high, rest, low], axis=0), pick, preferred_element_type=F32)
+    for k in range(4):
+        parts = [sums[(4 * part + k) * ext_y : (4 * part + k + 1) * ext_y] for part in range(3)]
+        face[k] = parts[0] + (parts[1] + parts[2])
+
+
+def lanes_on(values, step, lane, beyond=None):
     tiles = [values[:, k : k + 128] for k in range(0, values.shape[1], 128)]
     turned = [pltpu.roll(tile, step % 128, 1) for tile in tiles]
     edge = lane == (0 if step == 1 else 127)
-    return jnp.concatenate(
-        [jnp.where(edge, turned[(k - step) % len(tiles)], turned[k]) for k in range(len(tiles))], axis=1
-    )
+    entering = turned[1:] + turned[:1] if step == -1 else turned[-1:] + turned[:-1]
+    if beyond is not None:
+        entering[-1 if step == -1 else 0] = beyond
+    return jnp.concatenate([jnp.where(edge, new, tile) for new, tile in zip(entering, turned)], axis=1)
 
 
 def each_plane(count, step, unroll=8):
@@ -311,93 +313,87 @@
     each_plane(planes, rest)
 
 
-def diffuse_kernel(sides, source, root, ax, ay, aym, az, azm, keep, face, out, *scratch):
-    ping, pong, halo, root_h, ax_h, ay_h, aym_h, az_all, azm_all, keep_all, done, sems = scratch
+def diffuse_kernel(sides, source, root, ax, ay, aym, az, azm, keep, sent, face, out, *scratch):
+    ping, pong, halo, edge, az_all, azm_all, keep_all, done, sems = scratch
     planes, ext_y, size_z = root.shape
-    size_x, size_y = out.shape[1], out.shape[2]
-    ext_z = size_z + 128
+    size_x, size_y = done.shape[1], done.shape[2]
     stream, vert = lax.axis_index("stream"), lax.axis_index("vert")
     last = lax.axis_size("stream") - 1
-    for x in range(size_x, planes):
-        for c in range(3):
-            ping[c, x] = jnp.zeros((ext_y, ext_z), F32)
-            pong[c, x] = jnp.zeros((ext_y, ext_z), F32)
     lane = lax.broadcasted_iota(jnp.int32, (ext_y, 128), 1)
-    known = lax.broadcasted_iota(jnp.int32, (8, 128), 1) // 8 == vert * 15
-    for t, (c, x, y) in enumerate(face_tiles(planes, ext_y)):
-        turned = pltpu.roll(face[t // 16], (256 - 8 * (t % 16) - 8 * vert) & 127, 1)
-        if c == 3:
-            root_h[x, y : y + 8, :] = jnp.sqrt(jnp.where(known, turned, 0.0))
-        else:
-            halo[c, x, y : y + 8, :] = turned
-
-    def faces(x):
-        after = jnp.where(x == planes - 1, 0, x + 1)
-        here, low, high = root_h[x], root[x, :, 0:128], root[x, :, size_z - 128 :]
-        wall = ((x == planes - 1) & (stream == 0)) | ((x == size_x - 1) & (stream == last))
-        ax_h[x] = here * root_h[after] * jnp.where(wall, 0.0, 1.0)
-        up = here * pltpu.roll(here, ext_y - 1, 0)
-        ay_h[x] = up
-        aym_h[x] = pltpu.roll(up, 1, 0)
-        over, under = pltpu.roll(here, 127, 1), pltpu.roll(here, 1, 1)
-        az_h = here * jnp.where(lane == 127, pltpu.roll(low, 127, 1), over)
-        azm_h = here * jnp.where(lane == 0, pltpu.roll(high, 1, 1), under)
-        top = jnp.where(lane == 127, high * over, 0.0)
-        bottom = jnp.where(lane == 0, low * under, 0.0)
+    spot = (lane + 128 - vert) & 127
+    plane, near = spot % 32, spot < 32
+
+    def plane_on(values):
+        return jnp.where(plane == planes - 1, pltpu.roll(values, planes - 1, 1), pltpu.roll(values, 127, 1))
+
+    def plane_back(values):
+        return jnp.where(plane == 0, pltpu.roll(values, 129 - planes, 1), pltpu.roll(values, 1, 1))
+
+    here = jnp.sqrt(face[3])
+    wall = ((plane == planes - 1) & (stream == 0)) | ((plane == size_x - 1) & (stream == last))
+    ax_h = jnp.where(wall, 0.0, here * plane_on(here))
+    axm_h = plane_back(ax_h)
+    ay_h = here * pltpu.roll(here, ext_y - 1, 0)
+    aym_h = pltpu.roll(ay_h, 1, 0)
+    far_h = jnp.where(spot >= 96, 0.0, here * pltpu.roll(here, 96, 1))
+    back = (2 * vert - 1) & 127
+    joint = jnp.where(near, here * jnp.sqrt(pltpu.roll(sent[3], back, 1)), 0.0)
+    near_h = jnp.where(near, joint, pltpu.roll(far_h, 32, 1))
+    keep_h = 1.0 - (ax_h + axm_h + ay_h + aym_h + far_h + near_h)
+    for c in range(3):
+        halo[0, c] = face[c]
+        edge[c] = pltpu.roll(sent[c], back, 1)
+
+    above, below = (lane == 127) & (vert == 0), (lane == 0) & (vert == 1)
+
+    for x in range(planes):
+        beside = pltpu.roll(joint, 127 - x, 1)
+        top, bottom = jnp.where(above, beside, 0.0), jnp.where(below, beside, 0.0)
         none = [jnp.zeros((ext_y, 128), F32)] * (size_z // 128 - 1)
         top, bottom = jnp.concatenate([*none, top], axis=1), jnp.concatenate([bottom, *none], axis=1)
-        az_all[x, :, 0:size_z] = az[x] + top
-        az_all[x, :, size_z:] = az_h
-        azm_all[x, :, 0:size_z] = azm[x] + bottom
-        azm_all[x, :, size_z:] = azm_h
-        keep_all[x, :, 0:size_z] = keep[x] - (top + bottom)
-
-    each_plane(planes, faces)
-
-    def rest(x):
-        before = jnp.where(x == 0, planes - 1, x - 1)
-        sides_sum = ax_h[x] + ax_h[before] + ay_h[x] + aym_h[x]
-        keep_all[x, :, size_z:] = 1.0 - (sides_sum + az_all[x, :, size_z:] + azm_all[x, :, size_z:])
-
-    each_plane(planes, rest)
-
-    def wide(main, beside):
-        return jnp.concatenate([main, beside], axis=1)
-
-    for p in range(PASSES):
+        az_all[x] = az[x] + top
+        azm_all[x] = azm[x] + bottom
+        keep_all[x] = keep[x] - (top + bottom)
+
+    side = pl.ds(pl.multiple_of(jnp.where(vert == 0, size_z - 128, 0), 128), 128)
+    step, copies = size_x // sems.shape[0], []
+
+    def one_pass(p, old, new):
         deep = PASSES - 1 - p
-        old, new = (ping, pong) if p % 2 == 0 else (pong, ping)
-        first = (jnp.where(stream == 0, 0, planes - deep) if sides == 1 else planes - deep) if deep else 0
-
-        def value_of(c, x, old=old, p=p):
-            return wide(source[c, x], halo[c, x]) if p == 0 else old[c, x]
-
-        def one_plane(i, value_of=value_of, new=new, first=first, p=p):
-            x = i + first
-            x = jnp.where(x >= planes, x - planes, x)
-            after = jnp.where(x == planes - 1, 0, x + 1)
-            before = jnp.where(x == 0, planes - 1, x - 1)
+        now, later = p % 2, (p + 1) % 2
+        if deep:
             for c in range(3):
-                value = value_of(c, x)
+                value = halo[now, c]
+                moved = keep_h * value + ax_h * plane_on(value) + axm_h * plane_back(value)
+                moved += ay_h * pltpu.roll(value, ext_y - 1, 0) + aym_h * pltpu.roll(value, 1, 0)
+                moved += far_h * pltpu.roll(value, 96, 1)
+                halo[later, c] = moved + near_h * jnp.where(near, edge[c], pltpu.roll(value, 32, 1))
+
+        for x in range(planes if deep else size_x):
+            after, before = (x + 1) % planes, (x - 1) % planes
+            for c in range(3):
+                value = old[c, x]
+                beside = pltpu.roll(halo[now, c], 127 - x, 1)
                 moved = keep_all[x] * value
-                moved += wide(ax[x], ax_h[x]) * value_of(c, after) + wide(ax[before], ax_h[before]) * value_of(c, before)
-                moved += wide(ay[x], ay_h[x]) * pltpu.roll(value, ext_y - 1, 0)
-                moved += wide(aym[x], aym_h[x]) * pltpu.roll(value, 1, 0)
-                moved += az_all[x] * lanes_on(value, -1, lane) + azm_all[x] * lanes_on(value, 1, lane)
-                if p == PASSES - 1:
-                    done[c, x] = moved[0:size_y, 0:size_z]
-                else:
-                    new[c, x] = moved
-
-        if p < PASSES - 1:
-            each_plane(size_x + sides * deep, one_plane)
-    step = size_x // sems.shape[0]
-    copies = []
-    for k in range(sems.shape[0]):
-        each_plane(step, lambda i, k=k: one_plane(i + k * step))
-        part = pl.ds(k * step, step)
-        copies.append(pltpu.make_async_copy(done.at[:, part], out.at[:, part], sems.at[k]))
-        copies[-1].start()
+                moved += ax[x] * old[c, after] + ax[before] * old[c, before]
+                moved += ay[x] * pltpu.roll(value, ext_y - 1, 0) + aym[x] * pltpu.roll(value, 1, 0)
+                moved += az_all[x] * lanes_on(value, -1, lane, beside) + azm_all[x] * lanes_on(value, 1, lane, beside)
+                new[c, x] = moved if deep else moved[0:size_y]
+            if not deep and (x + 1) % step == 0:
+                part = pl.ds(x + 1 - step, step)
+                copies.append(pltpu.make_async_copy(done.at[:, part], out.at[:, part], sems.at[x // step]))
+                copies[-1].start()
+        if deep > 1:
+            for c in range(3):
+                beside = pltpu.roll(new[c, 0, :, side], 1, 1)
+                for x in range(1, planes):
+                    beside = jnp.where(spot == x, pltpu.roll(new[c, x, :, side], x + 1, 1), beside)
+                edge[c] = beside
+
+    one_pass(0, source, pong)
+    one_pass(1, pong, ping)
+    one_pass(2, ping, pong)
+    one_pass(3, pong, done)
     for copy in copies:
         copy.wait()
 
@@ -531,10 +527,9 @@
         *others,
         room=24,
     )
-    tiles = len(face_tiles(ext_x, ext_y))
     source, kappa_ext, face = call(
         functools.partial(extend_kernel, sides),
-        [shape(3, ext_x, ext_y, size_z), shape(ext_x, ext_y, size_z), shape(-(-tiles // 16), 8, 128)],
+        [shape(3, ext_x, ext_y, size_z), shape(ext_x, ext_y, size_z), shape(4, ext_y, 128)],
         [],
         1000,
         own,
@@ -546,12 +541,12 @@
         *others,
         *corners,
     )
-    face = lax.ppermute(face, "vert", [(0, 1), (1, 0)])
-    main, beside, wide = ((ext_x, ext_y, width) for width in (size_z, 128, size_z + 128))
+    other_face = lax.ppermute(face, "vert", [(0, 1), (1, 0)])
+    main = (ext_x, ext_y, size_z)
     coefficients = call(
         functools.partial(coefficient_kernel, sides, size_x), [shape(*main)] * 7, [], 30 * ext_x * ext_y * size_z, kappa_ext
     )
-    scratch = [(3, *wide)] * 2 + [(3, *beside)] + [beside] * 4 + [wide] * 3 + [(3, size_x, size_y, size_z)]
+    scratch = [(3, *main)] * 2 + [(2, 3, ext_y, 128), (3, ext_y, 128)] + [main] * 3 + [(3, size_x, size_y, size_z)]
     (field,) = call(
         functools.partial(diffuse_kernel, sides),
         [shape(3, size_x, size_y, size_z)],
@@ -560,6 +555,7 @@
         source,
         *coefficients,
         face,
+        other_face,
         room=20,
         far=True,
     )

time: 31.3 us -> 28.6 us (0.914)
  Pallas kernels: 19.1 us -> 16.4 us
    pallas_call x11, Pallas kernels: 19.1 us -> 16.4 us  [call(): pl.pallas_call(kernel, out_shape=outs, in_specs=[pl.BlockSpec(memory_spac...]
  transfers between devices with their start and end apart: 8 -> 8, of which waited for: 2 -> 2; matrix products, arithmetic and copies ran while one was open for 0% -> 0% of each run, Pallas kernels for 30% -> 33%
where the time goes in v6:
time: 28.6 us; the launch traced here: 28.4 us
  Pallas kernels  16.4 us (57%)
  starting transfers between devices  11.1 us (39%)
  waiting for transfers between devices  0.53 us (2%)
  between operations  0.29 us (1%)
    pallas_call x11, Pallas kernels, call(): pl.pallas_call(kernel, out_shape=outs, in_specs=[pl.BlockSpec(memory_spac...  16.4 us
    ppermute x5, starting transfers between devices, ring(): lax.ppermute(array, 'span', [(i, (i + step) % count) for i in range(count)])  8.19 us
    ppermute x2, starting transfers between devices, across_bands(): return [lax.ppermute(arrays[0], 'stream', [(0, 1), (1, 0)])]  2.88 us
  transfers between devices with their start and end apart: 8, of which 2 were waited for; matrix products, arithmetic and copies ran while one was open for 0% of the time, Pallas kernels for 33%

profile of v6, /device:TPU:0, one launch (start us, length us, event | category | flops | bytes accessed | tf_op | source)
XLA Modules:
  0.0 28.4 jit_solution(13984110176390669970)
XLA Ops:
  0.0 1.3 %shard_map.109 = (f32[8,1024]{1,0:T(8,128)S(1)}, f32[16,16,256]{2,1,0:T(8,128)S(1)}, f32[16,16,256]{2,1,0:T(8,128)S(1)}) custom-call(f32[1,1,1024]{2,1,0:T(1,128)} %refs_0_.1, f32[1,1,1024]{2,1,0:T(1,128)} %refs_1_.1, f32[1,1,1024]{2,1,0:T(1,128)} %refs_2_.1, s32[1,1024]{1,0:T(1,128)} %bitcast.1, s32[1,1,1024]{2,1,0:T(1,128)} %refs_4_.1, ...), custom_call_target="tpu_custom_call" | custom-call | flops 1000 | bytes 1107968 | tf_op jit(solution)/shard_map/pallas_call | solution.py:404
  1.3 3.1 %collective-permute-start.2 = (f32[8,1024]{1,0:T(8,128)S(1)}, f32[8,1024]{1,0:T(8,128)S(1)}, u32[]{:S(2)}, u32[]{:S(2)}) collective-permute-start(f32[8,1024]{1,0:T(8,128)S(1)} %get-tuple-element.20.payload.refs_0_), channel_id=1, source_target_pairs={{0,4},{4,8},{8,12},{12,0},{1,5},{5,9},{9,13},{13,1},{2,6},{6,10},{... | collective-permute-start | bytes 98312 | tf_op jit(solution)/shard_map/ppermute | solution.py:418
  4.4 2.1 %collective-permute-start.1 = (f32[8,1024]{1,0:T(8,128)S(1)}, f32[8,1024]{1,0:T(8,128)S(1)}, u32[]{:S(2)}, u32[]{:S(2)}) collective-permute-start(f32[8,1024]{1,0:T(8,128)S(1)} %get-tuple-element.20.payload.refs_0_), channel_id=1, source_target_pairs={{0,12},{4,0},{8,4},{12,8},{1,13},{5,1},{9,5},{13,9},{2,14},{6,2},{... | collective-permute-start | bytes 98312 | tf_op jit(solution)/shard_map/ppermute | solution.py:418
  6.5 0.9 %collective-permute-start = (f32[8,1024]{1,0:T(8,128)S(1)}, f32[8,1024]{1,0:T(8,128)S(1)}, u32[]{:S(2)}, u32[]{:S(2)}) collective-permute-start(f32[8,1024]{1,0:T(8,128)S(1)} %get-tuple-element.20.payload.refs_0_), channel_id=1, source_target_pairs={{0,8},{4,12},{8,0},{12,4},{1,9},{5,13},{9,1},{13,5},{2,10},{6,14},... | collective-permute-start | bytes 98312 | tf_op jit(solution)/shard_map/ppermute | solution.py:418
  7.5 0.1 shard_map.112
  7.5 1.4 %collective-permute-start.3 = (f32[16,8,256]{2,1,0:T(8,128)S(1)}, f32[16,8,256]{2,1,0:T(8,128)S(1)}, u32[]{:S(2)}, u32[]{:S(2)}) collective-permute-start(f32[16,8,256]{2,1,0:T(8,128)S(1)} %get-tuple-element.23), channel_id=1, source_target_pairs={{0,12},{4,0},{8,4},{12,8},{1,13},{5,1},{9,5},{13,9},{2,14},{6,2},{... | collective-permute-start | bytes 393224 | tf_op jit(solution)/shard_map/ppermute | solution.py:418
  8.9 0.7 %collective-permute-start.4 = (f32[16,8,256]{2,1,0:T(8,128)S(1)}, f32[16,8,256]{2,1,0:T(8,128)S(1)}, u32[]{:S(2)}, u32[]{:S(2)}) collective-permute-start(f32[16,8,256]{2,1,0:T(8,128)S(1)} %get-tuple-element.24), channel_id=1, source_target_pairs={{0,4},{4,8},{8,12},{12,0},{1,5},{5,9},{9,13},{13,1},{2,6},{6,10},{... | collective-permute-start | bytes 393224 | tf_op jit(solution)/shard_map/ppermute | solution.py:418
  9.6 1.7 %shard_map.110.refs_4_ = f32[3,384,256]{2,1,0:T(8,128)S(1)} custom-call(f32[8,1024]{1,0:T(8,128)S(1)} %get-tuple-element.20.payload.refs_0_), custom_call_target="tpu_custom_call" | custom-call | flops 1207959552 | bytes 1212416 | tf_op jit(solution)/shard_map/pallas_call | solution.py:404
  11.3 0.0 collective-permute-done.2.refs_3_
  11.3 0.0 collective-permute-done.1.refs_2_
  11.3 0.3 %collective-permute-done.refs_1_ = f32[8,1024]{1,0:T(8,128)S(1)} collective-permute-done((f32[8,1024]{1,0:T(8,128)S(1)}, f32[8,1024]{1,0:T(8,128)S(1)}, u32[]{:S(2)}, u32[]{:S(2)}) %collective-permute-start) | collective-permute-done | bytes 32800 | tf_op jit(solution)/shard_map/ppermute | solution.py:418
  11.7 1.7 %collective-permute-start.5 = (f32[32,8,256]{2,1,0:T(8,128)S(1)}, f32[32,8,256]{2,1,0:T(8,128)S(1)}, u32[]{:S(2)}, u32[]{:S(2)}) collective-permute-start(f32[32,8,256]{2,1,0:T(8,128)S(1)} %shard_map.115), channel_id=1, source_target_pairs={{0,2},{2,0},{1,3},{3,1},{4,6},{6,4},{5,7},{7,5},{8,10},{10,8},{9,1... | collective-permute-start | bytes 786440 | tf_op jit(solution)/shard_map/ppermute | solution.py:424
  13.4 3.4 %shard_map.111.refs_4_ = f32[3,384,256]{2,1,0:T(8,128)S(1)} custom-call(f32[8,1024]{1,0:T(8,128)S(1)} %get-tuple-element.20.payload.refs_0_, f32[8,1024]{1,0:T(8,128)S(1)} %collective-permute-done.refs_1_, f32[8,1024]{1,0:T(8,128)S(1)} %collective-permute-done.1.refs_2_, ...), custom_call_target="tpu_custom_call", output_to_operand_aliasing={{}: (4, {})} | custom-call | flops 3623878656 | bytes 2490368 | tf_op jit(solution)/shard_map/pallas_call | solution.py:404
  16.8 0.0 collective-permute-done.3.upper.refs_3_
  16.8 0.0 collective-permute-done.4.lower.refs_4_
  16.8 1.1 %collective-permute-start.6 = (f32[4,16,256]{2,1,0:T(8,128)S(1)}, f32[4,16,256]{2,1,0:T(8,128)S(1)}, u32[]{:S(2)}, u32[]{:S(2)}) collective-permute-start(f32[4,16,256]{2,1,0:T(8,128)S(1)} %shard_map.113.refs_5_), channel_id=1, source_target_pairs={{0,2},{2,0},{1,3},{3,1},{4,6},{6,4},{5,7},{7,5},{8,10},{10,8},{9,1... | collective-permute-start | bytes 196616 | tf_op jit(solution)/shard_map/ppermute | solution.py:424
  18.0 1.3 %shard_map.114.refs_0_ = f32[3,384,256]{2,1,0:T(8,128)S(1)} custom-call(f32[8,1024]{1,0:T(8,128)S(1)} %get-tuple-element.20.payload.refs_0_, f32[8,1024]{1,0:T(8,128)S(1)} %collective-permute-done.refs_1_, f32[8,1024]{1,0:T(8,128)S(1)} %collective-permute-done.1.refs_2_, ...), custom_call_target="tpu_custom_call", output_to_operand_aliasing={{}: (4, {})} | custom-call | flops 301989888 | bytes 2555904 | tf_op jit(solution)/shard_map/pallas_call | solution.py:404
  19.3 0.0 collective-permute-done.5.refs_0_.refs_6_
  19.3 1.9 %shard_map.116.refs_5_ = f32[3,96,256]{2,1,0:T(8,128)S(1)} custom-call(f32[32,8,256]{2,1,0:T(8,128)S(1)} %collective-permute-done.5.refs_0_.refs_6_), custom_call_target="tpu_custom_call" | custom-call | flops 1207959552 | bytes 557056 | tf_op jit(solution)/shard_map/pallas_call | solution.py:404
  21.2 0.0 collective-permute-done.6.refs_7_
  21.2 0.7 %shard_map.117 = (f32[3,20,24,256]{3,2,1,0:T(8,128)S(1)}, f32[20,24,256]{2,1,0:T(8,128)S(1)}, f32[4,24,128]{2,1,0:T(8,128)S(1)}) custom-call(f32[3,384,256]{2,1,0:T(8,128)S(1)} %shard_map.114.refs_0_, f32[16,16,256]{2,1,0:T(8,128)S(1)} %get-tuple-element.21.kappa.refs_4_.refs_1_, f32[16,16,256]{2,1,0:T(8,128)S(1)} %get-tuple-element.22.sigma.refs_5_.refs_2_, ...), custom_call_target="tpu_custom_call" | custom-call | flops 1000 | bytes 4603904 | tf_op jit(solution)/shard_map/pallas_call | solution.py:404
  21.9 0.1 collective-permute-start.7
  22.0 1.0 %shard_map.118 = (f32[20,24,256]{2,1,0:T(8,128)S(1)}, f32[20,24,256]{2,1,0:T(8,128)S(1)}, f32[20,24,256]{2,1,0:T(8,128)S(1)}, f32[20,24,256]{2,1,0:T(8,128)S(1)}...) custom-call(f32[20,24,256]{2,1,0:T(8,128)S(1)} %get-tuple-element.26.kappa_ext), custom_call_target="tpu_custom_call" | custom-call | flops 3686400 | bytes 3932160 | tf_op jit(solution)/shard_map/pallas_call | solution.py:404
  23.0 0.2 collective-permute-done.7.face
  23.2 5.1 %shard_map.119 = f32[3,16,16,256]{3,2,1,0:T(8,128)} custom-call(f32[3,20,24,256]{3,2,1,0:T(8,128)S(1)} %get-tuple-element.25.source, f32[20,24,256]{2,1,0:T(8,128)S(1)} %get-tuple-element.27.root, f32[20,24,256]{2,1,0:T(8,128)S(1)} %get-tuple-element.28.ax, f32[20,24,256]{2,1,0:T(8,128)S(1)} %get-tuple-element.29.ay, ...), custom_call_target="tpu_custom_call" | custom-call | flops 22118400 | bytes 5799936 | tf_op jit(solution)/shard_map/pallas_call | solution.py:404
  (2 shorter events, 0.0 us)
Async XLA Ops:
  1.3 9.9 %collective-permute-start.2 = (f32[8,1024]{1,0:T(8,128)S(1)}, f32[8,1024]{1,0:T(8,128)S(1)}, u32[]{:S(2)}, u32[]{:S(2)}) collective-permute-start(f32[8,1024]{1,0:T(8,128)S(1)} %get-tuple-element.20.payload.refs_0_), channel_id=1, source_target_pairs={{0,4},{4,8},{8,12},{12,0},{1,5},{5,9},{9,13},{13,1},{2,6},{6,10},{... | collective-permute-start | bytes 98312 | tf_op jit(solution)/shard_map/ppermute | solution.py:418
  4.4 6.9 %collective-permute-start.1 = (f32[8,1024]{1,0:T(8,128)S(1)}, f32[8,1024]{1,0:T(8,128)S(1)}, u32[]{:S(2)}, u32[]{:S(2)}) collective-permute-start(f32[8,1024]{1,0:T(8,128)S(1)} %get-tuple-element.20.payload.refs_0_), channel_id=1, source_target_pairs={{0,12},{4,0},{8,4},{12,8},{1,13},{5,1},{9,5},{13,9},{2,14},{6,2},{... | collective-permute-start | bytes 98312 | tf_op jit(solution)/shard_map/ppermute | solution.py:418
  6.5 5.1 %collective-permute-start = (f32[8,1024]{1,0:T(8,128)S(1)}, f32[8,1024]{1,0:T(8,128)S(1)}, u32[]{:S(2)}, u32[]{:S(2)}) collective-permute-start(f32[8,1024]{1,0:T(8,128)S(1)} %get-tuple-element.20.payload.refs_0_), channel_id=1, source_target_pairs={{0,8},{4,12},{8,0},{12,4},{1,9},{5,13},{9,1},{13,5},{2,10},{6,14},... | collective-permute-start | bytes 98312 | tf_op jit(solution)/shard_map/ppermute | solution.py:418
  7.5 9.3 %collective-permute-start.3 = (f32[16,8,256]{2,1,0:T(8,128)S(1)}, f32[16,8,256]{2,1,0:T(8,128)S(1)}, u32[]{:S(2)}, u32[]{:S(2)}) collective-permute-start(f32[16,8,256]{2,1,0:T(8,128)S(1)} %get-tuple-element.23), channel_id=1, source_target_pairs={{0,12},{4,0},{8,4},{12,8},{1,13},{5,1},{9,5},{13,9},{2,14},{6,2},{... | collective-permute-start | bytes 393224 | tf_op jit(solution)/shard_map/ppermute | solution.py:418
  8.9 7.9 %collective-permute-start.4 = (f32[16,8,256]{2,1,0:T(8,128)S(1)}, f32[16,8,256]{2,1,0:T(8,128)S(1)}, u32[]{:S(2)}, u32[]{:S(2)}) collective-permute-start(f32[16,8,256]{2,1,0:T(8,128)S(1)} %get-tuple-element.24), channel_id=1, source_target_pairs={{0,4},{4,8},{8,12},{12,0},{1,5},{5,9},{9,13},{13,1},{2,6},{6,10},{... | collective-permute-start | bytes 393224 | tf_op jit(solution)/shard_map/ppermute | solution.py:418
  11.7 7.6 %collective-permute-start.5 = (f32[32,8,256]{2,1,0:T(8,128)S(1)}, f32[32,8,256]{2,1,0:T(8,128)S(1)}, u32[]{:S(2)}, u32[]{:S(2)}) collective-permute-start(f32[32,8,256]{2,1,0:T(8,128)S(1)} %shard_map.115), channel_id=1, source_target_pairs={{0,2},{2,0},{1,3},{3,1},{4,6},{6,4},{5,7},{7,5},{8,10},{10,8},{9,1... | collective-permute-start | bytes 786440 | tf_op jit(solution)/shard_map/ppermute | solution.py:424
  16.8 4.4 %collective-permute-start.6 = (f32[4,16,256]{2,1,0:T(8,128)S(1)}, f32[4,16,256]{2,1,0:T(8,128)S(1)}, u32[]{:S(2)}, u32[]{:S(2)}) collective-permute-start(f32[4,16,256]{2,1,0:T(8,128)S(1)} %shard_map.113.refs_5_), channel_id=1, source_target_pairs={{0,2},{2,0},{1,3},{3,1},{4,6},{6,4},{5,7},{7,5},{8,10},{10,8},{9,1... | collective-permute-start | bytes 196616 | tf_op jit(solution)/shard_map/ppermute | solution.py:424
  21.9 1.3 %collective-permute-start.7 = (f32[4,24,128]{2,1,0:T(8,128)S(1)}, f32[4,24,128]{2,1,0:T(8,128)S(1)}, u32[]{:S(2)}, u32[]{:S(2)}) collective-permute-start(f32[4,24,128]{2,1,0:T(8,128)S(1)} %get-tuple-element.34.sent), channel_id=1, source_target_pairs={{0,1},{1,0},{2,3},{3,2},{4,5},{5,4},{6,7},{7,6},{8,9},{9,8},{10,11... | collective-permute-start | bytes 147464 | tf_op jit(solution)/shard_map/ppermute | solution.py:544

commit v7 on v6

--- a/solution.py
+++ b/solution.py
@@ -88,33 +88,38 @@
 
 def spread_points(payload_of, near, out, start_x, planes, size_y, size_z, first):
     ext_y = size_y + 2 * HALO
-    height = planes * ext_y
     points = payload_of(0).shape[1] // 4
-    count = len(near) * points
-    rows = [[payload_of(j)[r : r + 1, :] for r in (5, 6)] for j, _ in near]
-
-    def joined(r, k):
-        return jnp.concatenate([pair[r][:, k * points : (k + 1) * points] for pair in rows], axis=1)
-
-    px, pz = joined(0, 3), joined(1, 1)
-    py = jnp.concatenate(
-        [pair[1][:, 0:points] + F32(side * size_y) for pair, (_, side) in zip(rows, near)], axis=1
-    )
-    y_row = lax.broadcasted_iota(jnp.int32, (ext_y, count), 0)
-    by = bump(jnp.where(y_row < size_y + HALO, y_row, y_row - ext_y).astype(F32) - py)
-    x_cell = (lax.broadcasted_iota(jnp.int32, (planes, count), 0) + start_x).astype(F32)
-    bx = bump(x_cell - px)
-    z_cell = lax.broadcasted_iota(jnp.int32, (size_z, count), 0) + lax.axis_index("vert") * size_z
-    bz_high, bz_low = two_parts(bump(z_cell.astype(F32) - pz))
-    cross = jnp.concatenate([by * bx[x : x + 1] for x in range(planes)], axis=0)
-    parts = [two_parts(cross * joined(0, c)) for c in range(3)]
-    by_high = dot_lanes(jnp.concatenate([part for pair in parts for part in pair], axis=0), bz_high)
-    by_low = dot_lanes(jnp.concatenate([high for high, _ in parts], axis=0), bz_low)
-    for c in range(3):
-        high = 2 * c * height
-        both = by_high[high : high + height] + by_high[high + height : high + 2 * height]
-        both += by_low[c * height : (c + 1) * height]
-        out[c] = both if first is None else first[c] + both
+    y_row = lax.broadcasted_iota(jnp.int32, (ext_y, points), 0)
+    y_cell = jnp.where(y_row < size_y + HALO, y_row, y_row - ext_y).astype(F32)
+    x_cell = (lax.broadcasted_iota(jnp.int32, (planes, points), 0) + start_x).astype(F32)
+    z_cell = lax.broadcasted_iota(jnp.int32, (size_z, points), 0) + lax.axis_index("vert") * size_z
+    z_cell = z_cell.astype(F32)
+    written = set()
+    for j, side in near:
+        upper, lower = (payload_of(j)[r : r + 1, :] for r in (5, 6))
+        force = [upper[:, c * points : (c + 1) * points] for c in range(3)]
+        py = lower[:, 0:points] + F32(side * size_y)
+        bx, by = bump(x_cell - upper[:, 3 * points :]), bump(y_cell - py)
+        bz_high, bz_low = two_parts(bump(z_cell - lower[:, points : 2 * points]))
+        tiles = [t for t in range(0, ext_y, 8) if t >= size_y or side == 0 or t == (0 if side < 0 else size_y - 8)]
+        by = jnp.concatenate([by[t : t + 8] for t in tiles], axis=0)
+        cross = jnp.concatenate([by * bx[x : x + 1] for x in range(planes)], axis=0)
+        parts = [two_parts(cross * force[c]) for c in range(3)]
+        by_high = dot_lanes(jnp.concatenate([part for pair in parts for part in pair], axis=0), bz_high)
+        by_low = dot_lanes(jnp.concatenate([high for high, _ in parts], axis=0), bz_low)
+        height = cross.shape[0]
+        for c in range(3):
+            high = 2 * c * height
+            both = by_high[high : high + height] + by_high[high + height : high + 2 * height]
+            both += by_low[c * height : (c + 1) * height]
+            for x in range(planes):
+                for k, t in enumerate(tiles):
+                    rows = slice(x * ext_y + t, x * ext_y + t + 8)
+                    place = (x * len(tiles) + k) * 8
+                    value = both[place : place + 8]
+                    before = out if t in written else first
+                    out[c, rows, :] = value if before is None else before[c, rows, :] + value
+        written.update(tiles)
 
 
 def spread_gates(payload_of, spans, sources, out, start_x, planes, size_y, size_z, unroll=False):
@@ -257,11 +262,9 @@
     place = lax.broadcasted_iota(jnp.int32, (planes * 128, 128), 0)
     pick = jnp.where(place == lane % 32 * 128 + layer, 1.0, 0.0).astype(BF16)
     high, rest = two_parts(fields)
-    low = (fields - high.astype(F32) - rest.astype(F32)).astype(BF16)
-    sums = jnp.dot(jnp.concatenate([high, rest, low], axis=0), pick, preferred_element_type=F32)
+    sums = jnp.dot(jnp.concatenate([high, rest], axis=0), pick, preferred_element_type=F32)
     for k in range(4):
-        parts = [sums[(4 * part + k) * ext_y : (4 * part + k + 1) * ext_y] for part in range(3)]
-        face[k] = parts[0] + (parts[1] + parts[2])
+        face[k] = sums[k * ext_y : (k + 1) * ext_y] + sums[(4 + k) * ext_y : (5 + k) * ext_y]
 
 
 def lanes_on(values, step, lane, beyond=None):

time: 28.6 us -> 28.6 us (level)
  transfers between devices with their start and end apart: 8 -> 8, of which waited for: 2 -> 3; matrix products, arithmetic and copies ran while one was open for 0% -> 0% of each run, Pallas kernels for 33% -> 32%
where the time goes in v7:
time: 28.6 us; the launch traced here: 28.4 us
  Pallas kernels  16.2 us (57%)
  starting transfers between devices  11.1 us (39%)
  waiting for transfers between devices  0.75 us (3%)
    pallas_call x11, Pallas kernels, call(): pl.pallas_call(kernel, out_shape=outs, in_specs=[pl.BlockSpec(memory_spac...  16.2 us
    ppermute x5, starting transfers between devices, ring(): lax.ppermute(array, 'span', [(i, (i + step) % count) for i in range(count)])  8.19 us
    ppermute x2, starting transfers between devices, across_bands(): return [lax.ppermute(arrays[0], 'stream', [(0, 1), (1, 0)])]  2.88 us
  transfers between devices with their start and end apart: 8, of which 3 were waited for; matrix products, arithmetic and copies ran while one was open for 0% of the time, Pallas kernels for 32%

profile of v7, /device:TPU:0, one launch (start us, length us, event | category | flops | bytes accessed | tf_op | source)
XLA Modules:
  0.0 28.4 jit_solution(290741897594745125)
XLA Ops:
  0.0 1.3 %shard_map.109 = (f32[8,1024]{1,0:T(8,128)S(1)}, f32[16,16,256]{2,1,0:T(8,128)S(1)}, f32[16,16,256]{2,1,0:T(8,128)S(1)}) custom-call(f32[1,1,1024]{2,1,0:T(1,128)} %refs_0_.1, f32[1,1,1024]{2,1,0:T(1,128)} %refs_1_.1, f32[1,1,1024]{2,1,0:T(1,128)} %refs_2_.1, s32[1,1024]{1,0:T(1,128)} %bitcast.1, s32[1,1,1024]{2,1,0:T(1,128)} %refs_4_.1, ...), custom_call_target="tpu_custom_call" | custom-call | flops 1000 | bytes 1107968 | tf_op jit(solution)/shard_map/pallas_call | solution.py:407
  1.3 3.1 %collective-permute-start.2 = (f32[8,1024]{1,0:T(8,128)S(1)}, f32[8,1024]{1,0:T(8,128)S(1)}, u32[]{:S(2)}, u32[]{:S(2)}) collective-permute-start(f32[8,1024]{1,0:T(8,128)S(1)} %get-tuple-element.20.payload.refs_0_), channel_id=1, source_target_pairs={{0,4},{4,8},{8,12},{12,0},{1,5},{5,9},{9,13},{13,1},{2,6},{6,10},{... | collective-permute-start | bytes 98312 | tf_op jit(solution)/shard_map/ppermute | solution.py:421
  4.4 2.1 %collective-permute-start.1 = (f32[8,1024]{1,0:T(8,128)S(1)}, f32[8,1024]{1,0:T(8,128)S(1)}, u32[]{:S(2)}, u32[]{:S(2)}) collective-permute-start(f32[8,1024]{1,0:T(8,128)S(1)} %get-tuple-element.20.payload.refs_0_), channel_id=1, source_target_pairs={{0,12},{4,0},{8,4},{12,8},{1,13},{5,1},{9,5},{13,9},{2,14},{6,2},{... | collective-permute-start | bytes 98312 | tf_op jit(solution)/shard_map/ppermute | solution.py:421
  6.5 0.9 %collective-permute-start = (f32[8,1024]{1,0:T(8,128)S(1)}, f32[8,1024]{1,0:T(8,128)S(1)}, u32[]{:S(2)}, u32[]{:S(2)}) collective-permute-start(f32[8,1024]{1,0:T(8,128)S(1)} %get-tuple-element.20.payload.refs_0_), channel_id=1, source_target_pairs={{0,8},{4,12},{8,0},{12,4},{1,9},{5,13},{9,1},{13,5},{2,10},{6,14},... | collective-permute-start | bytes 98312 | tf_op jit(solution)/shard_map/ppermute | solution.py:421
  7.5 0.1 shard_map.112
  7.5 1.4 %collective-permute-start.3 = (f32[16,8,256]{2,1,0:T(8,128)S(1)}, f32[16,8,256]{2,1,0:T(8,128)S(1)}, u32[]{:S(2)}, u32[]{:S(2)}) collective-permute-start(f32[16,8,256]{2,1,0:T(8,128)S(1)} %get-tuple-element.23), channel_id=1, source_target_pairs={{0,12},{4,0},{8,4},{12,8},{1,13},{5,1},{9,5},{13,9},{2,14},{6,2},{... | collective-permute-start | bytes 393224 | tf_op jit(solution)/shard_map/ppermute | solution.py:421
  8.9 0.7 %collective-permute-start.4 = (f32[16,8,256]{2,1,0:T(8,128)S(1)}, f32[16,8,256]{2,1,0:T(8,128)S(1)}, u32[]{:S(2)}, u32[]{:S(2)}) collective-permute-start(f32[16,8,256]{2,1,0:T(8,128)S(1)} %get-tuple-element.24), channel_id=1, source_target_pairs={{0,4},{4,8},{8,12},{12,0},{1,5},{5,9},{9,13},{13,1},{2,6},{6,10},{... | collective-permute-start | bytes 393224 | tf_op jit(solution)/shard_map/ppermute | solution.py:421
  9.6 1.7 %shard_map.110.refs_4_ = f32[3,384,256]{2,1,0:T(8,128)S(1)} custom-call(f32[8,1024]{1,0:T(8,128)S(1)} %get-tuple-element.20.payload.refs_0_), custom_call_target="tpu_custom_call" | custom-call | flops 1207959552 | bytes 1212416 | tf_op jit(solution)/shard_map/pallas_call | solution.py:407
  11.3 0.0 collective-permute-done.2.refs_3_
  11.3 0.0 collective-permute-done.1.refs_2_
  11.3 0.4 %collective-permute-done.refs_1_ = f32[8,1024]{1,0:T(8,128)S(1)} collective-permute-done((f32[8,1024]{1,0:T(8,128)S(1)}, f32[8,1024]{1,0:T(8,128)S(1)}, u32[]{:S(2)}, u32[]{:S(2)}) %collective-permute-start) | collective-permute-done | bytes 32800 | tf_op jit(solution)/shard_map/ppermute | solution.py:421
  11.7 1.7 %collective-permute-start.5 = (f32[32,8,256]{2,1,0:T(8,128)S(1)}, f32[32,8,256]{2,1,0:T(8,128)S(1)}, u32[]{:S(2)}, u32[]{:S(2)}) collective-permute-start(f32[32,8,256]{2,1,0:T(8,128)S(1)} %shard_map.115), channel_id=1, source_target_pairs={{0,2},{2,0},{1,3},{3,1},{4,6},{6,4},{5,7},{7,5},{8,10},{10,8},{9,1... | collective-permute-start | bytes 786440 | tf_op jit(solution)/shard_map/ppermute | solution.py:427
  13.4 3.4 %shard_map.111.refs_4_ = f32[3,384,256]{2,1,0:T(8,128)S(1)} custom-call(f32[8,1024]{1,0:T(8,128)S(1)} %get-tuple-element.20.payload.refs_0_, f32[8,1024]{1,0:T(8,128)S(1)} %collective-permute-done.refs_1_, f32[8,1024]{1,0:T(8,128)S(1)} %collective-permute-done.1.refs_2_, ...), custom_call_target="tpu_custom_call", output_to_operand_aliasing={{}: (4, {})} | custom-call | flops 3623878656 | bytes 2490368 | tf_op jit(solution)/shard_map/pallas_call | solution.py:407
  16.8 0.0 collective-permute-done.3.upper.refs_3_
  16.8 0.0 collective-permute-done.4.lower.refs_4_
  16.8 1.1 %collective-permute-start.6 = (f32[4,16,256]{2,1,0:T(8,128)S(1)}, f32[4,16,256]{2,1,0:T(8,128)S(1)}, u32[]{:S(2)}, u32[]{:S(2)}) collective-permute-start(f32[4,16,256]{2,1,0:T(8,128)S(1)} %shard_map.113.refs_5_), channel_id=1, source_target_pairs={{0,2},{2,0},{1,3},{3,1},{4,6},{6,4},{5,7},{7,5},{8,10},{10,8},{9,1... | collective-permute-start | bytes 196616 | tf_op jit(solution)/shard_map/ppermute | solution.py:427
  18.0 1.1 %shard_map.114.refs_0_ = f32[3,384,256]{2,1,0:T(8,128)S(1)} custom-call(f32[8,1024]{1,0:T(8,128)S(1)} %get-tuple-element.20.payload.refs_0_, f32[8,1024]{1,0:T(8,128)S(1)} %collective-permute-done.refs_1_, f32[8,1024]{1,0:T(8,128)S(1)} %collective-permute-done.1.refs_2_, ...), custom_call_target="tpu_custom_call", output_to_operand_aliasing={{}: (4, {})} | custom-call | flops 301989888 | bytes 2555904 | tf_op jit(solution)/shard_map/pallas_call | solution.py:407
  19.1 0.0 collective-permute-done.5.refs_0_.refs_6_
  19.1 1.9 %shard_map.116.refs_5_ = f32[3,96,256]{2,1,0:T(8,128)S(1)} custom-call(f32[32,8,256]{2,1,0:T(8,128)S(1)} %collective-permute-done.5.refs_0_.refs_6_), custom_call_target="tpu_custom_call" | custom-call | flops 1207959552 | bytes 557056 | tf_op jit(solution)/shard_map/pallas_call | solution.py:407
  21.0 0.2 collective-permute-done.6.refs_7_
  21.2 0.7 %shard_map.117 = (f32[3,20,24,256]{3,2,1,0:T(8,128)S(1)}, f32[20,24,256]{2,1,0:T(8,128)S(1)}, f32[4,24,128]{2,1,0:T(8,128)S(1)}) custom-call(f32[3,384,256]{2,1,0:T(8,128)S(1)} %shard_map.114.refs_0_, f32[16,16,256]{2,1,0:T(8,128)S(1)} %get-tuple-element.21.kappa.refs_4_.refs_1_, f32[16,16,256]{2,1,0:T(8,128)S(1)} %get-tuple-element.22.sigma.refs_5_.refs_2_, ...), custom_call_target="tpu_custom_call" | custom-call | flops 1000 | bytes 4603904 | tf_op jit(solution)/shard_map/pallas_call | solution.py:407
  21.9 0.1 collective-permute-start.7
  22.0 1.0 %shard_map.118 = (f32[20,24,256]{2,1,0:T(8,128)S(1)}, f32[20,24,256]{2,1,0:T(8,128)S(1)}, f32[20,24,256]{2,1,0:T(8,128)S(1)}, f32[20,24,256]{2,1,0:T(8,128)S(1)}...) custom-call(f32[20,24,256]{2,1,0:T(8,128)S(1)} %get-tuple-element.26.kappa_ext), custom_call_target="tpu_custom_call" | custom-call | flops 3686400 | bytes 3932160 | tf_op jit(solution)/shard_map/pallas_call | solution.py:407
  23.0 0.2 collective-permute-done.7.face
  23.2 5.1 %shard_map.119 = f32[3,16,16,256]{3,2,1,0:T(8,128)} custom-call(f32[3,20,24,256]{3,2,1,0:T(8,128)S(1)} %get-tuple-element.25.source, f32[20,24,256]{2,1,0:T(8,128)S(1)} %get-tuple-element.27.root, f32[20,24,256]{2,1,0:T(8,128)S(1)} %get-tuple-element.28.ax, f32[20,24,256]{2,1,0:T(8,128)S(1)} %get-tuple-element.29.ay, ...), custom_call_target="tpu_custom_call" | custom-call | flops 22118400 | bytes 5799936 | tf_op jit(solution)/shard_map/pallas_call | solution.py:407
  (2 shorter events, 0.0 us)
Async XLA Ops:
  1.3 9.9 %collective-permute-start.2 = (f32[8,1024]{1,0:T(8,128)S(1)}, f32[8,1024]{1,0:T(8,128)S(1)}, u32[]{:S(2)}, u32[]{:S(2)}) collective-permute-start(f32[8,1024]{1,0:T(8,128)S(1)} %get-tuple-element.20.payload.refs_0_), channel_id=1, source_target_pairs={{0,4},{4,8},{8,12},{12,0},{1,5},{5,9},{9,13},{13,1},{2,6},{6,10},{... | collective-permute-start | bytes 98312 | tf_op jit(solution)/shard_map/ppermute | solution.py:421
  4.4 6.9 %collective-permute-start.1 = (f32[8,1024]{1,0:T(8,128)S(1)}, f32[8,1024]{1,0:T(8,128)S(1)}, u32[]{:S(2)}, u32[]{:S(2)}) collective-permute-start(f32[8,1024]{1,0:T(8,128)S(1)} %get-tuple-element.20.payload.refs_0_), channel_id=1, source_target_pairs={{0,12},{4,0},{8,4},{12,8},{1,13},{5,1},{9,5},{13,9},{2,14},{6,2},{... | collective-permute-start | bytes 98312 | tf_op jit(solution)/shard_map/ppermute | solution.py:421
  6.5 5.1 %collective-permute-start = (f32[8,1024]{1,0:T(8,128)S(1)}, f32[8,1024]{1,0:T(8,128)S(1)}, u32[]{:S(2)}, u32[]{:S(2)}) collective-permute-start(f32[8,1024]{1,0:T(8,128)S(1)} %get-tuple-element.20.payload.refs_0_), channel_id=1, source_target_pairs={{0,8},{4,12},{8,0},{12,4},{1,9},{5,13},{9,1},{13,5},{2,10},{6,14},... | collective-permute-start | bytes 98312 | tf_op jit(solution)/shard_map/ppermute | solution.py:421
  7.5 9.3 %collective-permute-start.3 = (f32[16,8,256]{2,1,0:T(8,128)S(1)}, f32[16,8,256]{2,1,0:T(8,128)S(1)}, u32[]{:S(2)}, u32[]{:S(2)}) collective-permute-start(f32[16,8,256]{2,1,0:T(8,128)S(1)} %get-tuple-element.23), channel_id=1, source_target_pairs={{0,12},{4,0},{8,4},{12,8},{1,13},{5,1},{9,5},{13,9},{2,14},{6,2},{... | collective-permute-start | bytes 393224 | tf_op jit(solution)/shard_map/ppermute | solution.py:421
  8.9 7.9 %collective-permute-start.4 = (f32[16,8,256]{2,1,0:T(8,128)S(1)}, f32[16,8,256]{2,1,0:T(8,128)S(1)}, u32[]{:S(2)}, u32[]{:S(2)}) collective-permute-start(f32[16,8,256]{2,1,0:T(8,128)S(1)} %get-tuple-element.24), channel_id=1, source_target_pairs={{0,4},{4,8},{8,12},{12,0},{1,5},{5,9},{9,13},{13,1},{2,6},{6,10},{... | collective-permute-start | bytes 393224 | tf_op jit(solution)/shard_map/ppermute | solution.py:421
  11.7 7.4 %collective-permute-start.5 = (f32[32,8,256]{2,1,0:T(8,128)S(1)}, f32[32,8,256]{2,1,0:T(8,128)S(1)}, u32[]{:S(2)}, u32[]{:S(2)}) collective-permute-start(f32[32,8,256]{2,1,0:T(8,128)S(1)} %shard_map.115), channel_id=1, source_target_pairs={{0,2},{2,0},{1,3},{3,1},{4,6},{6,4},{5,7},{7,5},{8,10},{10,8},{9,1... | collective-permute-start | bytes 786440 | tf_op jit(solution)/shard_map/ppermute | solution.py:427
  16.8 4.3 %collective-permute-start.6 = (f32[4,16,256]{2,1,0:T(8,128)S(1)}, f32[4,16,256]{2,1,0:T(8,128)S(1)}, u32[]{:S(2)}, u32[]{:S(2)}) collective-permute-start(f32[4,16,256]{2,1,0:T(8,128)S(1)} %shard_map.113.refs_5_), channel_id=1, source_target_pairs={{0,2},{2,0},{1,3},{3,1},{4,6},{6,4},{5,7},{7,5},{8,10},{10,8},{9,1... | collective-permute-start | bytes 196616 | tf_op jit(solution)/shard_map/ppermute | solution.py:427
  21.9 1.3 %collective-permute-start.7 = (f32[4,24,128]{2,1,0:T(8,128)S(1)}, f32[4,24,128]{2,1,0:T(8,128)S(1)}, u32[]{:S(2)}, u32[]{:S(2)}) collective-permute-start(f32[4,24,128]{2,1,0:T(8,128)S(1)} %get-tuple-element.34.sent), channel_id=1, source_target_pairs={{0,1},{1,0},{2,3},{3,2},{4,5},{5,4},{6,7},{7,6},{8,9},{9,8},{10,11... | collective-permute-start | bytes 147464 | tf_op jit(solution)/shard_map/ppermute | solution.py:547
